TPU v7x, 32 devices: a whole 2x2x4 slice. The times are simulated.
32 devices in a mesh: tm: 8 (over z, y), band: 4 (over x, core).
Axes of the slice: x: 2, y: 2, z: 4, core: 2. Of those that a mesh axis runs over, the one named last changes fastest.
Arguments:
- queries: bfloat16 [16, 16, 16, 5120], P('tm', 'band'), may hold values from -118 to 118
- key_states: bfloat16 [16, 16, 16, 5120], P('tm', 'band'), may hold values from -4 to 4
- value_states: bfloat16 [16, 16, 16, 5120], P('tm', 'band'), may hold values from -5 to 5
- cotangent: bfloat16 [16, 16, 16, 5120], P('tm', 'band'), may hold values from -5 to 5
- frame_blocks: int32 [16], replicated, may hold values from 0 to 7, never falling along the last dimension, each value on 1 to 3 neighbouring positions
- tile_lists: int32 [8, 2, 2, 10], replicated, may hold values from 0 to 11, as said below
Outputs:
- attended: bfloat16 [16, 16, 16, 5120], P('tm', 'band')
- grad_queries: bfloat16 [16, 16, 16, 5120], P('tm', 'band')
- grad_keys: bfloat16 [16, 16, 16, 5120], P('tm', 'band')
- grad_values: bfloat16 [16, 16, 16, 5120], P('tm', 'band')
Inputs may be any that keep to these rules, and one draw needn't show every extreme that they name: tile_lists[s, a, b] holds 10 distinct ids for tile a * 2 + b of slab s; id d * 4 + i names tile i of the slab d slabs earlier; the first id is always the tile itself.
All inputs are finite; a program needn't handle non-finite values.
Results may differ from a plain program's by a relative error of at most 0.011.
Values may be sent and summed in bfloat16 or wider, within the bound.
No kernel may reach another device: no remote copies, remote signals or barrier semaphores. Data moves between devices by JAX's collectives and lax.ppermute only.
A program may use at most 128 MiB of HBM per device.

v0:
```python
import jax
import jax.numpy as jnp
from jax import lax
from jax.sharding import PartitionSpec as P

HEAD_DIM = 128
TT = 2
TH = 8
TW = 8
NTH = 2
NTW = 2
K_NB = 10
TPS = 4
TILE = 128


MASKED = -1e30


def shifted(value, axis, steps):
    count = lax.axis_size(axis)
    initial, last = (max(0, -steps), min(count, count - steps))
    return lax.ppermute(value, axis, [(source, source + steps) for source in range(initial, last)])


def to_tiles(array_in):
    frames = array_in.shape[0]
    channels = array_in.shape[-1]
    tiled_view = array_in.reshape(frames // TT, TT, NTH, TH, NTW, TW, channels)
    tiled_view = tiled_view.transpose(0, 2, 4, 1, 3, 5, 6)
    return tiled_view.reshape(frames // TT, NTH * NTW, TT * TH * TW, channels)


def from_tiles(tiled_in):
    slab_count = tiled_in.shape[0]
    channels = tiled_in.shape[-1]
    tiled_view = tiled_in.reshape(slab_count, NTH, NTW, TT, TH, TW, channels)
    tiled_view = tiled_view.transpose(0, 3, 1, 4, 2, 5, 6)
    return tiled_view.reshape(slab_count * TT, NTH * TH, NTW * TW, channels)


def block_lookup(lookup_table, slot_ids):
    places = jnp.arange(lookup_table.shape[0], dtype=jnp.int32)
    return jnp.sum(
        jnp.where(slot_ids[:, None] == places[None, :], lookup_table[None, :], 0), axis=1
    )


def window_blocks(frame_blocks, slab_index):
    padded = jnp.concatenate([jnp.zeros((2 * TT,), jnp.int32), frame_blocks])
    return lax.dynamic_slice_in_dim(padded, slab_index * TT, 3 * TT)


def key_mask(listed_ids, slab_index, blocks_here):
    frames = jnp.arange(TT * TH * TW, dtype=jnp.int32) // (TH * TW)
    distance = listed_ids // TPS
    slot_ids = ((2 - distance)[:, None] * TT + frames[None, :]).reshape(-1)
    present = jnp.repeat(slab_index - distance >= 0, TT * TH * TW)
    key_block = block_lookup(blocks_here, slot_ids)
    query_block = block_lookup(blocks_here, 2 * TT + frames)
    return present[None, :] & (key_block[None, :] <= query_block[:, None])


def window_mask(listed_ids, slab_index, blocks_here):
    window_ids = jnp.arange(3 * TPS, dtype=jnp.int32)
    listed = jnp.any(listed_ids[:, None] == window_ids[None, :], axis=0)
    base_mask = key_mask(window_ids, slab_index, blocks_here)
    return base_mask & jnp.repeat(listed, TILE)[None, :]


def head_view(array_in):
    return array_in.reshape(array_in.shape[0], -1, HEAD_DIM)


def masked_scores(q_tile, k_keys, allowed):
    scores = jnp.einsum(
        "qhd,khd->hqk", head_view(q_tile), head_view(k_keys), preferred_element_type=jnp.float32
    )
    return jnp.where(allowed[None], scores * HEAD_DIM ** (-0.5), MASKED)


def score_grads(scores, c_tile, v_keys, log_sums, row_delta):
    back_probs = jnp.exp(scores - log_sums[..., None])
    dprobs = jnp.einsum(
        "qhd,khd->hqk", head_view(c_tile), head_view(v_keys), preferred_element_type=jnp.float32
    )
    dscores = (back_probs * (dprobs - row_delta[..., None])).astype(jnp.bfloat16)
    return (back_probs, dscores)


def query_grad(dscores, k_keys):
    grad_q = jnp.einsum(
        "hqk,khd->qhd", dscores, head_view(k_keys), preferred_element_type=jnp.float32
    )
    return (grad_q * HEAD_DIM ** (-0.5)).reshape(grad_q.shape[0], -1)


def key_value_grads(dscores, back_probs, q_tile, c_tile):
    grad_k = jnp.einsum(
        "hqk,qhd->khd", dscores, head_view(q_tile), preferred_element_type=jnp.float32
    ) * HEAD_DIM ** (-0.5)
    grad_v = jnp.einsum(
        "hqk,qhd->khd",
        back_probs.astype(jnp.bfloat16),
        head_view(c_tile),
        preferred_element_type=jnp.float32,
    )
    return (grad_k.reshape(grad_k.shape[0], -1), grad_v.reshape(grad_v.shape[0], -1))


def on_device(queries, key_states, value_states, cotangent, frame_blocks, tile_lists):
    q_rows, k_rows, v_rows, c_rows = (
        lax.all_to_all(queries, "band", split_axis=3, concat_axis=1, tiled=True),
        lax.all_to_all(key_states, "band", split_axis=3, concat_axis=1, tiled=True),
        lax.all_to_all(value_states, "band", split_axis=3, concat_axis=1, tiled=True),
        lax.all_to_all(cotangent, "band", split_axis=3, concat_axis=1, tiled=True),
    )
    q_tiles = to_tiles(q_rows)[0]
    k_tiles = to_tiles(k_rows)[0]
    v_tiles = to_tiles(v_rows)[0]
    c_tiles = to_tiles(c_rows)[0]
    channels = q_tiles.shape[-1]
    head_count = channels // HEAD_DIM
    slab_index = lax.axis_index("tm")
    own_kv = jnp.stack([k_tiles.reshape(-1, channels), v_tiles.reshape(-1, channels)])
    near_kv = shifted(own_kv, "tm", 1)
    far_kv = shifted(own_kv, "tm", 2)
    window_kv = jnp.concatenate([own_kv, near_kv, far_kv], axis=1)
    window_keys = window_kv[0]
    window_values = window_kv[1]
    own_rows = TPS * TILE
    tile_ids = lax.dynamic_index_in_dim(tile_lists, slab_index, 0, keepdims=False).reshape(
        TPS, K_NB
    )
    blocks_here = window_blocks(frame_blocks, slab_index)

    def forward_step(running, tile_item):
        q_tile, listed_ids = tile_item
        allowed = window_mask(listed_ids, slab_index, blocks_here)
        scores = masked_scores(q_tile, window_keys, allowed)
        row_max = jnp.max(scores, axis=-1)
        raised = jnp.exp(scores - row_max[..., None])
        row_sum = jnp.sum(raised, axis=-1)
        weights = (raised / row_sum[..., None]).astype(jnp.bfloat16)
        mixed = jnp.einsum(
            "hqk,khd->qhd", weights, head_view(window_values), preferred_element_type=jnp.float32
        )
        return (
            running,
            (mixed.reshape(q_tile.shape).astype(jnp.bfloat16), row_max + jnp.log(row_sum)),
        )

    _, (out_tiles, lse_tiles) = lax.scan(forward_step, None, (q_tiles, tile_ids))
    attended = lax.all_to_all(
        from_tiles(out_tiles[None]), "band", split_axis=1, concat_axis=3, tiled=True
    )
    delta_tiles = jnp.sum(
        (c_tiles.astype(jnp.float32) * out_tiles.astype(jnp.float32)).reshape(
            TPS, TILE, head_count, HEAD_DIM
        ),
        axis=-1,
    ).transpose(0, 2, 1)

    def back_step(grad_tabs, tile_item):
        q_tile, c_tile, log_sums, row_delta, listed_ids = tile_item
        allowed = window_mask(listed_ids, slab_index, blocks_here)
        scores = masked_scores(q_tile, window_keys, allowed)
        back_probs, dscores = score_grads(scores, c_tile, window_values, log_sums, row_delta)
        grad_k, grad_v = key_value_grads(dscores, back_probs, q_tile, c_tile)
        grad_tabs = (grad_tabs[0] + grad_k, grad_tabs[1] + grad_v)
        return (grad_tabs, query_grad(dscores, window_keys).astype(jnp.bfloat16))

    zero_rows = jnp.zeros((3 * own_rows, channels), jnp.float32)
    (key_tab, value_tab), dq_tiles = lax.scan(
        back_step, (zero_rows, zero_rows), (q_tiles, c_tiles, lse_tiles, delta_tiles, tile_ids)
    )
    recv_near = shifted(
        (key_tab[own_rows : 2 * own_rows], value_tab[own_rows : 2 * own_rows]), "tm", -1
    )
    recv_far = (
        shifted(key_tab[2 * own_rows :].astype(jnp.bfloat16), "tm", -2).astype(jnp.float32),
        shifted(value_tab[2 * own_rows :].astype(jnp.bfloat16), "tm", -2).astype(jnp.float32),
    )
    key_grad = key_tab[:own_rows] + recv_near[0] + recv_far[0]
    value_grad = value_tab[:own_rows] + recv_near[1] + recv_far[1]
    dq_rows = from_tiles(dq_tiles[None])
    dk_rows = from_tiles(key_grad.astype(jnp.bfloat16).reshape(1, TPS, TILE, channels))
    dv_rows = from_tiles(value_grad.astype(jnp.bfloat16).reshape(1, TPS, TILE, channels))
    grad_queries, grad_keys, grad_values = (
        lax.all_to_all(dq_rows, "band", split_axis=1, concat_axis=3, tiled=True),
        lax.all_to_all(dk_rows, "band", split_axis=1, concat_axis=3, tiled=True),
        lax.all_to_all(dv_rows, "band", split_axis=1, concat_axis=3, tiled=True),
    )
    return (attended, grad_queries, grad_keys, grad_values)


def solution(mesh):
    placed = (
        P("tm", "band", None, None),
        P("tm", "band", None, None),
        P("tm", "band", None, None),
        P("tm", "band", None, None),
        P(),
        P(),
    )
    return jax.shard_map(
        on_device,
        mesh=mesh,
        in_specs=placed,
        out_specs=(
            P("tm", "band", None, None),
            P("tm", "band", None, None),
            P("tm", "band", None, None),
            P("tm", "band", None, None),
        ),
        check_vma=False,
    )
```

profile of v0, /device:TPU:0, one launch (start us, length us, event | category | flops | bytes accessed | tf_op | source)
XLA Modules:
  0.0 640.4 jit_solution(12445436238322890944)
XLA Ops:
  0.6 12.6 %copy.140 = bf16[2,4,16,5120]{2,1,0,3:T(4,128)(2,1)} copy(bf16[2,4,16,5120]{3,2,1,0:T(8,128)(2,1)} %param.11) | data formatting | bytes 2621440 | tf_op args[1]
  13.3 13.4 %reshape.451 = bf16[4,2,81920]{2,1,0:T(2,128)(2,1)} reshape(bf16[5120,2,4,16]{3,2,1,0:T(4,128)(2,1)} %bitcast.199) | data formatting | bytes 2621440
  30.9 10.0 %copy.144 = bf16[2,4,16,5120]{2,1,0,3:T(4,128)(2,1)} copy(bf16[2,4,16,5120]{3,2,1,0:T(8,128)(2,1)S(1)} %copy-done.10) | data formatting | bytes 2621440 | tf_op args[2]
  40.8 13.3 %reshape.449 = bf16[4,2,81920]{2,1,0:T(2,128)(2,1)} reshape(bf16[5120,2,4,16]{3,2,1,0:T(4,128)(2,1)} %bitcast.200) | data formatting | bytes 2621440
  57.7 9.3 %reshape.452 = bf16[5120,2,4,16]{3,2,1,0:T(4,128)(2,1)} reshape(bf16[4,2,81920]{2,1,0:T(2,128)(2,1)S(1)} %all-to-all-done.1) | data formatting | bytes 2621440
  67.0 12.8 %copy.142 = bf16[2,4,4,16,1280]{4,3,2,1,0:T(8,128)(2,1)} copy(bf16[2,4,4,16,1280]{3,2,0,4,1:T(4,128)(2,1)} %bitcast.195) | data formatting | bytes 2621440 | tf_op jit(solution)/shard_map/all_to_all | solution.py:114
  81.2 9.3 %reshape.450 = bf16[5120,2,4,16]{3,2,1,0:T(4,128)(2,1)} reshape(bf16[4,2,81920]{2,1,0:T(2,128)(2,1)S(1)} %all-to-all-done.2) | data formatting | bytes 2621440
  90.5 11.7 %copy.146 = bf16[2,4,4,16,1280]{4,3,2,1,0:T(8,128)(2,1)S(1)} copy(bf16[2,4,4,16,1280]{3,2,0,4,1:T(4,128)(2,1)} %bitcast.196) | data formatting | bytes 2621440 | tf_op jit(solution)/shard_map/all_to_all | solution.py:115
  116.0 10.0 %copy.136 = bf16[2,4,16,5120]{2,1,0,3:T(4,128)(2,1)} copy(bf16[2,4,16,5120]{3,2,1,0:T(8,128)(2,1)S(1)} %copy-done.11) | data formatting | bytes 2621440 | tf_op args[0]
  126.0 13.3 %reshape.447 = bf16[4,2,81920]{2,1,0:T(2,128)(2,1)} reshape(bf16[5120,2,4,16]{3,2,1,0:T(4,128)(2,1)} %bitcast.201) | data formatting | bytes 2621440
  142.9 12.6 %copy.156 = bf16[2,4,16,5120]{2,1,0,3:T(4,128)(2,1)} copy(bf16[2,4,16,5120]{3,2,1,0:T(8,128)(2,1)} %param.13) | data formatting | bytes 2621440 | tf_op args[3]
  155.5 13.3 %reshape.453 = bf16[4,2,81920]{2,1,0:T(2,128)(2,1)} reshape(bf16[5120,2,4,16]{3,2,1,0:T(4,128)(2,1)} %bitcast.202) | data formatting | bytes 2621440
  183.0 11.7 %copy.138 = bf16[2,4,4,16,1280]{4,3,2,1,0:T(8,128)(2,1)S(1)} copy(bf16[2,4,4,16,1280]{3,2,0,4,1:T(4,128)(2,1)} %bitcast.197) | data formatting | bytes 2621440 | tf_op jit(solution)/shard_map/all_to_all | solution.py:113
  197.6 9.7 %reshape.454 = bf16[5120,2,4,16]{3,2,1,0:T(4,128)(2,1)} reshape(bf16[4,2,81920]{2,1,0:T(2,128)(2,1)} %all-to-all-done.4) | data formatting | bytes 2621440
  207.2 12.8 %copy.158 = bf16[2,4,4,16,1280]{4,3,2,1,0:T(8,128)(2,1)} copy(bf16[2,4,4,16,1280]{3,2,0,4,1:T(4,128)(2,1)} %bitcast.198) | data formatting | bytes 2621440 | tf_op jit(solution)/shard_map/all_to_all | solution.py:116
  243.5 39.3 %while.33 = (s32[]{:T(128)}, bf16[4,128,1280]{2,1,0:T(8,128)(2,1)S(1)}, f32[4,10,128]{2,1,0:T(8,128)S(1)}, s32[]{:T(128)}, s32[6]{0:T(128)S(1)}, /*index=5*/s32[...) while((s32[]{:T(128)}, ...), condition=%wide.region_6.7_spmd, body=%wide.region_0.6_spmd.sunk | while | flops 1031009792 | bytes 50678228 | solution.py:153
  292.9 129.6 %while.34 = (s32[]{:T(128)}, f32[1536,1280]{0,1:T(8,128)}, f32[1536,1280]{0,1:T(8,128)}, bf16[4,128,1280]{2,1,0:T(8,128)(2,1)}, bf16[4,128,1280]{1,2,0:T(8,128)(...) while((s32[]{:T(128)}, f32[1536,1280]{0,1:T(8,128)}, ...), condition=%wide.region_12.13_spmd.clone, body=%wide.region_8.12_spmd.clone.sunk | while | flops 2547023616 | bytes 162861648 | solution.py:174
  312.4 9.5 %bitcast_add_fusion.3 = (f32[1536,1280]{0,1:T(8,128)}, f32[1536,1280]{0,1:T(8,128)}) fusion(f32[10,128,1536]{2,1,0:T(8,128)} %fusion.82, f32[1536,1280]{0,1:T(8,128)} %get-tuple-element.735, pred[]{:T(512)S(6)} %compare.24, f32[10,128,1536]{2,1,0:T(8,128)S(1)} %convolution_multiply_fusion.3, f32[1536,1280]{0,1:T(8,128)} %get-tuple-element.734), kind=kLoop, calls=%fused_computation.35.clone.1 | loop fusion | flops 7864320 | bytes 47185920 | tf_op jit(solution)/shard_map/while/body/eval_jaxpr/add | solution.py:170
  341.4 14.0 %bitcast_add_fusion.3 = (f32[1536,1280]{0,1:T(8,128)}, f32[1536,1280]{0,1:T(8,128)}) fusion(f32[10,128,1536]{2,1,0:T(8,128)} %fusion.82, f32[1536,1280]{0,1:T(8,128)} %get-tuple-element.735, pred[]{:T(512)S(6)} %compare.24, f32[10,128,1536]{2,1,0:T(8,128)S(1)} %convolution_multiply_fusion.3, f32[1536,1280]{0,1:T(8,128)} %get-tuple-element.734), kind=kLoop, calls=%fused_computation.35.clone.1 | loop fusion | flops 7864320 | bytes 47185920 | tf_op jit(solution)/shard_map/while/body/eval_jaxpr/add | solution.py:170
  375.0 14.0 %bitcast_add_fusion.3 = (f32[1536,1280]{0,1:T(8,128)}, f32[1536,1280]{0,1:T(8,128)}) fusion(f32[10,128,1536]{2,1,0:T(8,128)} %fusion.82, f32[1536,1280]{0,1:T(8,128)} %get-tuple-element.735, pred[]{:T(512)S(6)} %compare.24, f32[10,128,1536]{2,1,0:T(8,128)S(1)} %convolution_multiply_fusion.3, f32[1536,1280]{0,1:T(8,128)} %get-tuple-element.734), kind=kLoop, calls=%fused_computation.35.clone.1 | loop fusion | flops 7864320 | bytes 47185920 | tf_op jit(solution)/shard_map/while/body/eval_jaxpr/add | solution.py:170
  408.5 14.0 %bitcast_add_fusion.3 = (f32[1536,1280]{0,1:T(8,128)}, f32[1536,1280]{0,1:T(8,128)}) fusion(f32[10,128,1536]{2,1,0:T(8,128)} %fusion.82, f32[1536,1280]{0,1:T(8,128)} %get-tuple-element.735, pred[]{:T(512)S(6)} %compare.24, f32[10,128,1536]{2,1,0:T(8,128)S(1)} %convolution_multiply_fusion.3, f32[1536,1280]{0,1:T(8,128)} %get-tuple-element.734), kind=kLoop, calls=%fused_computation.35.clone.1 | loop fusion | flops 7864320 | bytes 47185920 | tf_op jit(solution)/shard_map/while/body/eval_jaxpr/add | solution.py:170
  464.8 11.7 %all-to-all-done.3 = bf16[2,16,16,1280]{3,2,0,1:T(8,128)(2,1)S(1)} async-done(((bf16[2,16,16,1280]{3,2,0,1:T(8,128)(2,1)}), bf16[2,16,16,1280]{3,2,0,1:T(8,128)(2,1)S(1)}, u32[]{:S(2)}, u32[]{:S(2)}) %all-to-all-start.3) | async-done | bytes 1310752 | tf_op jit(solution)/shard_map/all_to_all | solution.py:154
  480.1 102.6 %collective-permute-done.3 = bf16[512,1280]{1,0:T(8,128)(2,1)} collective-permute-done((bf16[512,1280]{1,0:T(8,128)(2,1)}, bf16[512,1280]{1,0:T(8,128)(2,1)}, u32[]{:S(2)}, u32[]{:S(2)}) %collective-permute-start.3) | collective-permute-done | bytes 1310752 | tf_op jit(solution)/shard_map/ppermute | solution.py:23
  591.8 17.9 %collective-permute-done.5 = bf16[512,1280]{1,0:T(8,128)(2,1)} collective-permute-done((bf16[512,1280]{1,0:T(8,128)(2,1)}, bf16[512,1280]{1,0:T(8,128)(2,1)}, u32[]{:S(2)}, u32[]{:S(2)}) %collective-permute-start.5) | collective-permute-done | bytes 1310752 | tf_op jit(solution)/shard_map/ppermute | solution.py:23
  (284 shorter events, 279.0 us)
Async XLA Ops:
  0.6 173.1 %copy-start = (s32[8,2,2,10]{3,2,1,0:T(2,128)S(1)}, s32[8,2,2,10]{3,2,1,0:T(2,128)}, u32[]{:S(2)}) copy-start(s32[8,2,2,10]{3,2,1,0:T(2,128)} %param.15) | copy-start | bytes 3844
  13.3 17.6 %copy-start.10 = (bf16[2,4,16,5120]{3,2,1,0:T(8,128)(2,1)S(1)}, bf16[2,4,16,5120]{3,2,1,0:T(8,128)(2,1)}, u32[]{:S(2)}) copy-start(bf16[2,4,16,5120]{3,2,1,0:T(8,128)(2,1)} %param.12) | copy-start | bytes 3932164
  26.6 27.5 %all-to-all-start.1 = ((bf16[4,2,81920]{2,1,0:T(2,128)(2,1)}), bf16[4,2,81920]{2,1,0:T(2,128)(2,1)S(1)}, u32[]{:S(2)}, u32[]{:S(2)}) async-start(bf16[4,2,81920]{2,1,0:T(2,128)(2,1)} %reshape.451), calls=%async_computation.1 | async-start | bytes 2621440 | tf_op jit(solution)/shard_map/all_to_all | solution.py:114
  54.1 27.0 %all-to-all-start.2 = ((bf16[4,2,81920]{2,1,0:T(2,128)(2,1)}), bf16[4,2,81920]{2,1,0:T(2,128)(2,1)S(1)}, u32[]{:S(2)}, u32[]{:S(2)}) async-start(bf16[4,2,81920]{2,1,0:T(2,128)(2,1)} %reshape.449), calls=%async_computation.2 | async-start | bytes 2621440 | tf_op jit(solution)/shard_map/all_to_all | solution.py:115
  102.3 13.8 %copy-start.11 = (bf16[2,4,16,5120]{3,2,1,0:T(8,128)(2,1)S(1)}, bf16[2,4,16,5120]{3,2,1,0:T(8,128)(2,1)}, u32[]{:S(2)}) copy-start(bf16[2,4,16,5120]{3,2,1,0:T(8,128)(2,1)} %param.10) | copy-start | bytes 3932164
  105.0 117.4 %collective-permute-start.1 = (bf16[2,512,1280]{2,1,0:T(8,128)(2,1)}, bf16[2,512,1280]{2,1,0:T(8,128)(2,1)}, u32[]{:S(2)}, u32[]{:S(2)}) collective-permute-start(bf16[2,512,1280]{2,1,0:T(8,128)(2,1)} %pad_maximum_fusion.1), channel_id=1, source_target_pairs={{0,8},{4,12},{8,16},{12,20},{16,24},{20,28},{1,9},{5,13},{9,17},{1... | collective-permute-start | bytes 7864328 | tf_op jit(solution)/shard_map/ppermute | solution.py:23
  110.8 111.6 %collective-permute-start = (bf16[2,512,1280]{2,1,0:T(8,128)(2,1)}, bf16[2,512,1280]{2,1,0:T(8,128)(2,1)}, u32[]{:S(2)}, u32[]{:S(2)}) collective-permute-start(bf16[2,512,1280]{2,1,0:T(8,128)(2,1)} %pad_maximum_fusion.1), channel_id=1, source_target_pairs={{0,4},{4,8},{8,12},{12,16},{16,20},{20,24},{24,28},{1,5},{5,9},{9,... | collective-permute-start | bytes 7864328 | tf_op jit(solution)/shard_map/ppermute | solution.py:23
  139.3 29.5 %all-to-all-start = ((bf16[4,2,81920]{2,1,0:T(2,128)(2,1)}), bf16[4,2,81920]{2,1,0:T(2,128)(2,1)S(1)}, u32[]{:S(2)}, u32[]{:S(2)}) async-start(bf16[4,2,81920]{2,1,0:T(2,128)(2,1)} %reshape.447), calls=%async_computation | async-start | bytes 2621440 | tf_op jit(solution)/shard_map/all_to_all | solution.py:113
  155.5 18.2 %copy-start.12 = (s32[16]{0:T(128)S(1)}, s32[16]{0:T(128)}, u32[]{:S(2)}) copy-start(s32[16]{0:T(128)} %param.14) | copy-start | bytes 196
  168.8 28.8 %all-to-all-start.4 = ((bf16[4,2,81920]{2,1,0:T(2,128)(2,1)}), bf16[4,2,81920]{2,1,0:T(2,128)(2,1)}, u32[]{:S(2)}, u32[]{:S(2)}) async-start(bf16[4,2,81920]{2,1,0:T(2,128)(2,1)} %reshape.453), calls=%async_computation.4 | async-start | bytes 2621440 | tf_op jit(solution)/shard_map/all_to_all | solution.py:116
  282.8 6.9 %copy-start.4 = (bf16[4,128,1280]{2,1,0:T(8,128)(2,1)}, bf16[4,128,1280]{2,1,0:T(8,128)(2,1)S(1)}, u32[]{:S(2)}) copy-start(bf16[4,128,1280]{2,1,0:T(8,128)(2,1)S(1)} %get-tuple-element.349) | copy-start | bytes 3932164
  301.7 5.2 copy-start.3
  330.7 5.2 copy-start.3
  435.0 147.7 %collective-permute-start.2 = (f32[512,1280]{1,0:T(8,128)}, f32[512,1280]{1,0:T(8,128)}, u32[]{:S(2)}, u32[]{:S(2)}) collective-permute-start(f32[512,1280]{1,0:T(8,128)} %slice.37), channel_id=1, source_target_pairs={{4,0},{8,4},{12,8},{16,12},{20,16},{24,20},{28,24},{5,1},{9,5},{13... | collective-permute-start | bytes 7864328 | tf_op jit(solution)/shard_map/ppermute | solution.py:23
  445.4 9.0 %copy-start.5 = (bf16[4,128,1280]{2,1,0:T(8,128)(2,1)S(1)}, bf16[4,128,1280]{2,1,0:T(8,128)(2,1)}, u32[]{:S(2)}) copy-start(bf16[4,128,1280]{2,1,0:T(8,128)(2,1)} %copy-done.4) | copy-start | bytes 3932164
  449.0 160.8 %collective-permute-start.4 = (f32[512,1280]{1,0:T(8,128)}, f32[512,1280]{1,0:T(8,128)}, u32[]{:S(2)}, u32[]{:S(2)}) collective-permute-start(f32[512,1280]{1,0:T(8,128)} %slice.40), channel_id=1, source_target_pairs={{4,0},{8,4},{12,8},{16,12},{20,16},{24,20},{28,24},{5,1},{9,5},{13... | collective-permute-start | bytes 7864328 | tf_op jit(solution)/shard_map/ppermute | solution.py:23
  453.2 129.5 %collective-permute-start.3 = (bf16[512,1280]{1,0:T(8,128)(2,1)}, bf16[512,1280]{1,0:T(8,128)(2,1)}, u32[]{:S(2)}, u32[]{:S(2)}) collective-permute-start(bf16[512,1280]{1,0:T(8,128)(2,1)} %slice.55), channel_id=1, source_target_pairs={{8,0},{12,4},{16,8},{20,12},{24,16},{28,20},{9,1},{13,5},{17,9},{2... | collective-permute-start | bytes 3932168 | tf_op jit(solution)/shard_map/ppermute | solution.py:23
  454.6 9.0 %copy-start.7 = (bf16[4,128,1280]{2,1,0:T(8,128)(2,1)S(1)}, bf16[4,128,1280]{2,1,0:T(8,128)(2,1)}, u32[]{:S(2)}) copy-start(bf16[4,128,1280]{2,1,0:T(8,128)(2,1)} %get-tuple-element.351) | copy-start | bytes 3932164
  455.8 20.8 %all-to-all-start.3 = ((bf16[2,16,16,1280]{3,2,0,1:T(8,128)(2,1)}), bf16[2,16,16,1280]{3,2,0,1:T(8,128)(2,1)S(1)}, u32[]{:S(2)}, u32[]{:S(2)}) async-start(bf16[2,16,16,1280]{3,2,0,1:T(8,128)(2,1)} %copy.153), calls=%async_computation.3 | async-start | bytes 2621440 | tf_op jit(solution)/shard_map/all_to_all | solution.py:154
  462.3 147.5 %collective-permute-start.5 = (bf16[512,1280]{1,0:T(8,128)(2,1)}, bf16[512,1280]{1,0:T(8,128)(2,1)}, u32[]{:S(2)}, u32[]{:S(2)}) collective-permute-start(bf16[512,1280]{1,0:T(8,128)(2,1)} %slice.54), channel_id=1, source_target_pairs={{8,0},{12,4},{16,8},{20,12},{24,16},{28,20},{9,1},{13,5},{17,9},{2... | collective-permute-start | bytes 3932168 | tf_op jit(solution)/shard_map/ppermute | solution.py:23
  476.6 110.7 %all-to-all-start.5 = ((bf16[2,16,16,1280]{3,2,0,1:T(8,128)(2,1)}), bf16[2,16,16,1280]{3,2,0,1:T(8,128)(2,1)S(1)}, u32[]{:S(2)}, u32[]{:S(2)}) async-start(bf16[2,16,16,1280]{3,2,0,1:T(8,128)(2,1)} %copy.168), calls=%async_computation.5 | async-start | bytes 2621440 | tf_op jit(solution)/shard_map/all_to_all | solution.py:190
  587.3 27.1 %all-to-all-start.6 = ((bf16[2,16,16,1280]{3,2,0,1:T(8,128)(2,1)}), bf16[2,16,16,1280]{3,2,0,1:T(8,128)(2,1)}, u32[]{:S(2)}, u32[]{:S(2)}) async-start(bf16[2,16,16,1280]{3,2,0,1:T(8,128)(2,1)} %copy.175), calls=%async_computation.6 | async-start | bytes 2621440 | tf_op jit(solution)/shard_map/all_to_all | solution.py:191
  614.4 21.6 %all-to-all-start.7 = ((bf16[2,16,16,1280]{3,2,0,1:T(8,128)(2,1)}), bf16[2,16,16,1280]{3,2,0,1:T(8,128)(2,1)}, u32[]{:S(2)}, u32[]{:S(2)}) async-start(bf16[2,16,16,1280]{3,2,0,1:T(8,128)(2,1)} %copy.182), calls=%async_computation.7 | async-start | bytes 2621440 | tf_op jit(solution)/shard_map/all_to_all | solution.py:192
  627.2 13.0 %copy-start.1 = (s32[8,2,2,10]{3,2,1,0:T(2,128)S(1)}, s32[8,2,2,10]{3,2,1,0:T(2,128)}, u32[]{:S(2)}) copy-start(s32[8,2,2,10]{3,2,1,0:T(2,128)} %param.15) | copy-start | bytes 3844
  (15 other events, 55.2 us)
where the time goes:
time: 652 us; the launch traced here: 640 us
  local copies, waits for them, and re-layouts  279 us (43%)
  waiting for transfers between devices  137 us (21%)
  matrix products  90.9 us (14%)
  other arithmetic  83.6 us (13%)
  starting transfers between devices  48.1 us (7%)
    unnamed x30, local copies, waits for them, and re-layouts  137 us
    ppermute x6, waiting for transfers between devices, shifted(): lax.ppermute(value, axis, [(source, source + steps) for source in range(i...  121 us
    add x4, other arithmetic, back_step(): grad_tabs = (grad_tabs[0] + grad_k, grad_tabs[1] + grad_v)  51.4 us
    dot_general x8, matrix products, masked_scores(): jnp.einsum('qhd,khd->hqk', head_view(q_tile), head_view(k_keys), preferre...  29.6 us
    dot_general x4, matrix products, key_value_grads(): jnp.einsum('hqk,qhd->khd', back_probs.astype(jnp.bfloat16), head_view(c_t...  19.4 us
    while x2, local copies, waits for them, and re-layouts, on_device(): lax.scan(back_step, (zero_rows, zero_rows), (q_tiles, c_tiles, lse_tiles,...  18.3 us
    ppermute x6, starting transfers between devices, shifted(): lax.ppermute(value, axis, [(source, source + steps) for source in range(i...  16.1 us
    while x3, local copies, waits for them, and re-layouts, on_device(): lax.scan(forward_step, None, (q_tiles, tile_ids))  14.3 us
  transfers between devices with their start and end apart: 14, of which 4 were waited for; matrix products, arithmetic and copies ran while one was open for 28% of the time, Pallas kernels for 0%

commit v1 on v0

v1 whole, which is shorter than its diff:
```python
import functools
import math

import jax
import jax.numpy as jnp
from jax import lax
from jax.experimental import pallas as pl
from jax.experimental.pallas import tpu as pltpu
from jax.sharding import Mesh, PartitionSpec as P

HEAD_DIM = 128
TT = 2
TH = 8
TW = 8
NTW = 2
TPS = 4
K_NB = 10
MASKED = -1e30
CHUNKS = ((0, 2), (2, 2), (4, 1))
VMEM_LIMIT = 48 * 1024 * 1024


def run_copies(copies):
    for copy in copies:
        copy.start()
    for copy in copies:
        copy.wait()


def pack(arrays, members, heads, first, count):
    n = len(arrays)
    tokens = arrays[0].shape[0]
    width = count * HEAD_DIM

    def body(*refs):
        ins, out, sems = refs[:n], refs[n], refs[n + 1]
        run_copies(
            [
                pltpu.make_async_copy(
                    ins[a].at[:, pl.ds((p * heads + first) * HEAD_DIM, width)],
                    out.at[p, a],
                    sems.at[p * n + a],
                )
                for p in range(members)
                for a in range(n)
            ]
        )

    return pl.pallas_call(
        body,
        out_shape=jax.ShapeDtypeStruct((members, n, tokens, width), arrays[0].dtype),
        in_specs=[pl.BlockSpec(memory_space=pl.ANY)] * n,
        out_specs=pl.BlockSpec(memory_space=pl.ANY),
        scratch_shapes=[pltpu.SemaphoreType.DMA((members * n,))],
        cost_estimate=pl.CostEstimate(
            flops=0, bytes_accessed=4 * members * n * tokens * width, transcendentals=0
        ),
        name="pack",
    )(*arrays)


def unpack(received, outputs, shape, heads, first, count):
    members, n, tokens, width = received.shape
    filled = outputs is not None

    def body(*refs):
        source = refs[0]
        outs = refs[1 + n : 1 + 2 * n] if filled else refs[1 : 1 + n]
        sems = refs[-1]
        run_copies(
            [
                pltpu.make_async_copy(
                    source.at[p, a],
                    outs[a].at[:, pl.ds((p * heads + first) * HEAD_DIM, width)],
                    sems.at[p * n + a],
                )
                for p in range(members)
                for a in range(n)
            ]
        )

    args = (received,) + (tuple(outputs) if filled else ())
    return pl.pallas_call(
        body,
        out_shape=[jax.ShapeDtypeStruct(shape, received.dtype)] * n,
        in_specs=[pl.BlockSpec(memory_space=pl.ANY)] * len(args),
        out_specs=[pl.BlockSpec(memory_space=pl.ANY)] * n,
        scratch_shapes=[pltpu.SemaphoreType.DMA((members * n,))],
        input_output_aliases={1 + a: a for a in range(n)} if filled else {},
        cost_estimate=pl.CostEstimate(
            flops=0, bytes_accessed=4 * members * n * tokens * width, transcendentals=0
        ),
        name="unpack",
    )(*args)


def attention_body(
    bias_ref, class_ref, q_ref, c_ref, kc_ref, vc_ref, kp_ref, vp_ref,
    odq_ref, cur_ref, prev_ref, k_all, v_all, dk_all, dv_all,
):
    parts, rows = q_ref.shape[0], q_ref.shape[1]
    plane = parts * rows
    slab = plane // 2
    scale = HEAD_DIM ** -0.5
    scale2 = scale * math.log2(math.e)
    half = parts // 2
    k_all[:plane] = kp_ref[...].reshape(plane, HEAD_DIM)
    k_all[plane:] = kc_ref[...].reshape(plane, HEAD_DIM)
    v_all[:plane] = vp_ref[...].reshape(plane, HEAD_DIM)
    v_all[plane:] = vc_ref[...].reshape(plane, HEAD_DIM)
    dk_all[...] = jnp.zeros_like(dk_all)
    dv_all[...] = jnp.zeros_like(dv_all)
    nt = (((1,), (1,)), ((), ()))
    tn = (((0,), (0,)), ((), ()))
    for y in range(2):
        window = pl.ds(y * slab, 3 * slab)
        for piece in range(2):
            here = pl.ds(y * half + piece * (half // 2), half // 2)
            block = slab // 2
            q = q_ref[here].reshape(block, HEAD_DIM)
            c = c_ref[here].reshape(block, HEAD_DIM)
            k = k_all[window]
            v = v_all[window]
            classes = class_ref[pl.ds(piece * block, block)]
            s = lax.dot_general(
                jnp.concatenate([q, classes], axis=1),
                jnp.concatenate([k, bias_ref[y]], axis=1),
                nt,
                preferred_element_type=jnp.float32,
            )
            m = jnp.max(s, axis=1, keepdims=True)
            e = jnp.exp2((s - m) * scale2)
            p = e * (1.0 / jnp.sum(e, axis=1, keepdims=True))
            w = p.astype(jnp.bfloat16)
            o = jnp.dot(w, v, preferred_element_type=jnp.float32).astype(jnp.bfloat16)
            delta = jnp.sum(
                c.astype(jnp.float32) * o.astype(jnp.float32), axis=1, keepdims=True
            )
            dp = lax.dot_general(c, v, nt, preferred_element_type=jnp.float32)
            ds = (p * (dp - delta)).astype(jnp.bfloat16)
            dq = jnp.dot(ds, k, preferred_element_type=jnp.float32) * scale
            odq_ref[here, 0] = o.reshape(half // 2, rows, HEAD_DIM)
            odq_ref[here, 1] = dq.astype(jnp.bfloat16).reshape(half // 2, rows, HEAD_DIM)
            dk_all[window] += lax.dot_general(ds, q, tn, preferred_element_type=jnp.float32)
            dv_all[window] += lax.dot_general(w, c, tn, preferred_element_type=jnp.float32)
    prev_ref[:, 0] = (dk_all[:plane] * scale).astype(jnp.bfloat16).reshape(kp_ref.shape)
    prev_ref[:, 1] = dv_all[:plane].astype(jnp.bfloat16).reshape(kp_ref.shape)
    cur_ref[:, 0] = (dk_all[plane:] * scale).reshape(kp_ref.shape)
    cur_ref[:, 1] = dv_all[plane:].reshape(kp_ref.shape)


def attention(bias, classes, qc, kv, kv_prev):
    parts, _, rows, width = qc.shape
    plane = parts * rows
    heads = width // HEAD_DIM
    products = heads * 2 * (plane // 2) * 3 * (plane // 2)

    def one(array):
        return pl.BlockSpec(
            (parts, None, rows, HEAD_DIM), lambda h, array=array: (0, array, 0, h)
        )

    both = pl.BlockSpec((parts, 2, rows, HEAD_DIM), lambda h: (0, 0, 0, h))
    return pl.pallas_call(
        attention_body,
        grid=(heads,),
        out_shape=[
            jax.ShapeDtypeStruct(qc.shape, jnp.bfloat16),
            jax.ShapeDtypeStruct(qc.shape, jnp.float32),
            jax.ShapeDtypeStruct(qc.shape, jnp.bfloat16),
        ],
        in_specs=[
            pl.BlockSpec(bias.shape, lambda h: (0, 0, 0)),
            pl.BlockSpec(classes.shape, lambda h: (0, 0)),
            one(0), one(1), one(0), one(1), one(0), one(1),
        ],
        out_specs=[both, both, both],
        scratch_shapes=[
            pltpu.VMEM((2 * plane, HEAD_DIM), jnp.bfloat16),
            pltpu.VMEM((2 * plane, HEAD_DIM), jnp.bfloat16),
            pltpu.VMEM((2 * plane, HEAD_DIM), jnp.float32),
            pltpu.VMEM((2 * plane, HEAD_DIM), jnp.float32),
        ],
        compiler_params=pltpu.CompilerParams(vmem_limit_bytes=VMEM_LIMIT),
        cost_estimate=pl.CostEstimate(
            flops=24 * products * HEAD_DIM,
            bytes_accessed=2 * 9 * qc.size,
            transcendentals=products,
        ),
        name="attention",
    )(bias, classes, qc, qc, kv, kv, kv_prev, kv_prev)


def mask_operands(frame_blocks, tile_lists, z, bands, frame_rows, frame_cols):
    blocks = frame_blocks.reshape(-1, TT)
    padded = jnp.concatenate([jnp.zeros((2, TT), jnp.int32), blocks])
    tile_rows = frame_rows // TH
    lists = lax.dynamic_slice_in_dim(tile_lists, 2 * z, 2).reshape(2, TPS, K_NB)
    near = lax.dynamic_slice_in_dim(padded, 2 * z, 4)
    key_blocks = jnp.stack([near[0:3], near[1:4]])
    query_blocks = near[2:4]
    distance = 2 - jnp.arange(3, dtype=jnp.int32)
    ids = distance[:, None] * TPS + jnp.arange(TPS, dtype=jnp.int32)[None, :]
    listed = jnp.any(lists[:, :, None, None, :] == ids[None, None, :, :, None], axis=-1)
    present = (2 * z + jnp.arange(2, dtype=jnp.int32))[:, None] >= distance[None, :]
    causal = key_blocks[:, :, :, None] <= query_blocks[:, None, None, :]
    allowed = (
        listed.transpose(0, 2, 3, 1)[:, :, :, None, :, None]
        & present[:, :, None, None, None, None]
        & causal[:, :, None, :, None, :]
    )
    table = jnp.where(allowed, 0.0, MASKED).astype(jnp.bfloat16)
    table = table.reshape(2, 3, tile_rows, NTW, TT, TPS * TT)
    table = table.transpose(0, 1, 2, 4, 3, 5)
    table = jnp.pad(table, [(0, 0)] * 5 + [(0, HEAD_DIM - TPS * TT)])
    per_band = frame_rows // bands
    bias = jnp.broadcast_to(
        table[:, :, :, None, :, None, :, None, :],
        (2, 3, tile_rows, bands // tile_rows, TT, per_band, NTW, TW, HEAD_DIM),
    ).reshape(2, -1, HEAD_DIM)
    row = lax.broadcasted_iota(jnp.int32, (bands * TT * per_band * frame_cols, HEAD_DIM), 0)
    lane = lax.broadcasted_iota(jnp.int32, row.shape, 1)
    per_frame = per_band * frame_cols
    band = row // (TT * per_frame)
    frame = row // per_frame % TT
    tile = band // (bands // tile_rows) * NTW + row % frame_cols // TW
    classes = (lane == tile * TT + frame).astype(jnp.bfloat16)
    return bias, classes


def on_device(planes, bands, queries, key_states, value_states, cotangent, frame_blocks, tile_lists):
    members = 2 * bands
    width = queries.shape[-1]
    heads = width // HEAD_DIM // members
    z = lax.axis_index("plane")
    group = ("half", "band")
    q, k, v, c = (
        array.reshape(-1, width) for array in (queries, key_states, value_states, cotangent)
    )
    up = [(i, i + 1) for i in range(planes - 1)]
    down = [(i + 1, i) for i in range(planes - 1)]

    def exchange(array):
        return lax.all_to_all(array, group, split_axis=0, concat_axis=0, tiled=True)

    chunks = [(first, count) for first, count in CHUNKS if first + count <= heads]
    if sum(count for _, count in chunks) != heads:
        chunks = [(0, heads)]
    received = []
    for first, count in chunks:
        kv = exchange(pack((k, v), members, heads, first, count))
        kv_prev = lax.ppermute(kv, "plane", up)
        qc = exchange(pack((q, c), members, heads, first, count))
        received.append((qc, kv, kv_prev))
    bias, classes = mask_operands(
        frame_blocks, tile_lists, z, bands, queries.shape[1] * bands, queries.shape[2]
    )
    out_odq = out_dkv = None
    for (first, count), (qc, kv, kv_prev) in zip(chunks, received):
        odq, dkv, dkv_prev = attention(bias, classes, qc, kv, kv_prev)
        dkv_next = lax.ppermute(dkv_prev, "plane", down)
        out_odq = unpack(exchange(odq), out_odq, q.shape, heads, first, count)
        total = (dkv + dkv_next.astype(jnp.float32)).astype(jnp.bfloat16)
        out_dkv = unpack(exchange(total), out_dkv, q.shape, heads, first, count)
    return tuple(array.reshape(queries.shape) for array in (*out_odq, *out_dkv))


def solution(mesh):
    slabs, bands = mesh.shape["tm"], mesh.shape["band"]
    planes = slabs // 2
    split = Mesh(mesh.devices.reshape(planes, 2, bands), ("plane", "half", "band"))
    rows = P(("plane", "half"), "band", None, None)
    return jax.shard_map(
        functools.partial(on_device, planes, bands),
        mesh=split,
        in_specs=(rows, rows, rows, rows, P(), P()),
        out_specs=(rows, rows, rows, rows),
        check_vma=False,
    )
```

time: 652 us -> 506 us (0.78); the launches traced: 640 us -> 505 us
  Pallas kernels: 0 us -> 373 us
  local copies, waits for them, and re-layouts: 279 us -> 13.2 us
  waiting for transfers between devices: 137 us -> 42.1 us
  matrix products: 90.9 us -> 0 us
  other arithmetic: 83.6 us -> 9.11 us
  starting transfers between devices: 48.1 us -> 66.5 us
    pallas_call x0 -> x15, Pallas kernels: none -> 373 us  [the longest x6 166 us: unpack(): pl.pallas_call(body, out_shape=[jax.ShapeDtypeStruct(shape, received.dtyp...]
    unnamed x30 -> x42, local copies, waits for them, and re-layouts: 137 us -> 12.3 us
    dot_general x28 -> x0, matrix products: 90.9 us -> none  [the longest x8 29.6 us: masked_scores(): jnp.einsum('qhd,khd->hqk', head_view(q_tile), head_view(k_keys), preferre...]
    ppermute x6, waiting for transfers between devices: 121 us -> 32.1 us  [the longest x3 29.4 us: on_device(): dkv_next = lax.ppermute(dkv_prev, 'plane', down)]
    all_to_all x12 -> x0, local copies, waits for them, and re-layouts: 65.7 us -> none  [the longest x1 12.8 us: on_device(): lax.all_to_all(key_states, 'band', split_axis=3, concat_axis=1, tiled=True)]
    add x16 -> x2, other arithmetic: 52 us -> 0.07 us  [the longest x1 0.07 us: mask_operands(): ids = distance[:, None] * TPS + jnp.arange(TPS, dtype=jnp.int32)[None, :]]
    while x37 -> x0, local copies, waits for them, and re-layouts: 34.2 us -> none  [the longest x2 18.3 us: on_device(): lax.scan(back_step, (zero_rows, zero_rows), (q_tiles, c_tiles, lse_tiles,...]
    all_to_all x8 -> x12, starting transfers between devices: 32 us -> 50.9 us  [exchange(): return lax.all_to_all(array, group, split_axis=0, concat_axis=0, tiled=True)]
  transfers between devices with their start and end apart: 14 -> 18, of which waited for: 4 -> 6; matrix products, arithmetic and copies ran while one was open for 28% -> 2% of each run, Pallas kernels for 0% -> 67%
where the time goes in v1:
time: 506 us; the launch traced here: 505 us
  Pallas kernels  373 us (74%)
  starting transfers between devices  66.5 us (13%)
  waiting for transfers between devices  42.1 us (8%)
  local copies, waits for them, and re-layouts  13.2 us (3%)
  other arithmetic  9.11 us (2%)
    pallas_call x6, Pallas kernels, unpack(): pl.pallas_call(body, out_shape=[jax.ShapeDtypeStruct(shape, received.dtyp...  166 us
    pallas_call x6, Pallas kernels, pack(): pl.pallas_call(body, out_shape=jax.ShapeDtypeStruct((members, n, tokens,...  166 us
    all_to_all x12, starting transfers between devices, exchange(): return lax.all_to_all(array, group, split_axis=0, concat_axis=0, tiled=True)  50.9 us
    pallas_call x3, Pallas kernels, attention(): pl.pallas_call(attention_body, grid=(heads,), out_shape=[jax.ShapeDtypeSt...  40 us
    ppermute x3, waiting for transfers between devices, on_device(): dkv_next = lax.ppermute(dkv_prev, 'plane', down)  29.4 us
    unnamed x42, local copies, waits for them, and re-layouts  12.3 us
    ppermute x3, starting transfers between devices, on_device(): kv_prev = lax.ppermute(kv, 'plane', up)  11.5 us
  transfers between devices with their start and end apart: 18, of which 6 were waited for; matrix products, arithmetic and copies ran while one was open for 2% of the time, Pallas kernels for 67%

profile of v1, /device:TPU:0, one launch (start us, length us, event | category | flops | bytes accessed | tf_op | source)
XLA Modules:
  0.0 504.8 jit_solution(17088000541397656039)
XLA Ops:
  0.6 17.1 %pack.6 = bf16[8,2,128,128]{3,2,1,0:T(8,128)(2,1)} custom-call(bf16[128,5120]{1,0:T(8,128)(2,1)} %bitcast.27, bf16[128,5120]{1,0:T(8,128)(2,1)} %bitcast.30), custom_call_target="tpu_custom_call" | custom-call | bytes 1048576 | tf_op jit(solution)/shard_map/pack/pallas_call | solution.py:49
  17.8 5.2 %all-to-all-start = ((bf16[8,2,128,128]{3,2,1,0:T(8,128)(2,1)}), bf16[8,2,128,128]{3,2,1,0:T(8,128)(2,1)S(1)}, u32[]{:S(2)}, u32[]{:S(2)}) async-start(bf16[8,2,128,128]{3,2,1,0:T(8,128)(2,1)} %pack.6), calls=%async_computation | async-start | bytes 1048576 | tf_op jit(solution)/shard_map/all_to_all | solution.py:244
  23.0 17.1 %pack.7 = bf16[8,2,128,128]{3,2,1,0:T(8,128)(2,1)} custom-call(bf16[128,5120]{1,0:T(8,128)(2,1)} %bitcast.21, bf16[128,5120]{1,0:T(8,128)(2,1)} %bitcast.24), custom_call_target="tpu_custom_call" | custom-call | bytes 1048576 | tf_op jit(solution)/shard_map/pack/pallas_call | solution.py:49
  44.3 33.0 %pack.10 = bf16[8,2,128,256]{3,2,1,0:T(8,128)(2,1)} custom-call(bf16[128,5120]{1,0:T(8,128)(2,1)} %bitcast.28, bf16[128,5120]{1,0:T(8,128)(2,1)} %bitcast.31), custom_call_target="tpu_custom_call" | custom-call | bytes 2097152 | tf_op jit(solution)/shard_map/pack/pallas_call | solution.py:49
  82.4 33.0 %pack.9 = bf16[8,2,128,256]{3,2,1,0:T(8,128)(2,1)} custom-call(bf16[128,5120]{1,0:T(8,128)(2,1)} %bitcast.22, bf16[128,5120]{1,0:T(8,128)(2,1)} %bitcast.25), custom_call_target="tpu_custom_call" | custom-call | bytes 2097152 | tf_op jit(solution)/shard_map/pack/pallas_call | solution.py:49
  119.7 33.0 %pack.11 = bf16[8,2,128,256]{3,2,1,0:T(8,128)(2,1)} custom-call(bf16[128,5120]{1,0:T(8,128)(2,1)} %bitcast.23, bf16[128,5120]{1,0:T(8,128)(2,1)} %bitcast.26), custom_call_target="tpu_custom_call" | custom-call | bytes 2097152 | tf_op jit(solution)/shard_map/pack/pallas_call | solution.py:49
  158.6 4.5 collective-permute-start.1
  163.1 33.0 %pack.8 = bf16[8,2,128,256]{3,2,1,0:T(8,128)(2,1)} custom-call(bf16[128,5120]{1,0:T(8,128)(2,1)} %bitcast.29, bf16[128,5120]{1,0:T(8,128)(2,1)} %bitcast.32), custom_call_target="tpu_custom_call" | custom-call | bytes 2097152 | tf_op jit(solution)/shard_map/pack/pallas_call | solution.py:49
  213.4 7.9 %attention.3 = (bf16[8,2,128,128]{3,2,1,0:T(8,128)(2,1)S(1)}, f32[8,2,128,128]{3,2,1,0:T(8,128)S(1)}, bf16[8,2,128,128]{3,2,1,0:T(8,128)(2,1)S(1)}) custom-call(bf16[2,1536,128]{2,1,0:T(8,128)(2,1)S(1)} %bitcast.18, bf16[512,128]{1,0:T(8,128)(2,1)S(1)} %fusion.16.class_ref, bf16[8,2,128,128]{3,2,1,0:T(8,128)(2,1)S(1)} %copy-done.8, ...), custom_call_target="tpu_custom_call" | custom-call | flops 4831838208 | bytes 4718592 | tf_op jit(solution)/shard_map/attention/pallas_call | solution.py:164
  224.9 4.3 all-to-all-start.2
  230.4 16.1 %attention.4 = (bf16[8,2,128,256]{3,2,1,0:T(8,128)(2,1)S(1)}, f32[8,2,128,256]{3,2,1,0:T(8,128)}, bf16[8,2,128,256]{3,2,1,0:T(8,128)(2,1)S(1)}) custom-call(bf16[2,1536,128]{2,1,0:T(8,128)(2,1)S(1)} %bitcast.19, bf16[512,128]{1,0:T(8,128)(2,1)S(1)} %fusion.16.class_ref, bf16[8,2,128,256]{3,2,1,0:T(8,128)(2,1)} %all-to-all-done.3.q_ref.c_ref, ...), custom_call_target="tpu_custom_call" | custom-call | flops 9663676416 | bytes 9437184 | tf_op jit(solution)/shard_map/attention/pallas_call | solution.py:164
  248.4 4.4 all-to-all-start.5
  254.4 16.0 %attention.5 = (bf16[8,2,128,256]{3,2,1,0:T(8,128)(2,1)}, f32[8,2,128,256]{3,2,1,0:T(8,128)}, bf16[8,2,128,256]{3,2,1,0:T(8,128)(2,1)S(1)}) custom-call(bf16[2,1536,128]{2,1,0:T(8,128)(2,1)S(1)} %bitcast.20, bf16[512,128]{1,0:T(8,128)(2,1)S(1)} %fusion.16.class_ref, bf16[8,2,128,256]{3,2,1,0:T(8,128)(2,1)S(1)} %all-to-all-done.6.q_ref.c_ref, ...), custom_call_target="tpu_custom_call" | custom-call | flops 9663676416 | bytes 9437184 | tf_op jit(solution)/shard_map/attention/pallas_call | solution.py:164
  271.4 4.3 all-to-all-start.8
  276.9 4.3 collective-permute-done.4
  284.4 6.7 %all-to-all-done.8.refs_0_ = bf16[8,2,128,256]{3,2,1,0:T(8,128)(2,1)S(1)} async-done(((bf16[8,2,128,256]{3,2,1,0:T(8,128)(2,1)}), bf16[8,2,128,256]{3,2,1,0:T(8,128)(2,1)S(1)}, u32[]{:S(2)}, u32[]{:S(2)}) %all-to-all-start.8) | async-done | bytes 1048608 | tf_op jit(solution)/shard_map/all_to_all | solution.py:244
  295.6 9.0 %collective-permute-done.5 = bf16[8,2,128,256]{3,2,1,0:T(8,128)(2,1)} collective-permute-done((bf16[8,2,128,256]{3,2,1,0:T(8,128)(2,1)S(1)}, bf16[8,2,128,256]{3,2,1,0:T(8,128)(2,1)}, u32[]{:S(2)}, u32[]{:S(2)}) %collective-permute-start.5) | collective-permute-done | bytes 1048608 | tf_op jit(solution)/shard_map/ppermute | solution.py:261
  316.5 16.1 %collective-permute-done.3 = bf16[8,2,128,128]{3,2,1,0:T(8,128)(2,1)S(1)} collective-permute-done((bf16[8,2,128,128]{3,2,1,0:T(8,128)(2,1)S(1)}, bf16[8,2,128,128]{3,2,1,0:T(8,128)(2,1)S(1)}, u32[]{:S(2)}, u32[]{:S(2)}) %collective-permute-start.3) | collective-permute-done | bytes 524320 | tf_op jit(solution)/shard_map/ppermute | solution.py:261
  337.5 33.0 %unpack.6 = (bf16[128,5120]{1,0:T(8,128)(2,1)}, bf16[128,5120]{1,0:T(8,128)(2,1)}) custom-call(bf16[8,2,128,256]{3,2,1,0:T(8,128)(2,1)} %copy-done.18), custom_call_target="tpu_custom_call" | custom-call | bytes 2097152 | tf_op jit(solution)/shard_map/unpack/pallas_call | solution.py:83
  370.5 33.0 %unpack.7 = (bf16[128,5120]{1,0:T(8,128)(2,1)}, bf16[128,5120]{1,0:T(8,128)(2,1)}) custom-call(bf16[8,2,128,256]{3,2,1,0:T(8,128)(2,1)} %all-to-all-done.5.refs_0_, bf16[128,5120]{1,0:T(8,128)(2,1)} %get-tuple-element.28.refs_1_, bf16[128,5120]{1,0:T(8,128)(2,1)} %get-tuple-element.29.refs_2_), custom_call_target="tpu_custom_call", output_to_operand_aliasing={{0}: (1, {}), {1}: (2, {})} | custom-call | bytes 2097152 | tf_op jit(solution)/shard_map/unpack/pallas_call | solution.py:83
  403.5 17.1 %unpack.8 = (bf16[128,5120]{1,0:T(8,128)(2,1)}, bf16[128,5120]{1,0:T(8,128)(2,1)}) custom-call(bf16[8,2,128,128]{3,2,1,0:T(8,128)(2,1)} %all-to-all-done.2.refs_0_, bf16[128,5120]{1,0:T(8,128)(2,1)} %get-tuple-element.30.refs_1_, bf16[128,5120]{1,0:T(8,128)(2,1)} %get-tuple-element.31.refs_2_), custom_call_target="tpu_custom_call", output_to_operand_aliasing={{0}: (1, {}), {1}: (2, {})} | custom-call | bytes 1048576 | tf_op jit(solution)/shard_map/unpack/pallas_call | solution.py:83
  420.6 33.0 %unpack.9 = (bf16[128,5120]{1,0:T(8,128)(2,1)}, bf16[128,5120]{1,0:T(8,128)(2,1)}) custom-call(bf16[8,2,128,256]{3,2,1,0:T(8,128)(2,1)} %all-to-all-done.11.refs_0_), custom_call_target="tpu_custom_call" | custom-call | bytes 2097152 | tf_op jit(solution)/shard_map/unpack/pallas_call | solution.py:83
  453.6 33.0 %unpack.10 = (bf16[128,5120]{1,0:T(8,128)(2,1)}, bf16[128,5120]{1,0:T(8,128)(2,1)}) custom-call(bf16[8,2,128,256]{3,2,1,0:T(8,128)(2,1)} %copy-done.17, bf16[128,5120]{1,0:T(8,128)(2,1)} %get-tuple-element.40.refs_1_, bf16[128,5120]{1,0:T(8,128)(2,1)} %get-tuple-element.41.refs_2_), custom_call_target="tpu_custom_call", output_to_operand_aliasing={{0}: (1, {}), {1}: (2, {})} | custom-call | bytes 2097152 | tf_op jit(solution)/shard_map/unpack/pallas_call | solution.py:83
  487.5 17.1 %unpack.11 = (bf16[128,5120]{1,0:T(8,128)(2,1)}, bf16[128,5120]{1,0:T(8,128)(2,1)}) custom-call(bf16[8,2,128,128]{3,2,1,0:T(8,128)(2,1)} %copy-done.19, bf16[128,5120]{1,0:T(8,128)(2,1)} %get-tuple-element.42.refs_1_, bf16[128,5120]{1,0:T(8,128)(2,1)} %get-tuple-element.43.refs_2_), custom_call_target="tpu_custom_call", output_to_operand_aliasing={{0}: (1, {}), {1}: (2, {})} | custom-call | bytes 1048576 | tf_op jit(solution)/shard_map/unpack/pallas_call | solution.py:83
  (104 shorter events, 72.2 us)
Async XLA Ops:
  0.6 114.8 %copy-start = (s32[8,2,2,10]{3,2,1,0:T(2,128)S(1)}, s32[8,2,2,10]{3,2,1,0:T(2,128)}, u32[]{:S(2)}) copy-start(s32[8,2,2,10]{3,2,1,0:T(2,128)} %param.11) | copy-start | bytes 3844
  17.8 22.3 %all-to-all-start = ((bf16[8,2,128,128]{3,2,1,0:T(8,128)(2,1)}), bf16[8,2,128,128]{3,2,1,0:T(8,128)(2,1)S(1)}, u32[]{:S(2)}, u32[]{:S(2)}) async-start(bf16[8,2,128,128]{3,2,1,0:T(8,128)(2,1)} %pack.6), calls=%async_computation | async-start | bytes 1048576 | tf_op jit(solution)/shard_map/all_to_all | solution.py:244
  40.1 37.2 %copy-start.7 = (bf16[8,2,128,128]{3,2,1,0:T(8,128)(2,1)}, bf16[8,2,128,128]{3,2,1,0:T(8,128)(2,1)S(1)}, u32[]{:S(2)}) copy-start(bf16[8,2,128,128]{3,2,1,0:T(8,128)(2,1)S(1)} %all-to-all-done.q_ref.c_ref) | copy-start | bytes 1572868
  40.1 37.2 %all-to-all-start.1 = ((bf16[8,2,128,128]{3,2,1,0:T(8,128)(2,1)}), bf16[8,2,128,128]{3,2,1,0:T(8,128)(2,1)S(1)}, u32[]{:S(2)}, u32[]{:S(2)}) async-start(bf16[8,2,128,128]{3,2,1,0:T(8,128)(2,1)} %pack.7), calls=%async_computation.1 | async-start | bytes 1048576 | tf_op jit(solution)/shard_map/all_to_all | solution.py:244
  78.2 37.3 %all-to-all-start.6 = ((bf16[8,2,128,256]{3,2,1,0:T(8,128)(2,1)}), bf16[8,2,128,256]{3,2,1,0:T(8,128)(2,1)S(1)}, u32[]{:S(2)}, u32[]{:S(2)}) async-start(bf16[8,2,128,256]{3,2,1,0:T(8,128)(2,1)} %pack.10), calls=%async_computation.6 | async-start | bytes 2097152 | tf_op jit(solution)/shard_map/all_to_all | solution.py:244
  115.4 38.3 %all-to-all-start.4 = ((bf16[8,2,128,256]{3,2,1,0:T(8,128)(2,1)}), bf16[8,2,128,256]{3,2,1,0:T(8,128)(2,1)S(1)}, u32[]{:S(2)}, u32[]{:S(2)}) async-start(bf16[8,2,128,256]{3,2,1,0:T(8,128)(2,1)} %pack.9), calls=%async_computation.4 | async-start | bytes 2097152 | tf_op jit(solution)/shard_map/all_to_all | solution.py:244
  119.7 34.0 %copy-start.20 = (s32[16]{0:T(128)S(1)}, s32[16]{0:T(128)}, u32[]{:S(2)}) copy-start(s32[16]{0:T(128)} %param.10) | copy-start | bytes 196
  153.8 45.7 %all-to-all-start.7 = ((bf16[8,2,128,256]{3,2,1,0:T(8,128)(2,1)}), bf16[8,2,128,256]{3,2,1,0:T(8,128)(2,1)S(1)}, u32[]{:S(2)}, u32[]{:S(2)}) async-start(bf16[8,2,128,256]{3,2,1,0:T(8,128)(2,1)} %pack.11), calls=%async_computation.7 | async-start | bytes 2097152 | tf_op jit(solution)/shard_map/all_to_all | solution.py:244
  158.6 70.6 %collective-permute-start.1 = (bf16[8,2,128,256]{3,2,1,0:T(8,128)(2,1)S(1)}, bf16[8,2,128,256]{3,2,1,0:T(8,128)(2,1)}, u32[]{:S(2)}, u32[]{:S(2)}) collective-permute-start(bf16[8,2,128,256]{3,2,1,0:T(8,128)(2,1)S(1)} %all-to-all-done.4.kc_ref.vc_ref), channel_id=1, source_target_pairs={{0,8},{8,16},{16,24},{1,9},{9,17},{17,25},{2,10},{10,18},{18,26},{... | collective-permute-start | bytes 3145736 | tf_op jit(solution)/shard_map/ppermute | solution.py:252
  196.1 15.1 %collective-permute-start = (bf16[8,2,128,128]{3,2,1,0:T(8,128)(2,1)}, bf16[8,2,128,128]{3,2,1,0:T(8,128)(2,1)}, u32[]{:S(2)}, u32[]{:S(2)}) collective-permute-start(bf16[8,2,128,128]{3,2,1,0:T(8,128)(2,1)} %copy-done.9), channel_id=1, source_target_pairs={{0,8},{8,16},{16,24},{1,9},{9,17},{17,25},{2,10},{10,18},{18,26},{... | collective-permute-start | bytes 1572872 | tf_op jit(solution)/shard_map/ppermute | solution.py:252
  199.5 25.4 %all-to-all-start.3 = ((bf16[8,2,128,256]{3,2,1,0:T(8,128)(2,1)}), bf16[8,2,128,256]{3,2,1,0:T(8,128)(2,1)}, u32[]{:S(2)}, u32[]{:S(2)}) async-start(bf16[8,2,128,256]{3,2,1,0:T(8,128)(2,1)} %pack.8), calls=%async_computation.3 | async-start | bytes 2097152 | tf_op jit(solution)/shard_map/all_to_all | solution.py:244
  204.8 49.6 %collective-permute-start.2 = (bf16[8,2,128,256]{3,2,1,0:T(8,128)(2,1)S(1)}, bf16[8,2,128,256]{3,2,1,0:T(8,128)(2,1)}, u32[]{:S(2)}, u32[]{:S(2)}) collective-permute-start(bf16[8,2,128,256]{3,2,1,0:T(8,128)(2,1)S(1)} %all-to-all-done.7.kc_ref.vc_ref), channel_id=1, source_target_pairs={{0,8},{8,16},{16,24},{1,9},{9,17},{17,25},{2,10},{10,18},{18,26},{... | collective-permute-start | bytes 3145736 | tf_op jit(solution)/shard_map/ppermute | solution.py:252
  224.9 23.5 %all-to-all-start.2 = ((bf16[8,2,128,128]{3,2,1,0:T(8,128)(2,1)}), bf16[8,2,128,128]{3,2,1,0:T(8,128)(2,1)}, u32[]{:S(2)}, u32[]{:S(2)}) async-start(bf16[8,2,128,128]{3,2,1,0:T(8,128)(2,1)} %copy-done.11), calls=%async_computation.2 | async-start | bytes 1048576 | tf_op jit(solution)/shard_map/all_to_all | solution.py:244
  248.4 22.9 %all-to-all-start.5 = ((bf16[8,2,128,256]{3,2,1,0:T(8,128)(2,1)}), bf16[8,2,128,256]{3,2,1,0:T(8,128)(2,1)}, u32[]{:S(2)}, u32[]{:S(2)}) async-start(bf16[8,2,128,256]{3,2,1,0:T(8,128)(2,1)} %copy-done.3), calls=%async_computation.5 | async-start | bytes 2097152 | tf_op jit(solution)/shard_map/all_to_all | solution.py:244
  252.8 28.4 %collective-permute-start.4 = (bf16[8,2,128,256]{3,2,1,0:T(8,128)(2,1)}, bf16[8,2,128,256]{3,2,1,0:T(8,128)(2,1)}, u32[]{:S(2)}, u32[]{:S(2)}) collective-permute-start(bf16[8,2,128,256]{3,2,1,0:T(8,128)(2,1)} %copy-done.12), channel_id=1, source_target_pairs={{8,0},{16,8},{24,16},{9,1},{17,9},{25,17},{10,2},{18,10},{26,18},{... | collective-permute-start | bytes 3145736 | tf_op jit(solution)/shard_map/ppermute | solution.py:261
  271.4 19.7 %all-to-all-start.8 = ((bf16[8,2,128,256]{3,2,1,0:T(8,128)(2,1)}), bf16[8,2,128,256]{3,2,1,0:T(8,128)(2,1)S(1)}, u32[]{:S(2)}, u32[]{:S(2)}) async-start(bf16[8,2,128,256]{3,2,1,0:T(8,128)(2,1)} %get-tuple-element.27), calls=%async_computation.8 | async-start | bytes 2097152 | tf_op jit(solution)/shard_map/all_to_all | solution.py:244
  275.6 28.9 %collective-permute-start.5 = (bf16[8,2,128,256]{3,2,1,0:T(8,128)(2,1)S(1)}, bf16[8,2,128,256]{3,2,1,0:T(8,128)(2,1)}, u32[]{:S(2)}, u32[]{:S(2)}) collective-permute-start(bf16[8,2,128,256]{3,2,1,0:T(8,128)(2,1)S(1)} %copy-done.14), channel_id=1, source_target_pairs={{8,0},{16,8},{24,16},{9,1},{17,9},{25,17},{10,2},{18,10},{26,18},{... | collective-permute-start | bytes 3145736 | tf_op jit(solution)/shard_map/ppermute | solution.py:261
  292.0 18.9 %all-to-all-start.10 = ((bf16[8,2,128,256]{3,2,1,0:T(8,128)(2,1)}), bf16[8,2,128,256]{3,2,1,0:T(8,128)(2,1)S(1)}, u32[]{:S(2)}, u32[]{:S(2)}) async-start(bf16[8,2,128,256]{3,2,1,0:T(8,128)(2,1)} %add_convert_fusion.1), calls=%async_computation.10 | async-start | bytes 2097152 | tf_op jit(solution)/shard_map/all_to_all | solution.py:244
  307.7 7.5 %copy-start.16 = (bf16[8,2,128,128]{3,2,1,0:T(8,128)(2,1)S(1)}, bf16[8,2,128,128]{3,2,1,0:T(8,128)(2,1)}, u32[]{:S(2)}) copy-start(bf16[8,2,128,128]{3,2,1,0:T(8,128)(2,1)} %copy-done.15) | copy-start | bytes 1572868
  307.7 25.0 %copy-start.2 = (f32[8,2,128,128]{3,2,1,0:T(8,128)S(1)}, f32[8,2,128,128]{3,2,1,0:T(8,128)}, u32[]{:S(2)}) copy-start(f32[8,2,128,128]{3,2,1,0:T(8,128)} %copy-done.1) | copy-start | bytes 3145732
  310.9 22.6 %copy-start.17 = (bf16[8,2,128,256]{3,2,1,0:T(8,128)(2,1)}, bf16[8,2,128,256]{3,2,1,0:T(8,128)(2,1)S(1)}, u32[]{:S(2)}) copy-start(bf16[8,2,128,256]{3,2,1,0:T(8,128)(2,1)S(1)} %all-to-all-done.10.refs_0_) | copy-start | bytes 3145732
  310.9 22.6 %all-to-all-start.11 = ((bf16[8,2,128,256]{3,2,1,0:T(8,128)(2,1)}), bf16[8,2,128,256]{3,2,1,0:T(8,128)(2,1)}, u32[]{:S(2)}, u32[]{:S(2)}) async-start(bf16[8,2,128,256]{3,2,1,0:T(8,128)(2,1)} %add_convert_fusion), calls=%async_computation.11 | async-start | bytes 2097152 | tf_op jit(solution)/shard_map/all_to_all | solution.py:244
  315.2 17.4 %collective-permute-start.3 = (bf16[8,2,128,128]{3,2,1,0:T(8,128)(2,1)S(1)}, bf16[8,2,128,128]{3,2,1,0:T(8,128)(2,1)S(1)}, u32[]{:S(2)}, u32[]{:S(2)}) collective-permute-start(bf16[8,2,128,128]{3,2,1,0:T(8,128)(2,1)S(1)} %copy-done.16), channel_id=1, source_target_pairs={{8,0},{16,8},{24,16},{9,1},{17,9},{25,17},{10,2},{18,10},{26,18},{... | collective-permute-start | bytes 1572872 | tf_op jit(solution)/shard_map/ppermute | solution.py:261
  333.6 153.1 %all-to-all-start.9 = ((bf16[8,2,128,128]{3,2,1,0:T(8,128)(2,1)}), bf16[8,2,128,128]{3,2,1,0:T(8,128)(2,1)S(1)}, u32[]{:S(2)}, u32[]{:S(2)}) async-start(bf16[8,2,128,128]{3,2,1,0:T(8,128)(2,1)} %add_convert_fusion.2), calls=%async_computation.9 | async-start | bytes 1048576 | tf_op jit(solution)/shard_map/all_to_all | solution.py:244
  (15 other events, 22.5 us)

commit v2 on v1

--- a/solution.py
+++ b/solution.py
@@ -20,78 +20,59 @@
 VMEM_LIMIT = 48 * 1024 * 1024
 
 
-def run_copies(copies):
-    for copy in copies:
-        copy.start()
-    for copy in copies:
-        copy.wait()
-
-
-def pack(arrays, members, heads, first, count):
+def pack(arrays, members, heads, chunks):
     n = len(arrays)
     tokens = arrays[0].shape[0]
-    width = count * HEAD_DIM
 
     def body(*refs):
-        ins, out, sems = refs[:n], refs[n], refs[n + 1]
-        run_copies(
-            [
-                pltpu.make_async_copy(
-                    ins[a].at[:, pl.ds((p * heads + first) * HEAD_DIM, width)],
-                    out.at[p, a],
-                    sems.at[p * n + a],
-                )
-                for p in range(members)
-                for a in range(n)
-            ]
-        )
+        ins, outs = refs[:n], refs[n:]
+        for (first, count), out in zip(chunks, outs):
+            for a in range(n):
+                out[0, a] = ins[a][:, first * HEAD_DIM : (first + count) * HEAD_DIM]
 
     return pl.pallas_call(
         body,
-        out_shape=jax.ShapeDtypeStruct((members, n, tokens, width), arrays[0].dtype),
-        in_specs=[pl.BlockSpec(memory_space=pl.ANY)] * n,
-        out_specs=pl.BlockSpec(memory_space=pl.ANY),
-        scratch_shapes=[pltpu.SemaphoreType.DMA((members * n,))],
+        grid=(members,),
+        out_shape=[
+            jax.ShapeDtypeStruct((members, n, tokens, count * HEAD_DIM), arrays[0].dtype)
+            for _, count in chunks
+        ],
+        in_specs=[pl.BlockSpec((tokens, heads * HEAD_DIM), lambda p: (0, p))] * n,
+        out_specs=[
+            pl.BlockSpec((1, n, tokens, count * HEAD_DIM), lambda p: (p, 0, 0, 0))
+            for _, count in chunks
+        ],
         cost_estimate=pl.CostEstimate(
-            flops=0, bytes_accessed=4 * members * n * tokens * width, transcendentals=0
+            flops=0, bytes_accessed=4 * n * arrays[0].size, transcendentals=0
         ),
         name="pack",
     )(*arrays)
 
 
-def unpack(received, outputs, shape, heads, first, count):
-    members, n, tokens, width = received.shape
-    filled = outputs is not None
+def unpack(received, members, heads, chunks):
+    n, tokens = received[0].shape[1:3]
 
     def body(*refs):
-        source = refs[0]
-        outs = refs[1 + n : 1 + 2 * n] if filled else refs[1 : 1 + n]
-        sems = refs[-1]
-        run_copies(
-            [
-                pltpu.make_async_copy(
-                    source.at[p, a],
-                    outs[a].at[:, pl.ds((p * heads + first) * HEAD_DIM, width)],
-                    sems.at[p * n + a],
-                )
-                for p in range(members)
-                for a in range(n)
-            ]
-        )
-
-    args = (received,) + (tuple(outputs) if filled else ())
+        ins, outs = refs[: len(chunks)], refs[len(chunks) :]
+        for (first, count), source in zip(chunks, ins):
+            for a in range(n):
+                outs[a][:, first * HEAD_DIM : (first + count) * HEAD_DIM] = source[0, a]
+
+    shape = (tokens, members * heads * HEAD_DIM)
     return pl.pallas_call(
         body,
-        out_shape=[jax.ShapeDtypeStruct(shape, received.dtype)] * n,
-        in_specs=[pl.BlockSpec(memory_space=pl.ANY)] * len(args),
-        out_specs=[pl.BlockSpec(memory_space=pl.ANY)] * n,
-        scratch_shapes=[pltpu.SemaphoreType.DMA((members * n,))],
-        input_output_aliases={1 + a: a for a in range(n)} if filled else {},
+        grid=(members,),
+        out_shape=[jax.ShapeDtypeStruct(shape, received[0].dtype)] * n,
+        in_specs=[
+            pl.BlockSpec((1, n, tokens, count * HEAD_DIM), lambda p: (p, 0, 0, 0))
+            for _, count in chunks
+        ],
+        out_specs=[pl.BlockSpec((tokens, heads * HEAD_DIM), lambda p: (0, p))] * n,
         cost_estimate=pl.CostEstimate(
-            flops=0, bytes_accessed=4 * members * n * tokens * width, transcendentals=0
+            flops=0, bytes_accessed=4 * n * math.prod(shape), transcendentals=0
         ),
         name="unpack",
-    )(*args)
+    )(*received)
 
 
 def attention_body(
@@ -246,23 +227,24 @@
     chunks = [(first, count) for first, count in CHUNKS if first + count <= heads]
     if sum(count for _, count in chunks) != heads:
         chunks = [(0, heads)]
+    kv_sent = pack((k, v), members, heads, chunks)
+    qc_sent = pack((q, c), members, heads, chunks)
     received = []
-    for first, count in chunks:
-        kv = exchange(pack((k, v), members, heads, first, count))
-        kv_prev = lax.ppermute(kv, "plane", up)
-        qc = exchange(pack((q, c), members, heads, first, count))
-        received.append((qc, kv, kv_prev))
+    for kv_part, qc_part in zip(kv_sent, qc_sent):
+        kv = exchange(kv_part)
+        received.append((exchange(qc_part), kv, lax.ppermute(kv, "plane", up)))
     bias, classes = mask_operands(
         frame_blocks, tile_lists, z, bands, queries.shape[1] * bands, queries.shape[2]
     )
-    out_odq = out_dkv = None
-    for (first, count), (qc, kv, kv_prev) in zip(chunks, received):
+    odq_back, dkv_back = [], []
+    for qc, kv, kv_prev in received:
         odq, dkv, dkv_prev = attention(bias, classes, qc, kv, kv_prev)
         dkv_next = lax.ppermute(dkv_prev, "plane", down)
-        out_odq = unpack(exchange(odq), out_odq, q.shape, heads, first, count)
+        odq_back.append(exchange(odq))
         total = (dkv + dkv_next.astype(jnp.float32)).astype(jnp.bfloat16)
-        out_dkv = unpack(exchange(total), out_dkv, q.shape, heads, first, count)
-    return tuple(array.reshape(queries.shape) for array in (*out_odq, *out_dkv))
+        dkv_back.append(exchange(total))
+    outputs = unpack(odq_back, members, heads, chunks) + unpack(dkv_back, members, heads, chunks)
+    return tuple(array.reshape(queries.shape) for array in outputs)
 
 
 def solution(mesh):

time: 506 us -> 246 us (0.49)
  Pallas kernels: 373 us -> 64.5 us
  waiting for transfers between devices: 42.1 us -> 81.4 us
  blocking collectives: 0 us -> 13.9 us
    pallas_call x12 -> x4, Pallas kernels: 333 us -> 23.8 us  [the longest x2 12 us: pack(): pl.pallas_call(body, grid=(members,), out_shape=[jax.ShapeDtypeStruct((me...]
    all_to_all x12 -> x11, waiting for transfers between devices: 9.95 us -> 63.5 us  [exchange(): return lax.all_to_all(array, group, split_axis=0, concat_axis=0, tiled=True)]
    all_to_all x0 -> x1, blocking collectives: none -> 13.9 us  [exchange(): return lax.all_to_all(array, group, split_axis=0, concat_axis=0, tiled=True)]
    ppermute x3, waiting for transfers between devices: 29.4 us -> 17.9 us  [on_device(): dkv_next = lax.ppermute(dkv_prev, 'plane', down)]
    all_to_all x12 -> x11, starting transfers between devices: 50.9 us -> 44.4 us  [exchange(): return lax.all_to_all(array, group, split_axis=0, concat_axis=0, tiled=True)]
    unnamed x42 -> x36, local copies, waits for them, and re-layouts: 12.3 us -> 9.17 us
  transfers between devices with their start and end apart: 18 -> 17, of which waited for: 6 -> 10; matrix products, arithmetic and copies ran while one was open for 2% -> 5% of each run, Pallas kernels for 67% -> 22%
where the time goes in v2:
time: 246 us; the launch traced here: 244 us
  waiting for transfers between devices  81.4 us (33%)
  Pallas kernels  64.5 us (26%)
  starting transfers between devices  62.8 us (26%)
  blocking collectives  13.9 us (6%)
  other arithmetic  10.5 us (4%)
  local copies, waits for them, and re-layouts  10 us (4%)
    all_to_all x11, waiting for transfers between devices, exchange(): return lax.all_to_all(array, group, split_axis=0, concat_axis=0, tiled=True)  63.5 us
    all_to_all x11, starting transfers between devices, exchange(): return lax.all_to_all(array, group, split_axis=0, concat_axis=0, tiled=True)  44.4 us
    pallas_call x3, Pallas kernels, attention(): pl.pallas_call(attention_body, grid=(heads,), out_shape=[jax.ShapeDtypeSt...  40.7 us
    ppermute x3, waiting for transfers between devices, on_device(): dkv_next = lax.ppermute(dkv_prev, 'plane', down)  17.9 us
    ppermute x3, starting transfers between devices, on_device(): received.append((exchange(qc_part), kv, lax.ppermute(kv, 'plane', up)))  14.3 us
    all_to_all x1, blocking collectives, exchange(): return lax.all_to_all(array, group, split_axis=0, concat_axis=0, tiled=True)  13.9 us
    pallas_call x2, Pallas kernels, pack(): pl.pallas_call(body, grid=(members,), out_shape=[jax.ShapeDtypeStruct((me...  12 us
    pallas_call x2, Pallas kernels, unpack(): pl.pallas_call(body, grid=(members,), out_shape=[jax.ShapeDtypeStruct(sha...  11.8 us
  transfers between devices with their start and end apart: 17, of which 10 were waited for; matrix products, arithmetic and copies ran while one was open for 5% of the time, Pallas kernels for 22%

profile of v2, /device:TPU:0, one launch (start us, length us, event | category | flops | bytes accessed | tf_op | source)
XLA Modules:
  0.0 244.1 jit_solution(17868558294983274724)
XLA Ops:
  0.6 6.0 %pack.2 = (bf16[8,2,128,256]{3,2,1,0:T(8,128)(2,1)}, bf16[8,2,128,256]{3,2,1,0:T(8,128)(2,1)}, bf16[8,2,128,128]{3,2,1,0:T(8,128)(2,1)}) custom-call(bf16[128,5120]{1,0:T(8,128)(2,1)} %bitcast.21, bf16[128,5120]{1,0:T(8,128)(2,1)} %bitcast.22), custom_call_target="tpu_custom_call" | custom-call | bytes 5242880 | tf_op jit(solution)/shard_map/pack/pallas_call | solution.py:33
  6.6 5.2 %all-to-all-start.6 = ((bf16[8,2,128,128]{3,2,1,0:T(8,128)(2,1)}), bf16[8,2,128,128]{3,2,1,0:T(8,128)(2,1)S(1)}, u32[]{:S(2)}, u32[]{:S(2)}) async-start(bf16[8,2,128,128]{3,2,1,0:T(8,128)(2,1)} %get-tuple-element.29), calls=%async_computation.6 | async-start | bytes 1048576 | tf_op jit(solution)/shard_map/all_to_all | solution.py:225
  11.8 6.0 %pack.3 = (bf16[8,2,128,256]{3,2,1,0:T(8,128)(2,1)}, bf16[8,2,128,256]{3,2,1,0:T(8,128)(2,1)}, bf16[8,2,128,128]{3,2,1,0:T(8,128)(2,1)}) custom-call(bf16[128,5120]{1,0:T(8,128)(2,1)} %bitcast.23, bf16[128,5120]{1,0:T(8,128)(2,1)} %bitcast.24), custom_call_target="tpu_custom_call" | custom-call | bytes 5242880 | tf_op jit(solution)/shard_map/pack/pallas_call | solution.py:33
  21.6 13.9 %all_to_all.60.kc_ref.vc_ref = bf16[8,2,128,128]{3,2,1,0:T(8,128)(2,1)} all-to-all(bf16[8,2,128,128]{3,2,1,0:T(8,128)(2,1)} %get-tuple-element.30), channel_id=1, replica_groups=mesh['plane'=4,'half'=2,'band'=4] {'half','band'}, dimensions={0} | all-to-all | bytes 1048576 | tf_op jit(solution)/shard_map/all_to_all | solution.py:225
  39.8 14.6 %all-to-all-done.q_ref.c_ref = bf16[8,2,128,256]{3,2,1,0:T(8,128)(2,1)S(1)} async-done(((bf16[8,2,128,256]{3,2,1,0:T(8,128)(2,1)}), bf16[8,2,128,256]{3,2,1,0:T(8,128)(2,1)S(1)}, u32[]{:S(2)}, u32[]{:S(2)}) %all-to-all-start) | async-done | bytes 1048608 | tf_op jit(solution)/shard_map/all_to_all | solution.py:225
  58.7 14.7 %all-to-all-done.3.q_ref.c_ref = bf16[8,2,128,256]{3,2,1,0:T(8,128)(2,1)S(1)} async-done(((bf16[8,2,128,256]{3,2,1,0:T(8,128)(2,1)}), bf16[8,2,128,256]{3,2,1,0:T(8,128)(2,1)S(1)}, u32[]{:S(2)}, u32[]{:S(2)}) %all-to-all-start.3) | async-done | bytes 1048608 | tf_op jit(solution)/shard_map/all_to_all | solution.py:225
  77.4 4.3 %collective-permute-start.2 = (bf16[8,2,128,128]{3,2,1,0:T(8,128)(2,1)}, bf16[8,2,128,128]{3,2,1,0:T(8,128)(2,1)}, u32[]{:S(2)}, u32[]{:S(2)}) collective-permute-start(bf16[8,2,128,128]{3,2,1,0:T(8,128)(2,1)} %all_to_all.60.kc_ref.vc_ref), channel_id=1, source_target_pairs={{0,8},{8,16},{16,24},{1,9},{9,17},{17,25},{2,10},{10,18},{18,26},{... | collective-permute-start | bytes 1572872 | tf_op jit(solution)/shard_map/ppermute | solution.py:235
  81.7 10.6 %all-to-all-done.4.kc_ref.vc_ref = bf16[8,2,128,256]{3,2,1,0:T(8,128)(2,1)S(1)} async-done(((bf16[8,2,128,256]{3,2,1,0:T(8,128)(2,1)}), bf16[8,2,128,256]{3,2,1,0:T(8,128)(2,1)S(1)}, u32[]{:S(2)}, u32[]{:S(2)}) %all-to-all-start.4) | async-done | bytes 1048608 | tf_op jit(solution)/shard_map/all_to_all | solution.py:225
  92.3 4.2 %all-to-all-start.1 = ((bf16[8,2,128,256]{3,2,1,0:T(8,128)(2,1)}), bf16[8,2,128,256]{3,2,1,0:T(8,128)(2,1)}, u32[]{:S(2)}, u32[]{:S(2)}) async-start(bf16[8,2,128,256]{3,2,1,0:T(8,128)(2,1)} %get-tuple-element.24), calls=%async_computation.1 | async-start | bytes 2097152 | tf_op jit(solution)/shard_map/all_to_all | solution.py:225
  97.6 4.5 %collective-permute-start.1 = (bf16[8,2,128,256]{3,2,1,0:T(8,128)(2,1)S(1)}, bf16[8,2,128,256]{3,2,1,0:T(8,128)(2,1)}, u32[]{:S(2)}, u32[]{:S(2)}) collective-permute-start(bf16[8,2,128,256]{3,2,1,0:T(8,128)(2,1)S(1)} %all-to-all-done.4.kc_ref.vc_ref), channel_id=1, source_target_pairs={{0,8},{8,16},{16,24},{1,9},{9,17},{17,25},{2,10},{10,18},{18,26},{... | collective-permute-start | bytes 3145736 | tf_op jit(solution)/shard_map/ppermute | solution.py:235
  104.6 8.5 %attention.5 = (bf16[8,2,128,128]{3,2,1,0:T(8,128)(2,1)S(1)}, f32[8,2,128,128]{3,2,1,0:T(8,128)S(1)}, bf16[8,2,128,128]{3,2,1,0:T(8,128)(2,1)}) custom-call(bf16[2,1536,128]{2,1,0:T(8,128)(2,1)S(1)} %bitcast.18, bf16[512,128]{1,0:T(8,128)(2,1)S(1)} %fusion.16.class_ref, bf16[8,2,128,128]{3,2,1,0:T(8,128)(2,1)S(1)} %copy-done.7, ...), custom_call_target="tpu_custom_call" | custom-call | flops 4831838208 | bytes 4718592 | tf_op jit(solution)/shard_map/attention/pallas_call | solution.py:145
  116.1 4.2 %all-to-all-start.8 = ((bf16[8,2,128,128]{3,2,1,0:T(8,128)(2,1)}), bf16[8,2,128,128]{3,2,1,0:T(8,128)(2,1)}, u32[]{:S(2)}, u32[]{:S(2)}) async-start(bf16[8,2,128,128]{3,2,1,0:T(8,128)(2,1)} %copy-done.9), calls=%async_computation.8 | async-start | bytes 1048576 | tf_op jit(solution)/shard_map/all_to_all | solution.py:225
  120.2 5.5 %collective-permute-start = (bf16[8,2,128,256]{3,2,1,0:T(8,128)(2,1)}, bf16[8,2,128,256]{3,2,1,0:T(8,128)(2,1)}, u32[]{:S(2)}, u32[]{:S(2)}) collective-permute-start(bf16[8,2,128,256]{3,2,1,0:T(8,128)(2,1)} %all-to-all-done.1.kc_ref.vc_ref), channel_id=1, source_target_pairs={{0,8},{8,16},{16,24},{1,9},{9,17},{17,25},{2,10},{10,18},{18,26},{... | collective-permute-start | bytes 3145736 | tf_op jit(solution)/shard_map/ppermute | solution.py:235
  125.8 5.1 %collective-permute-done.5 = bf16[8,2,128,128]{3,2,1,0:T(8,128)(2,1)} collective-permute-done((bf16[8,2,128,128]{3,2,1,0:T(8,128)(2,1)}, bf16[8,2,128,128]{3,2,1,0:T(8,128)(2,1)}, u32[]{:S(2)}, u32[]{:S(2)}) %collective-permute-start.5) | collective-permute-done | bytes 524320 | tf_op jit(solution)/shard_map/ppermute | solution.py:242
  133.2 4.3 %all-to-all-start.11 = ((bf16[8,2,128,128]{3,2,1,0:T(8,128)(2,1)}), bf16[8,2,128,128]{3,2,1,0:T(8,128)(2,1)}, u32[]{:S(2)}, u32[]{:S(2)}) async-start(bf16[8,2,128,128]{3,2,1,0:T(8,128)(2,1)} %add_convert_fusion.2), calls=%async_computation.11 | async-start | bytes 1048576 | tf_op jit(solution)/shard_map/all_to_all | solution.py:225
  138.6 16.1 %attention.4 = (bf16[8,2,128,256]{3,2,1,0:T(8,128)(2,1)S(1)}, f32[8,2,128,256]{3,2,1,0:T(8,128)}, bf16[8,2,128,256]{3,2,1,0:T(8,128)(2,1)S(1)}) custom-call(bf16[2,1536,128]{2,1,0:T(8,128)(2,1)S(1)} %bitcast.19, bf16[512,128]{1,0:T(8,128)(2,1)S(1)} %fusion.16.class_ref, bf16[8,2,128,256]{3,2,1,0:T(8,128)(2,1)S(1)} %all-to-all-done.3.q_ref.c_ref, ...), custom_call_target="tpu_custom_call" | custom-call | flops 9663676416 | bytes 9437184 | tf_op jit(solution)/shard_map/attention/pallas_call | solution.py:145
  156.7 4.4 %all-to-all-start.5 = ((bf16[8,2,128,256]{3,2,1,0:T(8,128)(2,1)}), bf16[8,2,128,256]{3,2,1,0:T(8,128)(2,1)}, u32[]{:S(2)}, u32[]{:S(2)}) async-start(bf16[8,2,128,256]{3,2,1,0:T(8,128)(2,1)} %copy-done.1), calls=%async_computation.5 | async-start | bytes 2097152 | tf_op jit(solution)/shard_map/all_to_all | solution.py:225
  162.7 16.1 %attention.3 = (bf16[8,2,128,256]{3,2,1,0:T(8,128)(2,1)}, f32[8,2,128,256]{3,2,1,0:T(8,128)}, bf16[8,2,128,256]{3,2,1,0:T(8,128)(2,1)S(1)}) custom-call(bf16[2,1536,128]{2,1,0:T(8,128)(2,1)S(1)} %bitcast.20, bf16[512,128]{1,0:T(8,128)(2,1)S(1)} %fusion.16.class_ref, bf16[8,2,128,256]{3,2,1,0:T(8,128)(2,1)S(1)} %all-to-all-done.q_ref.c_ref, ...), custom_call_target="tpu_custom_call" | custom-call | flops 9663676416 | bytes 9437184 | tf_op jit(solution)/shard_map/attention/pallas_call | solution.py:145
  179.7 4.2 %all-to-all-start.2 = ((bf16[8,2,128,256]{3,2,1,0:T(8,128)(2,1)}), bf16[8,2,128,256]{3,2,1,0:T(8,128)(2,1)S(1)}, u32[]{:S(2)}, u32[]{:S(2)}) async-start(bf16[8,2,128,256]{3,2,1,0:T(8,128)(2,1)} %get-tuple-element.25), calls=%async_computation.2 | async-start | bytes 2097152 | tf_op jit(solution)/shard_map/all_to_all | solution.py:225
  191.7 7.7 %all-to-all-done.2.refs_0_ = bf16[8,2,128,256]{3,2,1,0:T(8,128)(2,1)S(1)} async-done(((bf16[8,2,128,256]{3,2,1,0:T(8,128)(2,1)}), bf16[8,2,128,256]{3,2,1,0:T(8,128)(2,1)S(1)}, u32[]{:S(2)}, u32[]{:S(2)}) %all-to-all-start.2) | async-done | bytes 1048608 | tf_op jit(solution)/shard_map/all_to_all | solution.py:225
  202.9 9.5 %collective-permute-done.3 = bf16[8,2,128,256]{3,2,1,0:T(8,128)(2,1)} collective-permute-done((bf16[8,2,128,256]{3,2,1,0:T(8,128)(2,1)S(1)}, bf16[8,2,128,256]{3,2,1,0:T(8,128)(2,1)}, u32[]{:S(2)}, u32[]{:S(2)}) %collective-permute-start.3) | collective-permute-done | bytes 1048608 | tf_op jit(solution)/shard_map/ppermute | solution.py:242
  221.8 5.9 %unpack.2 = (bf16[128,5120]{1,0:T(8,128)(2,1)}, bf16[128,5120]{1,0:T(8,128)(2,1)}) custom-call(bf16[8,2,128,256]{3,2,1,0:T(8,128)(2,1)} %copy-done.14, bf16[8,2,128,256]{3,2,1,0:T(8,128)(2,1)} %all-to-all-done.5.refs_1_, bf16[8,2,128,128]{3,2,1,0:T(8,128)(2,1)} %all-to-all-done.8.refs_2_), custom_call_target="tpu_custom_call" | custom-call | bytes 5242880 | tf_op jit(solution)/shard_map/unpack/pallas_call | solution.py:62
  227.8 9.4 %all-to-all-done.9.refs_0_ = bf16[8,2,128,256]{3,2,1,0:T(8,128)(2,1)S(1)} async-done(((bf16[8,2,128,256]{3,2,1,0:T(8,128)(2,1)}), bf16[8,2,128,256]{3,2,1,0:T(8,128)(2,1)S(1)}, u32[]{:S(2)}, u32[]{:S(2)}) %all-to-all-start.9) | async-done | bytes 1048608 | tf_op jit(solution)/shard_map/all_to_all | solution.py:225
  238.2 5.9 %unpack.3 = (bf16[128,5120]{1,0:T(8,128)(2,1)}, bf16[128,5120]{1,0:T(8,128)(2,1)}) custom-call(bf16[8,2,128,256]{3,2,1,0:T(8,128)(2,1)} %copy-done.16, bf16[8,2,128,256]{3,2,1,0:T(8,128)(2,1)} %copy-done.15, bf16[8,2,128,128]{3,2,1,0:T(8,128)(2,1)} %all-to-all-done.11.refs_2_), custom_call_target="tpu_custom_call" | custom-call | bytes 5242880 | tf_op jit(solution)/shard_map/unpack/pallas_call | solution.py:62
  (89 shorter events, 52.3 us)
Async XLA Ops:
  0.6 38.5 %copy-start = (s32[8,2,2,10]{3,2,1,0:T(2,128)S(1)}, s32[8,2,2,10]{3,2,1,0:T(2,128)}, u32[]{:S(2)}) copy-start(s32[8,2,2,10]{3,2,1,0:T(2,128)} %param.11) | copy-start | bytes 3844
  6.6 14.9 %all-to-all-start.6 = ((bf16[8,2,128,128]{3,2,1,0:T(8,128)(2,1)}), bf16[8,2,128,128]{3,2,1,0:T(8,128)(2,1)S(1)}, u32[]{:S(2)}, u32[]{:S(2)}) async-start(bf16[8,2,128,128]{3,2,1,0:T(8,128)(2,1)} %get-tuple-element.29), calls=%async_computation.6 | async-start | bytes 1048576 | tf_op jit(solution)/shard_map/all_to_all | solution.py:225
  21.6 13.9 %copy-start.6 = (bf16[8,2,128,128]{3,2,1,0:T(8,128)(2,1)}, bf16[8,2,128,128]{3,2,1,0:T(8,128)(2,1)S(1)}, u32[]{:S(2)}) copy-start(bf16[8,2,128,128]{3,2,1,0:T(8,128)(2,1)S(1)} %all-to-all-done.6.q_ref.c_ref) | copy-start | bytes 1572868
  35.4 22.9 %copy-start.17 = (s32[16]{0:T(128)S(1)}, s32[16]{0:T(128)}, u32[]{:S(2)}) copy-start(s32[16]{0:T(128)} %param.10) | copy-start | bytes 196
  35.4 19.0 %all-to-all-start = ((bf16[8,2,128,256]{3,2,1,0:T(8,128)(2,1)}), bf16[8,2,128,256]{3,2,1,0:T(8,128)(2,1)S(1)}, u32[]{:S(2)}, u32[]{:S(2)}) async-start(bf16[8,2,128,256]{3,2,1,0:T(8,128)(2,1)} %get-tuple-element.23), calls=%async_computation | async-start | bytes 2097152 | tf_op jit(solution)/shard_map/all_to_all | solution.py:225
  54.5 18.9 %all-to-all-start.3 = ((bf16[8,2,128,256]{3,2,1,0:T(8,128)(2,1)}), bf16[8,2,128,256]{3,2,1,0:T(8,128)(2,1)S(1)}, u32[]{:S(2)}, u32[]{:S(2)}) async-start(bf16[8,2,128,256]{3,2,1,0:T(8,128)(2,1)} %get-tuple-element.26), calls=%async_computation.3 | async-start | bytes 2097152 | tf_op jit(solution)/shard_map/all_to_all | solution.py:225
  73.4 18.9 %all-to-all-start.4 = ((bf16[8,2,128,256]{3,2,1,0:T(8,128)(2,1)}), bf16[8,2,128,256]{3,2,1,0:T(8,128)(2,1)S(1)}, u32[]{:S(2)}, u32[]{:S(2)}) async-start(bf16[8,2,128,256]{3,2,1,0:T(8,128)(2,1)} %get-tuple-element.27), calls=%async_computation.4 | async-start | bytes 2097152 | tf_op jit(solution)/shard_map/all_to_all | solution.py:225
  77.4 24.6 %collective-permute-start.2 = (bf16[8,2,128,128]{3,2,1,0:T(8,128)(2,1)}, bf16[8,2,128,128]{3,2,1,0:T(8,128)(2,1)}, u32[]{:S(2)}, u32[]{:S(2)}) collective-permute-start(bf16[8,2,128,128]{3,2,1,0:T(8,128)(2,1)} %all_to_all.60.kc_ref.vc_ref), channel_id=1, source_target_pairs={{0,8},{8,16},{16,24},{1,9},{9,17},{17,25},{2,10},{10,18},{18,26},{... | collective-permute-start | bytes 1572872 | tf_op jit(solution)/shard_map/ppermute | solution.py:235
  92.3 23.8 %all-to-all-start.1 = ((bf16[8,2,128,256]{3,2,1,0:T(8,128)(2,1)}), bf16[8,2,128,256]{3,2,1,0:T(8,128)(2,1)}, u32[]{:S(2)}, u32[]{:S(2)}) async-start(bf16[8,2,128,256]{3,2,1,0:T(8,128)(2,1)} %get-tuple-element.24), calls=%async_computation.1 | async-start | bytes 2097152 | tf_op jit(solution)/shard_map/all_to_all | solution.py:225
  97.6 39.9 %collective-permute-start.1 = (bf16[8,2,128,256]{3,2,1,0:T(8,128)(2,1)S(1)}, bf16[8,2,128,256]{3,2,1,0:T(8,128)(2,1)}, u32[]{:S(2)}, u32[]{:S(2)}) collective-permute-start(bf16[8,2,128,256]{3,2,1,0:T(8,128)(2,1)S(1)} %all-to-all-done.4.kc_ref.vc_ref), channel_id=1, source_target_pairs={{0,8},{8,16},{16,24},{1,9},{9,17},{17,25},{2,10},{10,18},{18,26},{... | collective-permute-start | bytes 3145736 | tf_op jit(solution)/shard_map/ppermute | solution.py:235
  102.2 10.9 %copy-start.3 = (bf16[2,3,2,2,2,4,2,8,128]{8,7,6,5,4,3,2,1,0:T(8,128)(2,1)}, bf16[2,3,2,2,2,4,2,8,128]{8,7,6,5,4,3,2,1,0:T(8,128)(2,1)S(1)}, u32[]{:S(2)}) copy-start(bf16[2,3,2,2,2,4,2,8,128]{8,7,6,5,4,3,2,1,0:T(8,128)(2,1)S(1)} %broadcast_in_dim.10) | copy-start | bytes 2359300
  114.8 16.1 %collective-permute-start.5 = (bf16[8,2,128,128]{3,2,1,0:T(8,128)(2,1)}, bf16[8,2,128,128]{3,2,1,0:T(8,128)(2,1)}, u32[]{:S(2)}, u32[]{:S(2)}) collective-permute-start(bf16[8,2,128,128]{3,2,1,0:T(8,128)(2,1)} %get-tuple-element.39), channel_id=1, source_target_pairs={{8,0},{16,8},{24,16},{9,1},{17,9},{25,17},{10,2},{18,10},{26,18},{... | collective-permute-start | bytes 1572872 | tf_op jit(solution)/shard_map/ppermute | solution.py:242
  116.1 17.1 %all-to-all-start.8 = ((bf16[8,2,128,128]{3,2,1,0:T(8,128)(2,1)}), bf16[8,2,128,128]{3,2,1,0:T(8,128)(2,1)}, u32[]{:S(2)}, u32[]{:S(2)}) async-start(bf16[8,2,128,128]{3,2,1,0:T(8,128)(2,1)} %copy-done.9), calls=%async_computation.8 | async-start | bytes 1048576 | tf_op jit(solution)/shard_map/all_to_all | solution.py:225
  120.2 42.4 %collective-permute-start = (bf16[8,2,128,256]{3,2,1,0:T(8,128)(2,1)}, bf16[8,2,128,256]{3,2,1,0:T(8,128)(2,1)}, u32[]{:S(2)}, u32[]{:S(2)}) collective-permute-start(bf16[8,2,128,256]{3,2,1,0:T(8,128)(2,1)} %all-to-all-done.1.kc_ref.vc_ref), channel_id=1, source_target_pairs={{0,8},{8,16},{16,24},{1,9},{9,17},{17,25},{2,10},{10,18},{18,26},{... | collective-permute-start | bytes 3145736 | tf_op jit(solution)/shard_map/ppermute | solution.py:235
  133.2 23.6 %all-to-all-start.11 = ((bf16[8,2,128,128]{3,2,1,0:T(8,128)(2,1)}), bf16[8,2,128,128]{3,2,1,0:T(8,128)(2,1)}, u32[]{:S(2)}, u32[]{:S(2)}) async-start(bf16[8,2,128,128]{3,2,1,0:T(8,128)(2,1)} %add_convert_fusion.2), calls=%async_computation.11 | async-start | bytes 1048576 | tf_op jit(solution)/shard_map/all_to_all | solution.py:225
  156.7 5.9 %copy-start.5 = (bf16[2,3,2,2,2,4,2,8,128]{8,7,6,5,4,3,2,1,0:T(8,128)(2,1)S(1)}, bf16[2,3,2,2,2,4,2,8,128]{8,7,6,5,4,3,2,1,0:T(8,128)(2,1)}, u32[]{:S(2)}) copy-start(bf16[2,3,2,2,2,4,2,8,128]{8,7,6,5,4,3,2,1,0:T(8,128)(2,1)} %copy-done.3) | copy-start | bytes 2359300
  156.7 23.0 %all-to-all-start.5 = ((bf16[8,2,128,256]{3,2,1,0:T(8,128)(2,1)}), bf16[8,2,128,256]{3,2,1,0:T(8,128)(2,1)}, u32[]{:S(2)}, u32[]{:S(2)}) async-start(bf16[8,2,128,256]{3,2,1,0:T(8,128)(2,1)} %copy-done.1), calls=%async_computation.5 | async-start | bytes 2097152 | tf_op jit(solution)/shard_map/all_to_all | solution.py:225
  161.1 27.4 %collective-permute-start.4 = (bf16[8,2,128,256]{3,2,1,0:T(8,128)(2,1)S(1)}, bf16[8,2,128,256]{3,2,1,0:T(8,128)(2,1)}, u32[]{:S(2)}, u32[]{:S(2)}) collective-permute-start(bf16[8,2,128,256]{3,2,1,0:T(8,128)(2,1)S(1)} %copy-done.11), channel_id=1, source_target_pairs={{8,0},{16,8},{24,16},{9,1},{17,9},{25,17},{10,2},{18,10},{26,18},{... | collective-permute-start | bytes 3145736 | tf_op jit(solution)/shard_map/ppermute | solution.py:242
  179.7 19.6 %all-to-all-start.2 = ((bf16[8,2,128,256]{3,2,1,0:T(8,128)(2,1)}), bf16[8,2,128,256]{3,2,1,0:T(8,128)(2,1)S(1)}, u32[]{:S(2)}, u32[]{:S(2)}) async-start(bf16[8,2,128,256]{3,2,1,0:T(8,128)(2,1)} %get-tuple-element.25), calls=%async_computation.2 | async-start | bytes 2097152 | tf_op jit(solution)/shard_map/all_to_all | solution.py:225
  184.0 28.5 %collective-permute-start.3 = (bf16[8,2,128,256]{3,2,1,0:T(8,128)(2,1)S(1)}, bf16[8,2,128,256]{3,2,1,0:T(8,128)(2,1)}, u32[]{:S(2)}, u32[]{:S(2)}) collective-permute-start(bf16[8,2,128,256]{3,2,1,0:T(8,128)(2,1)S(1)} %copy-done.13), channel_id=1, source_target_pairs={{8,0},{16,8},{24,16},{9,1},{17,9},{25,17},{10,2},{18,10},{26,18},{... | collective-permute-start | bytes 3145736 | tf_op jit(solution)/shard_map/ppermute | solution.py:242
  199.4 16.2 %copy-start.14 = (bf16[8,2,128,256]{3,2,1,0:T(8,128)(2,1)}, bf16[8,2,128,256]{3,2,1,0:T(8,128)(2,1)S(1)}, u32[]{:S(2)}) copy-start(bf16[8,2,128,256]{3,2,1,0:T(8,128)(2,1)S(1)} %all-to-all-done.2.refs_0_) | copy-start | bytes 3145732
  199.4 18.9 %all-to-all-start.10 = ((bf16[8,2,128,256]{3,2,1,0:T(8,128)(2,1)}), bf16[8,2,128,256]{3,2,1,0:T(8,128)(2,1)S(1)}, u32[]{:S(2)}, u32[]{:S(2)}) async-start(bf16[8,2,128,256]{3,2,1,0:T(8,128)(2,1)} %add_convert_fusion), calls=%async_computation.10 | async-start | bytes 2097152 | tf_op jit(solution)/shard_map/all_to_all | solution.py:225
  218.3 9.5 %copy-start.15 = (bf16[8,2,128,256]{3,2,1,0:T(8,128)(2,1)}, bf16[8,2,128,256]{3,2,1,0:T(8,128)(2,1)S(1)}, u32[]{:S(2)}) copy-start(bf16[8,2,128,256]{3,2,1,0:T(8,128)(2,1)S(1)} %all-to-all-done.10.refs_1_) | copy-start | bytes 3145732
  218.3 18.9 %all-to-all-start.9 = ((bf16[8,2,128,256]{3,2,1,0:T(8,128)(2,1)}), bf16[8,2,128,256]{3,2,1,0:T(8,128)(2,1)S(1)}, u32[]{:S(2)}, u32[]{:S(2)}) async-start(bf16[8,2,128,256]{3,2,1,0:T(8,128)(2,1)} %add_convert_fusion.1), calls=%async_computation.9 | async-start | bytes 2097152 | tf_op jit(solution)/shard_map/all_to_all | solution.py:225
  (11 other events, 17.8 us)

commit v3 on v2

--- a/solution.py
+++ b/solution.py
@@ -16,32 +16,36 @@
 TPS = 4
 K_NB = 10
 MASKED = -1e30
-CHUNKS = ((0, 2), (2, 2), (4, 1))
-VMEM_LIMIT = 48 * 1024 * 1024
-
-
-def pack(arrays, members, heads, chunks):
+CHUNKS = (2, 3)
+VMEM_LIMIT = 32 * 1024 * 1024
+
+
+def whole(count):
+    return [pl.BlockSpec(memory_space=pltpu.VMEM)] * count
+
+
+def pack(arrays, members, heads, groups):
     n = len(arrays)
     tokens = arrays[0].shape[0]
 
     def body(*refs):
         ins, outs = refs[:n], refs[n:]
-        for (first, count), out in zip(chunks, outs):
-            for a in range(n):
-                out[0, a] = ins[a][:, first * HEAD_DIM : (first + count) * HEAD_DIM]
+        for (first, count), out in zip(groups, outs):
+            for p in range(members):
+                for h in range(count):
+                    start = (p * heads + first + h) * HEAD_DIM
+                    for a in range(n):
+                        out[p, h * n + a] = ins[a][:, start : start + HEAD_DIM]
 
     return pl.pallas_call(
         body,
-        grid=(members,),
         out_shape=[
-            jax.ShapeDtypeStruct((members, n, tokens, count * HEAD_DIM), arrays[0].dtype)
-            for _, count in chunks
-        ],
-        in_specs=[pl.BlockSpec((tokens, heads * HEAD_DIM), lambda p: (0, p))] * n,
-        out_specs=[
-            pl.BlockSpec((1, n, tokens, count * HEAD_DIM), lambda p: (p, 0, 0, 0))
-            for _, count in chunks
-        ],
+            jax.ShapeDtypeStruct((members, n * count, tokens, HEAD_DIM), arrays[0].dtype)
+            for _, count in groups
+        ],
+        in_specs=whole(n),
+        out_specs=whole(len(groups)),
+        compiler_params=pltpu.CompilerParams(vmem_limit_bytes=VMEM_LIMIT),
         cost_estimate=pl.CostEstimate(
             flops=0, bytes_accessed=4 * n * arrays[0].size, transcendentals=0
         ),
@@ -49,25 +53,25 @@
     )(*arrays)
 
 
-def unpack(received, members, heads, chunks):
-    n, tokens = received[0].shape[1:3]
+def unpack(received, n, members, heads, groups):
+    tokens = received[0].shape[2]
 
     def body(*refs):
-        ins, outs = refs[: len(chunks)], refs[len(chunks) :]
-        for (first, count), source in zip(chunks, ins):
-            for a in range(n):
-                outs[a][:, first * HEAD_DIM : (first + count) * HEAD_DIM] = source[0, a]
+        ins, outs = refs[: len(groups)], refs[len(groups) :]
+        for (first, count), source in zip(groups, ins):
+            for p in range(members):
+                for h in range(count):
+                    start = (p * heads + first + h) * HEAD_DIM
+                    for a in range(n):
+                        outs[a][:, start : start + HEAD_DIM] = source[p, h * n + a]
 
     shape = (tokens, members * heads * HEAD_DIM)
     return pl.pallas_call(
         body,
-        grid=(members,),
         out_shape=[jax.ShapeDtypeStruct(shape, received[0].dtype)] * n,
-        in_specs=[
-            pl.BlockSpec((1, n, tokens, count * HEAD_DIM), lambda p: (p, 0, 0, 0))
-            for _, count in chunks
-        ],
-        out_specs=[pl.BlockSpec((tokens, heads * HEAD_DIM), lambda p: (0, p))] * n,
+        in_specs=whole(len(groups)),
+        out_specs=whole(n),
+        compiler_params=pltpu.CompilerParams(vmem_limit_bytes=VMEM_LIMIT),
         cost_estimate=pl.CostEstimate(
             flops=0, bytes_accessed=4 * n * math.prod(shape), transcendentals=0
         ),
@@ -130,18 +134,18 @@
     cur_ref[:, 1] = dv_all[plane:].reshape(kp_ref.shape)
 
 
-def attention(bias, classes, qc, kv, kv_prev):
-    parts, _, rows, width = qc.shape
+def attention(bias, classes, qc, kv, kv_prev, first):
+    parts, slots, rows, _ = qc.shape
     plane = parts * rows
-    heads = width // HEAD_DIM
+    heads = slots // 2
     products = heads * 2 * (plane // 2) * 3 * (plane // 2)
 
-    def one(array):
+    def one(slot):
         return pl.BlockSpec(
-            (parts, None, rows, HEAD_DIM), lambda h, array=array: (0, array, 0, h)
+            (parts, None, rows, HEAD_DIM), lambda h, slot=slot: (0, 2 * h + slot, 0, 0)
         )
 
-    both = pl.BlockSpec((parts, 2, rows, HEAD_DIM), lambda h: (0, 0, 0, h))
+    both = pl.BlockSpec((parts, 2, rows, HEAD_DIM), lambda h: (0, h, 0, 0))
     return pl.pallas_call(
         attention_body,
         grid=(heads,),
@@ -153,7 +157,7 @@
         in_specs=[
             pl.BlockSpec(bias.shape, lambda h: (0, 0, 0)),
             pl.BlockSpec(classes.shape, lambda h: (0, 0)),
-            one(0), one(1), one(0), one(1), one(0), one(1),
+            one(0), one(1), one(2 * first), one(2 * first + 1), one(0), one(1),
         ],
         out_specs=[both, both, both],
         scratch_shapes=[
@@ -221,29 +225,39 @@
     up = [(i, i + 1) for i in range(planes - 1)]
     down = [(i + 1, i) for i in range(planes - 1)]
 
+    last = []
+
     def exchange(array):
-        return lax.all_to_all(array, group, split_axis=0, concat_axis=0, tiled=True)
-
-    chunks = [(first, count) for first, count in CHUNKS if first + count <= heads]
-    if sum(count for _, count in chunks) != heads:
-        chunks = [(0, heads)]
-    kv_sent = pack((k, v), members, heads, chunks)
-    qc_sent = pack((q, c), members, heads, chunks)
-    received = []
-    for kv_part, qc_part in zip(kv_sent, qc_sent):
-        kv = exchange(kv_part)
-        received.append((exchange(qc_part), kv, lax.ppermute(kv, "plane", up)))
+        if last:
+            array, _ = lax.optimization_barrier((array, last[-1]))
+        last.append(lax.all_to_all(array, group, split_axis=0, concat_axis=0, tiled=True))
+        return last[-1]
+
+    counts = CHUNKS if sum(CHUNKS) == heads else (heads,)
+    groups = [(sum(counts[:i]), count) for i, count in enumerate(counts)]
+    kv_sent = pack((k, v), members, heads, [(0, heads)])[0]
+    kv = exchange(kv_sent)
+    kv_prev = []
+    for first, count in groups:
+        moved = kv[:, 2 * first : 2 * (first + count)]
+        if kv_prev:
+            moved, _ = lax.optimization_barrier((moved, kv_prev[-1]))
+        kv_prev.append(lax.ppermute(moved, "plane", up))
+    qc = [exchange(sent) for sent in pack((q, c), members, heads, groups)]
     bias, classes = mask_operands(
         frame_blocks, tile_lists, z, bands, queries.shape[1] * bands, queries.shape[2]
     )
-    odq_back, dkv_back = [], []
-    for qc, kv, kv_prev in received:
-        odq, dkv, dkv_prev = attention(bias, classes, qc, kv, kv_prev)
+    odq_back, dkv_back, waiting = [], [], None
+    for i, (first, count) in enumerate(groups):
+        odq, dkv, dkv_prev = attention(bias, classes, qc[i], kv, kv_prev[i], first)
         dkv_next = lax.ppermute(dkv_prev, "plane", down)
+        if waiting is not None:
+            dkv_back.append(exchange(waiting))
         odq_back.append(exchange(odq))
-        total = (dkv + dkv_next.astype(jnp.float32)).astype(jnp.bfloat16)
-        dkv_back.append(exchange(total))
-    outputs = unpack(odq_back, members, heads, chunks) + unpack(dkv_back, members, heads, chunks)
+        waiting = (dkv + dkv_next.astype(jnp.float32)).astype(jnp.bfloat16)
+    dkv_back.append(exchange(waiting))
+    outputs = unpack(odq_back, 2, members, heads, groups)
+    outputs += unpack(dkv_back, 2, members, heads, groups)
     return tuple(array.reshape(queries.shape) for array in outputs)
 
 

time: 246 us -> 229 us (0.931)
  waiting for transfers between devices: 81.4 us -> 112 us
  starting transfers between devices: 62.8 us -> 41.4 us
  Pallas kernels: 64.5 us -> 47.2 us
  blocking collectives: 13.9 us -> 0 us
  local copies, waits for them, and re-layouts: 10 us -> 17.4 us
    ppermute x3 -> x2, waiting for transfers between devices: 17.9 us -> 55.2 us  [on_device(): dkv_next = lax.ppermute(dkv_prev, 'plane', down)]
    pallas_call x4, Pallas kernels: 23.8 us -> 8.28 us  [the longest x2 7.38 us: unpack(): pl.pallas_call(body, out_shape=[jax.ShapeDtypeStruct(shape, received[0].d...]
    all_to_all x1 -> x0, blocking collectives: 13.9 us -> none  [exchange(): return lax.all_to_all(array, group, split_axis=0, concat_axis=0, tiled=True)]
    all_to_all x11 -> x7, starting transfers between devices: 44.4 us -> 30.7 us  [exchange(): lax.all_to_all(array, group, split_axis=0, concat_axis=0, tiled=True)]
    all_to_all x11 -> x7, waiting for transfers between devices: 63.5 us -> 57.2 us  [exchange(): lax.all_to_all(array, group, split_axis=0, concat_axis=0, tiled=True)]
    ppermute x3 -> x2, starting transfers between devices: 14.3 us -> 8.16 us  [on_device(): kv_prev.append(lax.ppermute(moved, 'plane', up))]
    unnamed x36 -> x26, local copies, waits for them, and re-layouts: 9.17 us -> 14 us
    slice x0 -> x2, local copies, waits for them, and re-layouts: none -> 2.5 us  [on_device(): moved = kv[:, 2 * first:2 * (first + count)]]
  transfers between devices with their start and end apart: 17 -> 11, of which waited for: 10 -> 5; matrix products, arithmetic and copies ran while one was open for 5% -> 5% of each run, Pallas kernels for 22% -> 19%
where the time goes in v3:
time: 229 us
  waiting for transfers between devices  112 us (49%)
  Pallas kernels  47.2 us (21%)
  starting transfers between devices  41.4 us (18%)
  local copies, waits for them, and re-layouts  17.4 us (8%)
  other arithmetic  9.25 us (4%)
    all_to_all x7, waiting for transfers between devices, exchange(): lax.all_to_all(array, group, split_axis=0, concat_axis=0, tiled=True)  57.2 us
    ppermute x2, waiting for transfers between devices, on_device(): dkv_next = lax.ppermute(dkv_prev, 'plane', down)  55.2 us
    pallas_call x2, Pallas kernels, attention(): pl.pallas_call(attention_body, grid=(heads,), out_shape=[jax.ShapeDtypeSt...  38.9 us
    all_to_all x7, starting transfers between devices, exchange(): lax.all_to_all(array, group, split_axis=0, concat_axis=0, tiled=True)  30.7 us
    unnamed x26, local copies, waits for them, and re-layouts  14 us
    ppermute x2, starting transfers between devices, on_device(): kv_prev.append(lax.ppermute(moved, 'plane', up))  8.16 us
    pallas_call x2, Pallas kernels, unpack(): pl.pallas_call(body, out_shape=[jax.ShapeDtypeStruct(shape, received[0].d...  7.38 us
    convert_element_type x2, other arithmetic, on_device(): waiting = (dkv + dkv_next.astype(jnp.float32)).astype(jnp.bfloat16)  7.29 us
  transfers between devices with their start and end apart: 11, of which 5 were waited for; matrix products, arithmetic and copies ran while one was open for 5% of the time, Pallas kernels for 19%

profile of v3, /device:TPU:0, one launch (start us, length us, event | category | flops | bytes accessed | tf_op | source)
XLA Modules:
  0.0 228.6 jit_solution(16289508200676692188)
XLA Ops:
  3.8 1.5 copy-done.1
  5.2 5.3 %all-to-all-start = ((bf16[8,10,128,128]{3,2,1,0:T(8,128)(2,1)}), bf16[8,10,128,128]{3,2,1,0:T(8,128)(2,1)S(1)}, u32[]{:S(2)}, u32[]{:S(2)}) async-start(bf16[8,10,128,128]{3,2,1,0:T(8,128)(2,1)} %copy-done.1), calls=%async_computation | async-start | bytes 5242880 | tf_op jit(solution)/shard_map/all_to_all | solution.py:233
  16.9 25.9 %all-to-all-done.kc_ref.vc_ref = bf16[8,10,128,128]{3,2,1,0:T(8,128)(2,1)S(1)} async-done(((bf16[8,10,128,128]{3,2,1,0:T(8,128)(2,1)}), bf16[8,10,128,128]{3,2,1,0:T(8,128)(2,1)S(1)}, u32[]{:S(2)}, u32[]{:S(2)}) %all-to-all-start) | async-done | bytes 2621472 | tf_op jit(solution)/shard_map/all_to_all | solution.py:233
  43.9 4.5 %collective-permute-start = (bf16[8,4,128,128]{3,2,1,0:T(8,128)(2,1)}, bf16[8,4,128,128]{3,2,1,0:T(8,128)(2,1)}, u32[]{:S(2)}, u32[]{:S(2)}) collective-permute-start(bf16[8,4,128,128]{3,2,1,0:T(8,128)(2,1)} %slice.20), channel_id=1, source_target_pairs={{0,8},{8,16},{16,24},{1,9},{9,17},{17,25},{2,10},{10,18},{18,26},{... | collective-permute-start | bytes 3145736 | tf_op jit(solution)/shard_map/ppermute | solution.py:245
  48.4 4.2 %all-to-all-start.1 = ((bf16[8,4,128,128]{3,2,1,0:T(8,128)(2,1)}), bf16[8,4,128,128]{3,2,1,0:T(8,128)(2,1)}, u32[]{:S(2)}, u32[]{:S(2)}) async-start(bf16[8,4,128,128]{3,2,1,0:T(8,128)(2,1)} %copy-done.10), calls=%async_computation.1 | async-start | bytes 2097152 | tf_op jit(solution)/shard_map/all_to_all | solution.py:233
  54.3 13.8 %all-to-all-done.1.q_ref.c_ref = bf16[8,4,128,128]{3,2,1,0:T(8,128)(2,1)} async-done(((bf16[8,4,128,128]{3,2,1,0:T(8,128)(2,1)}), bf16[8,4,128,128]{3,2,1,0:T(8,128)(2,1)}, u32[]{:S(2)}, u32[]{:S(2)}) %all-to-all-start.1) | async-done | bytes 1048608 | tf_op jit(solution)/shard_map/all_to_all | solution.py:233
  68.0 4.3 %all-to-all-start.2 = ((bf16[8,6,128,128]{3,2,1,0:T(8,128)(2,1)}), bf16[8,6,128,128]{3,2,1,0:T(8,128)(2,1)}, u32[]{:S(2)}, u32[]{:S(2)}) async-start(bf16[8,6,128,128]{3,2,1,0:T(8,128)(2,1)} %copy-done.4), calls=%async_computation.2 | async-start | bytes 3145728 | tf_op jit(solution)/shard_map/all_to_all | solution.py:233
  72.4 1.4 slice.21
  73.8 3.7 %collective-permute-start.1 = (bf16[8,6,128,128]{3,2,1,0:T(8,128)(2,1)}, bf16[8,6,128,128]{3,2,1,0:T(8,128)(2,1)}, u32[]{:S(2)}, u32[]{:S(2)}) collective-permute-start(bf16[8,6,128,128]{3,2,1,0:T(8,128)(2,1)} %slice.21), channel_id=1, source_target_pairs={{0,8},{8,16},{16,24},{1,9},{9,17},{17,25},{2,10},{10,18},{18,26},{... | collective-permute-start | bytes 4718600 | tf_op jit(solution)/shard_map/ppermute | solution.py:245
  77.6 15.9 %attention.2 = (bf16[8,4,128,128]{3,2,1,0:T(8,128)(2,1)S(1)}, f32[8,4,128,128]{3,2,1,0:T(8,128)S(1)}, bf16[8,4,128,128]{3,2,1,0:T(8,128)(2,1)}) custom-call(bf16[2,1536,128]{2,1,0:T(8,128)(2,1)S(1)} %bitcast.22, bf16[512,128]{1,0:T(8,128)(2,1)S(1)} %fusion.16.class_ref, bf16[8,4,128,128]{3,2,1,0:T(8,128)(2,1)} %all-to-all-done.1.q_ref.c_ref, ...), custom_call_target="tpu_custom_call" | custom-call | flops 9663676416 | bytes 9437184 | tf_op jit(solution)/shard_map/attention/pallas_call | solution.py:149
  93.5 1.4 copy-done.3
  97.2 4.3 %all-to-all-start.3 = ((bf16[8,4,128,128]{3,2,1,0:T(8,128)(2,1)}), bf16[8,4,128,128]{3,2,1,0:T(8,128)(2,1)}, u32[]{:S(2)}, u32[]{:S(2)}) async-start(bf16[8,4,128,128]{3,2,1,0:T(8,128)(2,1)} %copy-done.11), calls=%async_computation.3 | async-start | bytes 2097152 | tf_op jit(solution)/shard_map/all_to_all | solution.py:233
  101.4 21.7 %collective-permute-done.2 = bf16[8,4,128,128]{3,2,1,0:T(8,128)(2,1)} collective-permute-done((bf16[8,4,128,128]{3,2,1,0:T(8,128)(2,1)}, bf16[8,4,128,128]{3,2,1,0:T(8,128)(2,1)}, u32[]{:S(2)}, u32[]{:S(2)}) %collective-permute-start.2) | collective-permute-done | bytes 1048608 | tf_op jit(solution)/shard_map/ppermute | solution.py:253
  123.2 3.2 %add_convert_fusion.1 = bf16[8,4,128,128]{3,2,1,0:T(8,128)(2,1)} fusion(f32[8,4,128,128]{3,2,1,0:T(8,128)} %copy-done.3, bf16[8,4,128,128]{3,2,1,0:T(8,128)(2,1)} %collective-permute-done.2), kind=kLoop, calls=%fused_computation.1 | loop fusion | flops 1572864 | bytes 4194304 | tf_op jit(solution)/shard_map/convert_element_type | solution.py:257
  126.3 4.4 %all-to-all-start.4 = ((bf16[8,4,128,128]{3,2,1,0:T(8,128)(2,1)}), bf16[8,4,128,128]{3,2,1,0:T(8,128)(2,1)}, u32[]{:S(2)}, u32[]{:S(2)}) async-start(bf16[8,4,128,128]{3,2,1,0:T(8,128)(2,1)} %add_convert_fusion.1), calls=%async_computation.4 | async-start | bytes 2097152 | tf_op jit(solution)/shard_map/all_to_all | solution.py:233
  130.8 23.0 %attention.3 = (bf16[8,6,128,128]{3,2,1,0:T(8,128)(2,1)S(1)}, f32[8,6,128,128]{3,2,1,0:T(8,128)S(1)}, bf16[8,6,128,128]{3,2,1,0:T(8,128)(2,1)}) custom-call(bf16[2,1536,128]{2,1,0:T(8,128)(2,1)S(1)} %bitcast.23, bf16[512,128]{1,0:T(8,128)(2,1)S(1)} %fusion.16.class_ref, bf16[8,6,128,128]{3,2,1,0:T(8,128)(2,1)} %all-to-all-done.2.q_ref.c_ref, ...), custom_call_target="tpu_custom_call" | custom-call | flops 14495514624 | bytes 14155776 | tf_op jit(solution)/shard_map/attention/pallas_call | solution.py:149
  153.8 1.6 copy-done.2
  157.8 3.9 %all-to-all-start.5 = ((bf16[8,6,128,128]{3,2,1,0:T(8,128)(2,1)}), bf16[8,6,128,128]{3,2,1,0:T(8,128)(2,1)S(1)}, u32[]{:S(2)}, u32[]{:S(2)}) async-start(bf16[8,6,128,128]{3,2,1,0:T(8,128)(2,1)} %copy-done.5), calls=%async_computation.5 | async-start | bytes 3145728 | tf_op jit(solution)/shard_map/all_to_all | solution.py:233
  161.7 33.5 %collective-permute-done.3 = bf16[8,6,128,128]{3,2,1,0:T(8,128)(2,1)} collective-permute-done((bf16[8,6,128,128]{3,2,1,0:T(8,128)(2,1)}, bf16[8,6,128,128]{3,2,1,0:T(8,128)(2,1)}, u32[]{:S(2)}, u32[]{:S(2)}) %collective-permute-start.3) | collective-permute-done | bytes 1572896 | tf_op jit(solution)/shard_map/ppermute | solution.py:253
  195.2 4.1 %add_convert_fusion = bf16[8,6,128,128]{3,2,1,0:T(8,128)(2,1)} fusion(f32[8,6,128,128]{3,2,1,0:T(8,128)} %copy-done.2, bf16[8,6,128,128]{3,2,1,0:T(8,128)(2,1)} %collective-permute-done.3), kind=kLoop, calls=%fused_computation | loop fusion | flops 2359296 | bytes 6291456 | tf_op jit(solution)/shard_map/convert_element_type | solution.py:257
  199.3 4.3 %all-to-all-start.6 = ((bf16[8,6,128,128]{3,2,1,0:T(8,128)(2,1)}), bf16[8,6,128,128]{3,2,1,0:T(8,128)(2,1)}, u32[]{:S(2)}, u32[]{:S(2)}) async-start(bf16[8,6,128,128]{3,2,1,0:T(8,128)(2,1)} %add_convert_fusion), calls=%async_computation.6 | async-start | bytes 3145728 | tf_op jit(solution)/shard_map/all_to_all | solution.py:233
  203.6 3.4 %unpack.2 = (bf16[128,5120]{1,0:T(8,128)(2,1)}, bf16[128,5120]{1,0:T(8,128)(2,1)}) custom-call(bf16[8,4,128,128]{3,2,1,0:T(8,128)(2,1)} %all-to-all-done.3.refs_0_, bf16[8,6,128,128]{3,2,1,0:T(8,128)(2,1)S(1)} %all-to-all-done.5.refs_1_), custom_call_target="tpu_custom_call" | custom-call | bytes 5242880 | tf_op jit(solution)/shard_map/unpack/pallas_call | solution.py:69
  207.1 17.6 %all-to-all-done.6.refs_1_ = bf16[8,6,128,128]{3,2,1,0:T(8,128)(2,1)} async-done(((bf16[8,6,128,128]{3,2,1,0:T(8,128)(2,1)}), bf16[8,6,128,128]{3,2,1,0:T(8,128)(2,1)}, u32[]{:S(2)}, u32[]{:S(2)}) %all-to-all-start.6) | async-done | bytes 1572896 | tf_op jit(solution)/shard_map/all_to_all | solution.py:233
  224.7 3.9 %unpack.3 = (bf16[128,5120]{1,0:T(8,128)(2,1)}, bf16[128,5120]{1,0:T(8,128)(2,1)}) custom-call(bf16[8,4,128,128]{3,2,1,0:T(8,128)(2,1)} %all-to-all-done.4.refs_0_, bf16[8,6,128,128]{3,2,1,0:T(8,128)(2,1)} %all-to-all-done.6.refs_1_), custom_call_target="tpu_custom_call" | custom-call | bytes 5242880 | tf_op jit(solution)/shard_map/unpack/pallas_call | solution.py:69
  (66 shorter events, 16.9 us)
Async XLA Ops:
  0.6 15.5 %copy-start = (s32[8,2,2,10]{3,2,1,0:T(2,128)S(1)}, s32[8,2,2,10]{3,2,1,0:T(2,128)}, u32[]{:S(2)}) copy-start(s32[8,2,2,10]{3,2,1,0:T(2,128)} %param.11) | copy-start | bytes 3844
  0.6 1.3 copy-start.6
  2.0 1.3 copy-start.7
  3.7 1.5 copy-start.1
  5.2 5.3 %copy-start.12 = (s32[16]{0:T(128)S(1)}, s32[16]{0:T(128)}, u32[]{:S(2)}) copy-start(s32[16]{0:T(128)} %param.10) | copy-start | bytes 196
  5.2 37.6 %all-to-all-start = ((bf16[8,10,128,128]{3,2,1,0:T(8,128)(2,1)}), bf16[8,10,128,128]{3,2,1,0:T(8,128)(2,1)S(1)}, u32[]{:S(2)}, u32[]{:S(2)}) async-start(bf16[8,10,128,128]{3,2,1,0:T(8,128)(2,1)} %copy-done.1), calls=%async_computation | async-start | bytes 5242880 | tf_op jit(solution)/shard_map/all_to_all | solution.py:233
  10.9 1.3 copy-start.8
  12.2 1.3 copy-start.9
  13.9 1.2 copy-start.4
  15.1 1.0 copy-start.10
  43.9 29.9 %collective-permute-start = (bf16[8,4,128,128]{3,2,1,0:T(8,128)(2,1)}, bf16[8,4,128,128]{3,2,1,0:T(8,128)(2,1)}, u32[]{:S(2)}, u32[]{:S(2)}) collective-permute-start(bf16[8,4,128,128]{3,2,1,0:T(8,128)(2,1)} %slice.20), channel_id=1, source_target_pairs={{0,8},{8,16},{16,24},{1,9},{9,17},{17,25},{2,10},{10,18},{18,26},{... | collective-permute-start | bytes 3145736 | tf_op jit(solution)/shard_map/ppermute | solution.py:245
  48.4 19.7 %all-to-all-start.1 = ((bf16[8,4,128,128]{3,2,1,0:T(8,128)(2,1)}), bf16[8,4,128,128]{3,2,1,0:T(8,128)(2,1)}, u32[]{:S(2)}, u32[]{:S(2)}) async-start(bf16[8,4,128,128]{3,2,1,0:T(8,128)(2,1)} %copy-done.10), calls=%async_computation.1 | async-start | bytes 2097152 | tf_op jit(solution)/shard_map/all_to_all | solution.py:233
  68.0 29.1 %all-to-all-start.2 = ((bf16[8,6,128,128]{3,2,1,0:T(8,128)(2,1)}), bf16[8,6,128,128]{3,2,1,0:T(8,128)(2,1)}, u32[]{:S(2)}, u32[]{:S(2)}) async-start(bf16[8,6,128,128]{3,2,1,0:T(8,128)(2,1)} %copy-done.4), calls=%async_computation.2 | async-start | bytes 3145728 | tf_op jit(solution)/shard_map/all_to_all | solution.py:233
  73.8 57.0 %collective-permute-start.1 = (bf16[8,6,128,128]{3,2,1,0:T(8,128)(2,1)}, bf16[8,6,128,128]{3,2,1,0:T(8,128)(2,1)}, u32[]{:S(2)}, u32[]{:S(2)}) collective-permute-start(bf16[8,6,128,128]{3,2,1,0:T(8,128)(2,1)} %slice.21), channel_id=1, source_target_pairs={{0,8},{8,16},{16,24},{1,9},{9,17},{17,25},{2,10},{10,18},{18,26},{... | collective-permute-start | bytes 4718600 | tf_op jit(solution)/shard_map/ppermute | solution.py:245
  93.5 1.4 copy-start.3
  94.9 1.0 copy-start.11
  95.9 27.3 %collective-permute-start.2 = (bf16[8,4,128,128]{3,2,1,0:T(8,128)(2,1)}, bf16[8,4,128,128]{3,2,1,0:T(8,128)(2,1)}, u32[]{:S(2)}, u32[]{:S(2)}) collective-permute-start(bf16[8,4,128,128]{3,2,1,0:T(8,128)(2,1)} %get-tuple-element.32), channel_id=1, source_target_pairs={{8,0},{16,8},{24,16},{9,1},{17,9},{25,17},{10,2},{18,10},{26,18},{... | collective-permute-start | bytes 3145736 | tf_op jit(solution)/shard_map/ppermute | solution.py:253
  97.2 29.2 %all-to-all-start.3 = ((bf16[8,4,128,128]{3,2,1,0:T(8,128)(2,1)}), bf16[8,4,128,128]{3,2,1,0:T(8,128)(2,1)}, u32[]{:S(2)}, u32[]{:S(2)}) async-start(bf16[8,4,128,128]{3,2,1,0:T(8,128)(2,1)} %copy-done.11), calls=%async_computation.3 | async-start | bytes 2097152 | tf_op jit(solution)/shard_map/all_to_all | solution.py:233
  126.3 31.5 %all-to-all-start.4 = ((bf16[8,4,128,128]{3,2,1,0:T(8,128)(2,1)}), bf16[8,4,128,128]{3,2,1,0:T(8,128)(2,1)}, u32[]{:S(2)}, u32[]{:S(2)}) async-start(bf16[8,4,128,128]{3,2,1,0:T(8,128)(2,1)} %add_convert_fusion.1), calls=%async_computation.4 | async-start | bytes 2097152 | tf_op jit(solution)/shard_map/all_to_all | solution.py:233
  153.8 1.6 copy-start.2
  155.4 1.1 copy-start.5
  156.5 38.7 %collective-permute-start.3 = (bf16[8,6,128,128]{3,2,1,0:T(8,128)(2,1)}, bf16[8,6,128,128]{3,2,1,0:T(8,128)(2,1)}, u32[]{:S(2)}, u32[]{:S(2)}) collective-permute-start(bf16[8,6,128,128]{3,2,1,0:T(8,128)(2,1)} %get-tuple-element.38), channel_id=1, source_target_pairs={{8,0},{16,8},{24,16},{9,1},{17,9},{25,17},{10,2},{18,10},{26,18},{... | collective-permute-start | bytes 4718600 | tf_op jit(solution)/shard_map/ppermute | solution.py:253
  157.8 41.5 %all-to-all-start.5 = ((bf16[8,6,128,128]{3,2,1,0:T(8,128)(2,1)}), bf16[8,6,128,128]{3,2,1,0:T(8,128)(2,1)S(1)}, u32[]{:S(2)}, u32[]{:S(2)}) async-start(bf16[8,6,128,128]{3,2,1,0:T(8,128)(2,1)} %copy-done.5), calls=%async_computation.5 | async-start | bytes 3145728 | tf_op jit(solution)/shard_map/all_to_all | solution.py:233
  199.3 25.3 %all-to-all-start.6 = ((bf16[8,6,128,128]{3,2,1,0:T(8,128)(2,1)}), bf16[8,6,128,128]{3,2,1,0:T(8,128)(2,1)}, u32[]{:S(2)}, u32[]{:S(2)}) async-start(bf16[8,6,128,128]{3,2,1,0:T(8,128)(2,1)} %add_convert_fusion), calls=%async_computation.6 | async-start | bytes 3145728 | tf_op jit(solution)/shard_map/all_to_all | solution.py:233

commit v4 on v3

v4 whole, which is shorter than its diff:
```python
import functools
import math

import jax
import jax.numpy as jnp
from jax import lax
from jax.experimental import pallas as pl
from jax.experimental.pallas import tpu as pltpu
from jax.sharding import Mesh, PartitionSpec as P

HEAD_DIM = 128
TT = 2
TH = 8
TW = 8
NTW = 2
TPS = 4
K_NB = 10
MASKED = -1e30
CHUNKS = (2, 2, 1)
INWARD = ((("kv", 0),), (("kv", 1), ("qc", 0)), (("qc", 1), ("qc", 2), ("kv", 2)))
OUTWARD = ((("o", 0),), (("o", 1),), (("o", 2), ("d", 0)), (("d", 1), ("d", 2)))
VMEM_LIMIT = 32 * 1024 * 1024


STEPS = 2


def hbm(shape, dtype):
    return pltpu.HBM(shape, dtype)


def pack(pairs, members, heads, layouts):
    names = sorted({name for layout in layouts for name, _ in layout})
    arrays = [array for name in names for array in pairs[name]]
    tokens, width = arrays[0].shape
    here = members // STEPS

    def body(*refs):
        ins, outs = refs[: len(arrays)], refs[len(arrays) :]
        for layout, out in zip(layouts, outs):
            for p in range(here):
                for slot, (name, head) in enumerate(layout):
                    start = (p * heads + head) * HEAD_DIM
                    for a in range(2):
                        source = ins[2 * names.index(name) + a]
                        out[p, 2 * slot + a] = source[:, start : start + HEAD_DIM]

    shapes = [(2 * len(layout), tokens, HEAD_DIM) for layout in layouts]
    return pl.pallas_call(
        body,
        grid=(STEPS,),
        out_shape=[hbm((members, *shape), arrays[0].dtype) for shape in shapes],
        in_specs=[pl.BlockSpec((tokens, width // STEPS), lambda i: (0, i))] * len(arrays),
        out_specs=[pl.BlockSpec((here, *shape), lambda i: (i, 0, 0, 0)) for shape in shapes],
        compiler_params=pltpu.CompilerParams(vmem_limit_bytes=VMEM_LIMIT),
        cost_estimate=pl.CostEstimate(
            flops=0, bytes_accessed=4 * sum(array.size for array in arrays), transcendentals=0
        ),
        name="pack",
    )(*arrays)


def unpack(buffers, places, members, heads):
    tokens = buffers[0].shape[2]
    here = members // STEPS

    def body(*refs):
        ins, outs = refs[: len(buffers)], refs[len(buffers) :]
        for p in range(here):
            for head, (buffer, slot) in enumerate(places):
                start = (p * heads + head) * HEAD_DIM
                for a in range(2):
                    outs[a][:, start : start + HEAD_DIM] = ins[buffer][p, slot + a]

    width = members * heads * HEAD_DIM
    return pl.pallas_call(
        body,
        grid=(STEPS,),
        out_shape=[jax.ShapeDtypeStruct((tokens, width), buffers[0].dtype)] * 2,
        in_specs=[
            pl.BlockSpec((here, *buffer.shape[1:]), lambda i: (i, 0, 0, 0)) for buffer in buffers
        ],
        out_specs=[pl.BlockSpec((tokens, width // STEPS), lambda i: (0, i))] * 2,
        compiler_params=pltpu.CompilerParams(vmem_limit_bytes=VMEM_LIMIT),
        cost_estimate=pl.CostEstimate(
            flops=0, bytes_accessed=8 * tokens * width, transcendentals=0
        ),
        name="unpack",
    )(*buffers)


def attention_body(
    bias_ref, class_ref, q_ref, c_ref, kc_ref, vc_ref, kp_ref, vp_ref,
    odq_ref, cur_ref, prev_ref, k_all, v_all, kt_all, vt_all, dk_all, dv_all,
):
    parts, rows = q_ref.shape[0], q_ref.shape[1]
    plane = parts * rows
    slab = plane // 2
    scale = HEAD_DIM ** -0.5
    scale2 = scale * math.log2(math.e)
    half = parts // 2
    quarter = half // 2
    block = quarter * rows
    k_all[:plane] = kp_ref[...].reshape(plane, HEAD_DIM)
    k_all[plane:] = kc_ref[...].reshape(plane, HEAD_DIM)
    v_all[:plane] = vp_ref[...].reshape(plane, HEAD_DIM)
    v_all[plane:] = vc_ref[...].reshape(plane, HEAD_DIM)
    kt_all[...] = k_all[...].T
    vt_all[...] = v_all[...].T
    nt = (((1,), (1,)), ((), ()))
    for y in range(2):
        window = slice(y * slab, (y + 3) * slab)
        for piece in range(2):
            here = pl.ds(y * half + piece * quarter, quarter)
            q = q_ref[here].reshape(block, HEAD_DIM)
            c = c_ref[here].reshape(block, HEAD_DIM)
            classes = class_ref[piece * block : (piece + 1) * block]
            s = lax.dot_general(
                jnp.concatenate([k_all[window], bias_ref[y]], axis=1),
                jnp.concatenate([q, classes], axis=1),
                nt,
                preferred_element_type=jnp.float32,
            )
            m = jnp.max(s, axis=0, keepdims=True)
            e = jnp.exp2((s - m) * scale2)
            p = e * (1.0 / jnp.sum(e, axis=0, keepdims=True))
            w = p.astype(jnp.bfloat16)
            o = jnp.dot(vt_all[:, window], w, preferred_element_type=jnp.float32)
            o = o.astype(jnp.bfloat16).astype(jnp.float32)
            delta = jnp.sum(c.astype(jnp.float32).T * o, axis=0, keepdims=True)
            dp = lax.dot_general(v_all[window], c, nt, preferred_element_type=jnp.float32)
            ds = (p * (dp - delta)).astype(jnp.bfloat16)
            dq = jnp.dot(kt_all[:, window], ds, preferred_element_type=jnp.float32) * scale
            odq_ref[here, 0] = o.T.astype(jnp.bfloat16).reshape(quarter, rows, HEAD_DIM)
            odq_ref[here, 1] = dq.T.astype(jnp.bfloat16).reshape(quarter, rows, HEAD_DIM)
            dk = jnp.dot(ds, q, preferred_element_type=jnp.float32)
            dv = jnp.dot(w, c, preferred_element_type=jnp.float32)
            if y == 0 and piece == 0:
                dk_all[window] = dk
                dv_all[window] = dv
            elif y == 1 and piece == 0:
                dk_all[slab : 3 * slab] += dk[: 2 * slab]
                dv_all[slab : 3 * slab] += dv[: 2 * slab]
                dk_all[3 * slab :] = dk[2 * slab :]
                dv_all[3 * slab :] = dv[2 * slab :]
            else:
                dk_all[window] += dk
                dv_all[window] += dv
    prev_ref[:, 0] = (dk_all[:plane] * scale).astype(jnp.bfloat16).reshape(kp_ref.shape)
    prev_ref[:, 1] = dv_all[:plane].astype(jnp.bfloat16).reshape(kp_ref.shape)
    cur_ref[:, 0] = (dk_all[plane:] * scale).reshape(kp_ref.shape)
    cur_ref[:, 1] = dv_all[plane:].reshape(kp_ref.shape)


def attention(bias, classes, count, qc, kv, kv_prev):
    parts, _, rows, _ = qc[0].shape
    plane = parts * rows
    products = count * 2 * (plane // 2) * 3 * (plane // 2)

    def one(place, a):
        return pl.BlockSpec(
            (parts, None, rows, HEAD_DIM), lambda h: (0, place[1] + 2 * h + a, 0, 0)
        )

    shape = (parts, 2 * count, rows, HEAD_DIM)
    both = pl.BlockSpec((parts, 2, rows, HEAD_DIM), lambda h: (0, h, 0, 0))
    operands = [(place, a) for place in (qc, kv, kv_prev) for a in range(2)]
    return pl.pallas_call(
        attention_body,
        grid=(count,),
        out_shape=[
            hbm(shape, jnp.bfloat16),
            jax.ShapeDtypeStruct(shape, jnp.float32),
            hbm(shape, jnp.bfloat16),
        ],
        in_specs=[
            pl.BlockSpec(bias.shape, lambda h: (0, 0, 0)),
            pl.BlockSpec(classes.shape, lambda h: (0, 0)),
        ] + [one(place, a) for place, a in operands],
        out_specs=[both, both, both],
        scratch_shapes=[
            pltpu.VMEM((2 * plane, HEAD_DIM), jnp.bfloat16),
            pltpu.VMEM((2 * plane, HEAD_DIM), jnp.bfloat16),
            pltpu.VMEM((HEAD_DIM, 2 * plane), jnp.bfloat16),
            pltpu.VMEM((HEAD_DIM, 2 * plane), jnp.bfloat16),
            pltpu.VMEM((2 * plane, HEAD_DIM), jnp.float32),
            pltpu.VMEM((2 * plane, HEAD_DIM), jnp.float32),
        ],
        compiler_params=pltpu.CompilerParams(vmem_limit_bytes=VMEM_LIMIT),
        cost_estimate=pl.CostEstimate(
            flops=24 * products * HEAD_DIM,
            bytes_accessed=18 * math.prod(shape),
            transcendentals=products,
        ),
        name="attention",
    )(bias, classes, *[place[0] for place, _ in operands])


def mask_operands(frame_blocks, tile_lists, z, bands, frame_rows, frame_cols):
    blocks = frame_blocks.reshape(-1, TT)
    padded = jnp.concatenate([jnp.zeros((2, TT), jnp.int32), blocks])
    tile_rows = frame_rows // TH
    lists = lax.dynamic_slice_in_dim(tile_lists, 2 * z, 2).reshape(2, TPS, K_NB)
    near = lax.dynamic_slice_in_dim(padded, 2 * z, 4)
    key_blocks = jnp.stack([near[0:3], near[1:4]])
    query_blocks = near[2:4]
    distance = 2 - jnp.arange(3, dtype=jnp.int32)
    ids = distance[:, None] * TPS + jnp.arange(TPS, dtype=jnp.int32)[None, :]
    listed = jnp.any(lists[:, :, None, None, :] == ids[None, None, :, :, None], axis=-1)
    present = (2 * z + jnp.arange(2, dtype=jnp.int32))[:, None] >= distance[None, :]
    causal = key_blocks[:, :, :, None] <= query_blocks[:, None, None, :]
    allowed = (
        listed.transpose(0, 2, 3, 1)[:, :, :, None, :, None]
        & present[:, :, None, None, None, None]
        & causal[:, :, None, :, None, :]
    )
    table = jnp.where(allowed, 0.0, MASKED).astype(jnp.bfloat16)
    table = table.reshape(2, 3, tile_rows, NTW, TT, TPS * TT)
    table = table.transpose(0, 1, 2, 4, 3, 5)
    table = jnp.pad(table, [(0, 0)] * 5 + [(0, HEAD_DIM - TPS * TT)])
    per_band = frame_rows // bands
    bias = jnp.broadcast_to(
        table[:, :, :, None, :, None, :, None, :],
        (2, 3, tile_rows, bands // tile_rows, TT, per_band, NTW, TW, HEAD_DIM),
    ).reshape(2, -1, HEAD_DIM)
    row = lax.broadcasted_iota(jnp.int32, (bands * TT * per_band * frame_cols, HEAD_DIM), 0)
    lane = lax.broadcasted_iota(jnp.int32, row.shape, 1)
    per_frame = per_band * frame_cols
    band = row // (TT * per_frame)
    frame = row // per_frame % TT
    tile = band // (bands // tile_rows) * NTW + row % frame_cols // TW
    classes = (lane == tile * TT + frame).astype(jnp.bfloat16)
    return bias, classes


def on_device(planes, bands, queries, key_states, value_states, cotangent, frame_blocks, tile_lists):
    members = 2 * bands
    width = queries.shape[-1]
    heads = width // HEAD_DIM // members
    z = lax.axis_index("plane")
    group = ("half", "band")
    q, k, v, c = (
        array.reshape(-1, width) for array in (queries, key_states, value_states, cotangent)
    )
    up = [(i, i + 1) for i in range(planes - 1)]
    down = [(i + 1, i) for i in range(planes - 1)]

    if sum(CHUNKS) == heads:
        counts, inward, outward = CHUNKS, INWARD, OUTWARD
    else:
        counts = (heads,)
        inward, outward = ((("kv", 0),), (("qc", 0),)), ((("o", 0),), (("d", 0),))
    firsts = [sum(counts[:i]) for i in range(len(counts))]
    last = []

    def after(array, other):
        return lax.optimization_barrier((array, other))[0]

    def exchange(array):
        if last:
            array = after(array, last[-1])
        last.append(lax.all_to_all(array, group, split_axis=0, concat_axis=0, tiled=True))
        return last[-1]

    def layout(items):
        return [(name, firsts[i] + h) for name, i in items for h in range(counts[i])]

    pairs = {"kv": (k, v), "qc": (q, c)}
    sent = pack(pairs, members, heads, [layout(inward[0])])
    sent += pack(pairs, members, heads, [layout(items) for items in inward[1:]])
    place, shifted = {}, []
    for items, buffer in zip(inward, sent):
        buffer = exchange(buffer)
        slot = 0
        for name, i in items:
            place[name, i] = (buffer, slot)
            if name == "kv":
                moved = buffer[:, slot : slot + 2 * counts[i]]
                if shifted:
                    moved = after(moved, shifted[-1])
                shifted.append(lax.ppermute(moved, "plane", up))
            slot += 2 * counts[i]
    bias, classes = mask_operands(
        frame_blocks, tile_lists, z, bands, queries.shape[1] * bands, queries.shape[2]
    )
    made, owed = {}, []
    for i, count in enumerate(counts):
        odq, dkv, dkv_prev = attention(
            bias, classes, count, place["qc", i], place["kv", i], (shifted[i], 0)
        )
        made["o", i] = odq
        owed.append((dkv, lax.ppermute(dkv_prev, "plane", down)))
    for i, (dkv, dkv_next) in enumerate(owed):
        if i + 1 < len(owed):
            dkv_next = after(dkv_next, owed[-1][0])
        made["d", i] = (dkv + dkv_next.astype(jnp.float32)).astype(jnp.bfloat16)
    back, found = [], {}
    for items in outward:
        parts = [made[item] for item in items]
        back.append(exchange(jnp.concatenate(parts, axis=1) if len(parts) > 1 else parts[0]))
        for slot, (name, head) in enumerate(layout(items)):
            found[name, head] = (len(back) - 1, 2 * slot)
    outputs = []
    for name in ("o", "d"):
        used = sorted({found[name, head][0] for head in range(heads)})
        places = [(used.index(found[name, h][0]), found[name, h][1]) for h in range(heads)]
        outputs += unpack([back[i] for i in used], places, members, heads)
    return tuple(array.reshape(queries.shape) for array in outputs)


def solution(mesh):
    slabs, bands = mesh.shape["tm"], mesh.shape["band"]
    planes = slabs // 2
    split = Mesh(mesh.devices.reshape(planes, 2, bands), ("plane", "half", "band"))
    rows = P(("plane", "half"), "band", None, None)
    return jax.shard_map(
        functools.partial(on_device, planes, bands),
        mesh=split,
        in_specs=(rows, rows, rows, rows, P(), P()),
        out_specs=(rows, rows, rows, rows),
        check_vma=False,
    )
```

time: 229 us -> 197 us (0.86)
  waiting for transfers between devices: 112 us -> 65.7 us
  Pallas kernels: 47.2 us -> 56.5 us
  starting transfers between devices: 41.4 us -> 47 us
    ppermute x4 -> x6, waiting for transfers between devices: 55.2 us -> 15.7 us  [the longest x3 15.7 us: on_device(): owed.append((dkv, lax.ppermute(dkv_prev, 'plane', down)))]
    pallas_call x6 -> x7, Pallas kernels: 47.2 us -> 56.5 us  [the longest x3 49.1 us: attention(): pl.pallas_call(attention_body, grid=(count,), out_shape=[hbm(shape, jnp.b...]
    ppermute x4 -> x6, starting transfers between devices: 10.7 us -> 18.3 us  [the longest x3 14.2 us: on_device(): shifted.append(lax.ppermute(moved, 'plane', up))]
    all_to_all x7, waiting for transfers between devices: 57.2 us -> 49.9 us  [exchange(): lax.all_to_all(array, group, split_axis=0, concat_axis=0, tiled=True)]
    convert_element_type x2 -> x3, other arithmetic: 7.29 us -> 3.59 us  [on_device(): made['d', i] = (dkv + dkv_next.astype(jnp.float32)).astype(jnp.bfloat16)]
    concatenate x0 -> x2, other arithmetic: none -> 2.6 us  [on_device(): jnp.concatenate(parts, axis=1)]
    unnamed x26 -> x46, local copies, waits for them, and re-layouts: 14 us -> 13.5 us
  transfers between devices with their start and end apart: 11 -> 13, of which waited for: 5 -> 6; matrix products, arithmetic and copies ran while one was open for 5% -> 6% of each run, Pallas kernels for 19% -> 27%
where the time goes in v4:
time: 197 us; the launch traced here: 196 us
  waiting for transfers between devices  65.7 us (33%)
  Pallas kernels  56.5 us (29%)
  starting transfers between devices  47 us (24%)
  local copies, waits for them, and re-layouts  17.3 us (9%)
  other arithmetic  8.12 us (4%)
    all_to_all x7, waiting for transfers between devices, exchange(): lax.all_to_all(array, group, split_axis=0, concat_axis=0, tiled=True)  49.9 us
    pallas_call x3, Pallas kernels, attention(): pl.pallas_call(attention_body, grid=(count,), out_shape=[hbm(shape, jnp.b...  49.1 us
    all_to_all x7, starting transfers between devices, exchange(): lax.all_to_all(array, group, split_axis=0, concat_axis=0, tiled=True)  28.7 us
    ppermute x3, waiting for transfers between devices, on_device(): owed.append((dkv, lax.ppermute(dkv_prev, 'plane', down)))  15.7 us
    ppermute x3, starting transfers between devices, on_device(): shifted.append(lax.ppermute(moved, 'plane', up))  14.2 us
    unnamed x46, local copies, waits for them, and re-layouts  13.5 us
    ppermute x3, starting transfers between devices, on_device(): owed.append((dkv, lax.ppermute(dkv_prev, 'plane', down)))  4.12 us
  transfers between devices with their start and end apart: 13, of which 6 were waited for; matrix products, arithmetic and copies ran while one was open for 6% of the time, Pallas kernels for 27%

profile of v4, /device:TPU:0, one launch (start us, length us, event | category | flops | bytes accessed | tf_op | source)
XLA Modules:
  0.0 195.7 jit_solution(15714762869190054160)
XLA Ops:
  4.5 5.3 %all-to-all-start = ((bf16[8,4,128,128]{3,2,1,0:T(8,128)(2,1)}), bf16[8,4,128,128]{3,2,1,0:T(8,128)(2,1)}, u32[]{:S(2)}, u32[]{:S(2)}) async-start(bf16[8,4,128,128]{3,2,1,0:T(8,128)(2,1)} %pack.3), calls=%async_computation | async-start | bytes 2097152 | tf_op jit(solution)/shard_map/all_to_all | solution.py:262
  12.6 2.7 %pack.2 = (bf16[8,8,128,128]{3,2,1,0:T(8,128)(2,1)}, bf16[8,8,128,128]{3,2,1,0:T(8,128)(2,1)}) custom-call(bf16[128,5120]{1,0:T(8,128)(2,1)S(1)} %bitcast.19, bf16[128,5120]{1,0:T(8,128)(2,1)S(1)} %bitcast.21, bf16[128,5120]{1,0:T(8,128)(2,1)S(1)} %bitcast.22, bf16[128,5120]{1,0:T(8,128)(2,1)S(1)} %bitcast.23), custom_call_target="tpu_custom_call" | custom-call | bytes 10485760 | tf_op jit(solution)/shard_map/pack/pallas_call | solution.py:49
  15.3 10.1 %all-to-all-done.kc_ref.vc_ref = bf16[8,4,128,128]{3,2,1,0:T(8,128)(2,1)} async-done(((bf16[8,4,128,128]{3,2,1,0:T(8,128)(2,1)}), bf16[8,4,128,128]{3,2,1,0:T(8,128)(2,1)}, u32[]{:S(2)}, u32[]{:S(2)}) %all-to-all-start) | async-done | bytes 1048608 | tf_op jit(solution)/shard_map/all_to_all | solution.py:262
  25.4 3.6 %all-to-all-start.1 = ((bf16[8,8,128,128]{3,2,1,0:T(8,128)(2,1)}), bf16[8,8,128,128]{3,2,1,0:T(8,128)(2,1)S(1)}, u32[]{:S(2)}, u32[]{:S(2)}) async-start(bf16[8,8,128,128]{3,2,1,0:T(8,128)(2,1)} %get-tuple-element.30), calls=%async_computation.1 | async-start | bytes 4194304 | tf_op jit(solution)/shard_map/all_to_all | solution.py:262
  29.5 4.0 %collective-permute-start = (bf16[8,4,128,128]{3,2,1,0:T(8,128)(2,1)}, bf16[8,4,128,128]{3,2,1,0:T(8,128)(2,1)S(1)}, u32[]{:S(2)}, u32[]{:S(2)}) collective-permute-start(bf16[8,4,128,128]{3,2,1,0:T(8,128)(2,1)} %all-to-all-done.kc_ref.vc_ref), channel_id=1, source_target_pairs={{0,8},{8,16},{16,24},{1,9},{9,17},{17,25},{2,10},{10,18},{18,26},{... | collective-permute-start | bytes 3145736 | tf_op jit(solution)/shard_map/ppermute | solution.py:281
  34.6 20.9 %all-to-all-done.1.q_ref.c_ref.kc_ref.vc_ref = bf16[8,8,128,128]{3,2,1,0:T(8,128)(2,1)S(1)} async-done(((bf16[8,8,128,128]{3,2,1,0:T(8,128)(2,1)}), bf16[8,8,128,128]{3,2,1,0:T(8,128)(2,1)S(1)}, u32[]{:S(2)}, u32[]{:S(2)}) %all-to-all-start.1) | async-done | bytes 2097184 | tf_op jit(solution)/shard_map/all_to_all | solution.py:262
  55.5 4.3 %all-to-all-start.2 = ((bf16[8,8,128,128]{3,2,1,0:T(8,128)(2,1)}), bf16[8,8,128,128]{3,2,1,0:T(8,128)(2,1)}, u32[]{:S(2)}, u32[]{:S(2)}) async-start(bf16[8,8,128,128]{3,2,1,0:T(8,128)(2,1)} %get-tuple-element.33), calls=%async_computation.2 | async-start | bytes 4194304 | tf_op jit(solution)/shard_map/all_to_all | solution.py:262
  61.1 4.9 %collective-permute-start.1 = (bf16[8,4,128,128]{3,2,1,0:T(8,128)(2,1)}, bf16[8,4,128,128]{3,2,1,0:T(8,128)(2,1)}, u32[]{:S(2)}, u32[]{:S(2)}) collective-permute-start(bf16[8,4,128,128]{3,2,1,0:T(8,128)(2,1)} %slice.20), channel_id=1, source_target_pairs={{0,8},{8,16},{16,24},{1,9},{9,17},{17,25},{2,10},{10,18},{18,26},{... | collective-permute-start | bytes 3145736 | tf_op jit(solution)/shard_map/ppermute | solution.py:281
  67.1 19.2 %attention.3 = (bf16[8,4,128,128]{3,2,1,0:T(8,128)(2,1)}, f32[8,4,128,128]{3,2,1,0:T(8,128)S(1)}, bf16[8,4,128,128]{3,2,1,0:T(8,128)(2,1)}) custom-call(bf16[2,1536,128]{2,1,0:T(8,128)(2,1)S(1)} %bitcast.24, bf16[512,128]{1,0:T(8,128)(2,1)S(1)} %fusion.16.class_ref, bf16[8,8,128,128]{3,2,1,0:T(8,128)(2,1)S(1)} %all-to-all-done.1.q_ref.c_ref.kc_ref.vc_ref, ...), custom_call_target="tpu_custom_call" | custom-call | flops 9663676416 | bytes 9437184 | tf_op jit(solution)/shard_map/attention/pallas_call | solution.py:168
  88.5 4.1 %all-to-all-start.3 = ((bf16[8,4,128,128]{3,2,1,0:T(8,128)(2,1)}), bf16[8,4,128,128]{3,2,1,0:T(8,128)(2,1)S(1)}, u32[]{:S(2)}, u32[]{:S(2)}) async-start(bf16[8,4,128,128]{3,2,1,0:T(8,128)(2,1)} %get-tuple-element.34), calls=%async_computation.3 | async-start | bytes 2097152 | tf_op jit(solution)/shard_map/all_to_all | solution.py:262
  93.9 1.9 slice.21
  95.8 5.3 %collective-permute-start.2 = (bf16[8,2,128,128]{3,2,1,0:T(8,128)(2,1)}, bf16[8,2,128,128]{3,2,1,0:T(8,128)(2,1)}, u32[]{:S(2)}, u32[]{:S(2)}) collective-permute-start(bf16[8,2,128,128]{3,2,1,0:T(8,128)(2,1)} %slice.21), channel_id=1, source_target_pairs={{0,8},{8,16},{16,24},{1,9},{9,17},{17,25},{2,10},{10,18},{18,26},{... | collective-permute-start | bytes 1572872 | tf_op jit(solution)/shard_map/ppermute | solution.py:281
  102.3 19.2 %attention.4 = (bf16[8,4,128,128]{3,2,1,0:T(8,128)(2,1)}, f32[8,4,128,128]{3,2,1,0:T(8,128)S(1)}, bf16[8,4,128,128]{3,2,1,0:T(8,128)(2,1)}) custom-call(bf16[2,1536,128]{2,1,0:T(8,128)(2,1)S(1)} %bitcast.25, bf16[512,128]{1,0:T(8,128)(2,1)S(1)} %fusion.16.class_ref, bf16[8,8,128,128]{3,2,1,0:T(8,128)(2,1)} %all-to-all-done.2.q_ref.c_ref.kc_ref.vc_ref, ...), custom_call_target="tpu_custom_call" | custom-call | flops 9663676416 | bytes 9437184 | tf_op jit(solution)/shard_map/attention/pallas_call | solution.py:168
  124.3 4.2 %all-to-all-start.4 = ((bf16[8,4,128,128]{3,2,1,0:T(8,128)(2,1)}), bf16[8,4,128,128]{3,2,1,0:T(8,128)(2,1)S(1)}, u32[]{:S(2)}, u32[]{:S(2)}) async-start(bf16[8,4,128,128]{3,2,1,0:T(8,128)(2,1)} %get-tuple-element.37), calls=%async_computation.4 | async-start | bytes 2097152 | tf_op jit(solution)/shard_map/all_to_all | solution.py:262
  128.5 10.8 %attention.5 = (bf16[8,2,128,128]{3,2,1,0:T(8,128)(2,1)}, f32[8,2,128,128]{3,2,1,0:T(8,128)S(1)}, bf16[8,2,128,128]{3,2,1,0:T(8,128)(2,1)}) custom-call(bf16[2,1536,128]{2,1,0:T(8,128)(2,1)S(1)} %bitcast.26, bf16[512,128]{1,0:T(8,128)(2,1)S(1)} %fusion.16.class_ref, bf16[8,8,128,128]{3,2,1,0:T(8,128)(2,1)} %all-to-all-done.2.q_ref.c_ref.kc_ref.vc_ref, ...), custom_call_target="tpu_custom_call" | custom-call | flops 4831838208 | bytes 4718592 | tf_op jit(solution)/shard_map/attention/pallas_call | solution.py:168
  139.3 1.9 add_convert_fusion.1
  144.9 3.6 %all-to-all-start.5 = ((bf16[8,6,128,128]{3,2,1,0:T(8,128)(2,1)}), bf16[8,6,128,128]{3,2,1,0:T(8,128)(2,1)S(1)}, u32[]{:S(2)}, u32[]{:S(2)}) async-start(bf16[8,6,128,128]{3,2,1,0:T(8,128)(2,1)} %pad_maximum_fusion), calls=%async_computation.5 | async-start | bytes 3145728 | tf_op jit(solution)/shard_map/all_to_all | solution.py:262
  148.5 1.4 collective-permute-start.5
  149.9 15.7 %collective-permute-done.5 = bf16[8,2,128,128]{3,2,1,0:T(8,128)(2,1)S(1)} collective-permute-done((bf16[8,2,128,128]{3,2,1,0:T(8,128)(2,1)S(1)}, bf16[8,2,128,128]{3,2,1,0:T(8,128)(2,1)S(1)}, u32[]{:S(2)}, u32[]{:S(2)}) %collective-permute-start.5) | collective-permute-done | bytes 524320 | tf_op jit(solution)/shard_map/ppermute | solution.py:292
  165.8 1.5 add_convert_fusion
  169.4 3.6 %all-to-all-start.6 = ((bf16[8,6,128,128]{3,2,1,0:T(8,128)(2,1)}), bf16[8,6,128,128]{3,2,1,0:T(8,128)(2,1)S(1)}, u32[]{:S(2)}, u32[]{:S(2)}) async-start(bf16[8,6,128,128]{3,2,1,0:T(8,128)(2,1)} %pad_maximum_fusion.1), calls=%async_computation.6 | async-start | bytes 3145728 | tf_op jit(solution)/shard_map/all_to_all | solution.py:262
  175.5 1.7 unpack.2
  177.2 16.8 %all-to-all-done.6.refs_1_ = bf16[8,6,128,128]{3,2,1,0:T(8,128)(2,1)S(1)} async-done(((bf16[8,6,128,128]{3,2,1,0:T(8,128)(2,1)}), bf16[8,6,128,128]{3,2,1,0:T(8,128)(2,1)S(1)}, u32[]{:S(2)}, u32[]{:S(2)}) %all-to-all-start.6) | async-done | bytes 1572896 | tf_op jit(solution)/shard_map/all_to_all | solution.py:262
  194.0 1.7 unpack.3
  (94 shorter events, 26.2 us)
Async XLA Ops:
  0.6 28.6 %copy-start = (s32[8,2,2,10]{3,2,1,0:T(2,128)S(1)}, s32[8,2,2,10]{3,2,1,0:T(2,128)}, u32[]{:S(2)}) copy-start(s32[8,2,2,10]{3,2,1,0:T(2,128)} %param.11) | copy-start | bytes 3844
  3.3 6.6 %copy-start.4 = (bf16[2,4,16,5120]{3,2,1,0:T(8,128)(2,1)S(1)}, bf16[2,4,16,5120]{3,2,1,0:T(8,128)(2,1)}, u32[]{:S(2)}) copy-start(bf16[2,4,16,5120]{3,2,1,0:T(8,128)(2,1)} %param.8) | copy-start | bytes 3932164
  4.5 5.3 %copy-start.21 = (s32[16]{0:T(128)S(1)}, s32[16]{0:T(128)}, u32[]{:S(2)}) copy-start(s32[16]{0:T(128)} %param.10) | copy-start | bytes 196
  4.5 5.4 %copy-start.2 = (bf16[2,4,16,5120]{3,2,1,0:T(8,128)(2,1)S(1)}, bf16[2,4,16,5120]{3,2,1,0:T(8,128)(2,1)}, u32[]{:S(2)}) copy-start(bf16[2,4,16,5120]{3,2,1,0:T(8,128)(2,1)} %param.7) | copy-start | bytes 3932164
  4.5 20.8 %all-to-all-start = ((bf16[8,4,128,128]{3,2,1,0:T(8,128)(2,1)}), bf16[8,4,128,128]{3,2,1,0:T(8,128)(2,1)}, u32[]{:S(2)}, u32[]{:S(2)}) async-start(bf16[8,4,128,128]{3,2,1,0:T(8,128)(2,1)} %pack.3), calls=%async_computation | async-start | bytes 2097152 | tf_op jit(solution)/shard_map/all_to_all | solution.py:262
  25.4 30.2 %all-to-all-start.1 = ((bf16[8,8,128,128]{3,2,1,0:T(8,128)(2,1)}), bf16[8,8,128,128]{3,2,1,0:T(8,128)(2,1)S(1)}, u32[]{:S(2)}, u32[]{:S(2)}) async-start(bf16[8,8,128,128]{3,2,1,0:T(8,128)(2,1)} %get-tuple-element.30), calls=%async_computation.1 | async-start | bytes 4194304 | tf_op jit(solution)/shard_map/all_to_all | solution.py:262
  29.5 31.6 %collective-permute-start = (bf16[8,4,128,128]{3,2,1,0:T(8,128)(2,1)}, bf16[8,4,128,128]{3,2,1,0:T(8,128)(2,1)S(1)}, u32[]{:S(2)}, u32[]{:S(2)}) collective-permute-start(bf16[8,4,128,128]{3,2,1,0:T(8,128)(2,1)} %all-to-all-done.kc_ref.vc_ref), channel_id=1, source_target_pairs={{0,8},{8,16},{16,24},{1,9},{9,17},{17,25},{2,10},{10,18},{18,26},{... | collective-permute-start | bytes 3145736 | tf_op jit(solution)/shard_map/ppermute | solution.py:281
  55.5 33.0 %all-to-all-start.2 = ((bf16[8,8,128,128]{3,2,1,0:T(8,128)(2,1)}), bf16[8,8,128,128]{3,2,1,0:T(8,128)(2,1)}, u32[]{:S(2)}, u32[]{:S(2)}) async-start(bf16[8,8,128,128]{3,2,1,0:T(8,128)(2,1)} %get-tuple-element.33), calls=%async_computation.2 | async-start | bytes 4194304 | tf_op jit(solution)/shard_map/all_to_all | solution.py:262
  61.1 34.7 %collective-permute-start.1 = (bf16[8,4,128,128]{3,2,1,0:T(8,128)(2,1)}, bf16[8,4,128,128]{3,2,1,0:T(8,128)(2,1)}, u32[]{:S(2)}, u32[]{:S(2)}) collective-permute-start(bf16[8,4,128,128]{3,2,1,0:T(8,128)(2,1)} %slice.20), channel_id=1, source_target_pairs={{0,8},{8,16},{16,24},{1,9},{9,17},{17,25},{2,10},{10,18},{18,26},{... | collective-permute-start | bytes 3145736 | tf_op jit(solution)/shard_map/ppermute | solution.py:281
  88.5 35.7 %all-to-all-start.3 = ((bf16[8,4,128,128]{3,2,1,0:T(8,128)(2,1)}), bf16[8,4,128,128]{3,2,1,0:T(8,128)(2,1)S(1)}, u32[]{:S(2)}, u32[]{:S(2)}) async-start(bf16[8,4,128,128]{3,2,1,0:T(8,128)(2,1)} %get-tuple-element.34), calls=%async_computation.3 | async-start | bytes 2097152 | tf_op jit(solution)/shard_map/all_to_all | solution.py:262
  92.6 46.7 %collective-permute-start.3 = (bf16[8,4,128,128]{3,2,1,0:T(8,128)(2,1)}, bf16[8,4,128,128]{3,2,1,0:T(8,128)(2,1)}, u32[]{:S(2)}, u32[]{:S(2)}) collective-permute-start(bf16[8,4,128,128]{3,2,1,0:T(8,128)(2,1)} %get-tuple-element.41), channel_id=1, source_target_pairs={{8,0},{16,8},{24,16},{9,1},{17,9},{25,17},{10,2},{18,10},{26,18},{... | collective-permute-start | bytes 3145736 | tf_op jit(solution)/shard_map/ppermute | solution.py:292
  95.8 32.7 %collective-permute-start.2 = (bf16[8,2,128,128]{3,2,1,0:T(8,128)(2,1)}, bf16[8,2,128,128]{3,2,1,0:T(8,128)(2,1)}, u32[]{:S(2)}, u32[]{:S(2)}) collective-permute-start(bf16[8,2,128,128]{3,2,1,0:T(8,128)(2,1)} %slice.21), channel_id=1, source_target_pairs={{0,8},{8,16},{16,24},{1,9},{9,17},{17,25},{2,10},{10,18},{18,26},{... | collective-permute-start | bytes 1572872 | tf_op jit(solution)/shard_map/ppermute | solution.py:281
  122.8 5.7 %copy-start.19 = (bf16[2,3,2,2,2,4,2,8,128]{8,7,6,5,4,3,2,1,0:T(8,128)(2,1)S(1)}, bf16[2,3,2,2,2,4,2,8,128]{8,7,6,5,4,3,2,1,0:T(8,128)(2,1)}, u32[]{:S(2)}) copy-start(bf16[2,3,2,2,2,4,2,8,128]{8,7,6,5,4,3,2,1,0:T(8,128)(2,1)} %copy-done.17) | copy-start | bytes 2359300
  122.8 43.0 %collective-permute-start.4 = (bf16[8,4,128,128]{3,2,1,0:T(8,128)(2,1)}, bf16[8,4,128,128]{3,2,1,0:T(8,128)(2,1)}, u32[]{:S(2)}, u32[]{:S(2)}) collective-permute-start(bf16[8,4,128,128]{3,2,1,0:T(8,128)(2,1)} %get-tuple-element.48), channel_id=1, source_target_pairs={{8,0},{16,8},{24,16},{9,1},{17,9},{25,17},{10,2},{18,10},{26,18},{... | collective-permute-start | bytes 3145736 | tf_op jit(solution)/shard_map/ppermute | solution.py:292
  124.3 15.0 %copy-start.5 = (bf16[8,4,128,128]{3,2,1,0:T(8,128)(2,1)}, bf16[8,4,128,128]{3,2,1,0:T(8,128)(2,1)S(1)}, u32[]{:S(2)}) copy-start(bf16[8,4,128,128]{3,2,1,0:T(8,128)(2,1)S(1)} %all-to-all-done.3.refs_0_) | copy-start | bytes 3145732
  124.3 19.6 %all-to-all-start.4 = ((bf16[8,4,128,128]{3,2,1,0:T(8,128)(2,1)}), bf16[8,4,128,128]{3,2,1,0:T(8,128)(2,1)S(1)}, u32[]{:S(2)}, u32[]{:S(2)}) async-start(bf16[8,4,128,128]{3,2,1,0:T(8,128)(2,1)} %get-tuple-element.37), calls=%async_computation.4 | async-start | bytes 2097152 | tf_op jit(solution)/shard_map/all_to_all | solution.py:262
  128.5 10.8 %copy-start.12 = (f32[8,4,128,128]{3,2,1,0:T(8,128)S(1)}, f32[8,4,128,128]{3,2,1,0:T(8,128)}, u32[]{:S(2)}) copy-start(f32[8,4,128,128]{3,2,1,0:T(8,128)} %copy-done.11) | copy-start | bytes 6291460
  139.3 1.9 copy-start.15
  142.6 5.9 %copy-start.22 = (bf16[8,2,128,128]{3,2,1,0:T(8,128)(2,1)S(1)}, bf16[8,2,128,128]{3,2,1,0:T(8,128)(2,1)}, u32[]{:S(2)}) copy-start(bf16[8,2,128,128]{3,2,1,0:T(8,128)(2,1)} %get-tuple-element.50) | copy-start | bytes 1572868
  142.6 23.1 %copy-start.16 = (f32[8,2,128,128]{3,2,1,0:T(8,128)S(1)}, f32[8,2,128,128]{3,2,1,0:T(8,128)}, u32[]{:S(2)}) copy-start(f32[8,2,128,128]{3,2,1,0:T(8,128)} %copy-done.15) | copy-start | bytes 3145732
  144.9 24.5 %all-to-all-start.5 = ((bf16[8,6,128,128]{3,2,1,0:T(8,128)(2,1)}), bf16[8,6,128,128]{3,2,1,0:T(8,128)(2,1)S(1)}, u32[]{:S(2)}, u32[]{:S(2)}) async-start(bf16[8,6,128,128]{3,2,1,0:T(8,128)(2,1)} %pad_maximum_fusion), calls=%async_computation.5 | async-start | bytes 3145728 | tf_op jit(solution)/shard_map/all_to_all | solution.py:262
  148.5 17.3 %copy-start.10 = (f32[8,4,128,128]{3,2,1,0:T(8,128)S(1)}, f32[8,4,128,128]{3,2,1,0:T(8,128)}, u32[]{:S(2)}) copy-start(f32[8,4,128,128]{3,2,1,0:T(8,128)} %copy-done.9) | copy-start | bytes 6291460
  148.5 17.1 %collective-permute-start.5 = (bf16[8,2,128,128]{3,2,1,0:T(8,128)(2,1)S(1)}, bf16[8,2,128,128]{3,2,1,0:T(8,128)(2,1)S(1)}, u32[]{:S(2)}, u32[]{:S(2)}) collective-permute-start(bf16[8,2,128,128]{3,2,1,0:T(8,128)(2,1)S(1)} %copy-done.22), channel_id=1, source_target_pairs={{8,0},{16,8},{24,16},{9,1},{17,9},{25,17},{10,2},{18,10},{26,18},{... | collective-permute-start | bytes 1572872 | tf_op jit(solution)/shard_map/ppermute | solution.py:292
  169.4 24.5 %all-to-all-start.6 = ((bf16[8,6,128,128]{3,2,1,0:T(8,128)(2,1)}), bf16[8,6,128,128]{3,2,1,0:T(8,128)(2,1)S(1)}, u32[]{:S(2)}, u32[]{:S(2)}) async-start(bf16[8,6,128,128]{3,2,1,0:T(8,128)(2,1)} %pad_maximum_fusion.1), calls=%async_computation.6 | async-start | bytes 3145728 | tf_op jit(solution)/shard_map/all_to_all | solution.py:262
  (12 other events, 15.4 us)

commit v5 on v4

--- a/solution.py
+++ b/solution.py
@@ -29,6 +29,10 @@
     return pltpu.HBM(shape, dtype)
 
 
+def in_hbm(arrays):
+    return [pltpu.with_memory_space_constraint(array, pltpu.HBM) for array in arrays]
+
+
 def pack(pairs, members, heads, layouts):
     names = sorted({name for layout in layouts for name, _ in layout})
     arrays = [array for name in names for array in pairs[name]]
@@ -57,7 +61,7 @@
             flops=0, bytes_accessed=4 * sum(array.size for array in arrays), transcendentals=0
         ),
         name="pack",
-    )(*arrays)
+    )(*in_hbm(arrays))
 
 
 def unpack(buffers, places, members, heads):
@@ -86,12 +90,12 @@
             flops=0, bytes_accessed=8 * tokens * width, transcendentals=0
         ),
         name="unpack",
-    )(*buffers)
+    )(*in_hbm(buffers))
 
 
 def attention_body(
     bias_ref, class_ref, q_ref, c_ref, kc_ref, vc_ref, kp_ref, vp_ref,
-    odq_ref, cur_ref, prev_ref, k_all, v_all, kt_all, vt_all, dk_all, dv_all,
+    odq_ref, cur_ref, prev_ref, k_all, v_all, dk_all, dv_all,
 ):
     parts, rows = q_ref.shape[0], q_ref.shape[1]
     plane = parts * rows
@@ -99,53 +103,44 @@
     scale = HEAD_DIM ** -0.5
     scale2 = scale * math.log2(math.e)
     half = parts // 2
-    quarter = half // 2
-    block = quarter * rows
     k_all[:plane] = kp_ref[...].reshape(plane, HEAD_DIM)
     k_all[plane:] = kc_ref[...].reshape(plane, HEAD_DIM)
     v_all[:plane] = vp_ref[...].reshape(plane, HEAD_DIM)
     v_all[plane:] = vc_ref[...].reshape(plane, HEAD_DIM)
-    kt_all[...] = k_all[...].T
-    vt_all[...] = v_all[...].T
     nt = (((1,), (1,)), ((), ()))
+    tn = (((0,), (0,)), ((), ()))
     for y in range(2):
         window = slice(y * slab, (y + 3) * slab)
-        for piece in range(2):
-            here = pl.ds(y * half + piece * quarter, quarter)
-            q = q_ref[here].reshape(block, HEAD_DIM)
-            c = c_ref[here].reshape(block, HEAD_DIM)
-            classes = class_ref[piece * block : (piece + 1) * block]
-            s = lax.dot_general(
-                jnp.concatenate([k_all[window], bias_ref[y]], axis=1),
-                jnp.concatenate([q, classes], axis=1),
-                nt,
-                preferred_element_type=jnp.float32,
-            )
-            m = jnp.max(s, axis=0, keepdims=True)
-            e = jnp.exp2((s - m) * scale2)
-            p = e * (1.0 / jnp.sum(e, axis=0, keepdims=True))
-            w = p.astype(jnp.bfloat16)
-            o = jnp.dot(vt_all[:, window], w, preferred_element_type=jnp.float32)
-            o = o.astype(jnp.bfloat16).astype(jnp.float32)
-            delta = jnp.sum(c.astype(jnp.float32).T * o, axis=0, keepdims=True)
-            dp = lax.dot_general(v_all[window], c, nt, preferred_element_type=jnp.float32)
-            ds = (p * (dp - delta)).astype(jnp.bfloat16)
-            dq = jnp.dot(kt_all[:, window], ds, preferred_element_type=jnp.float32) * scale
-            odq_ref[here, 0] = o.T.astype(jnp.bfloat16).reshape(quarter, rows, HEAD_DIM)
-            odq_ref[here, 1] = dq.T.astype(jnp.bfloat16).reshape(quarter, rows, HEAD_DIM)
-            dk = jnp.dot(ds, q, preferred_element_type=jnp.float32)
-            dv = jnp.dot(w, c, preferred_element_type=jnp.float32)
-            if y == 0 and piece == 0:
-                dk_all[window] = dk
-                dv_all[window] = dv
-            elif y == 1 and piece == 0:
-                dk_all[slab : 3 * slab] += dk[: 2 * slab]
-                dv_all[slab : 3 * slab] += dv[: 2 * slab]
-                dk_all[3 * slab :] = dk[2 * slab :]
-                dv_all[3 * slab :] = dv[2 * slab :]
-            else:
-                dk_all[window] += dk
-                dv_all[window] += dv
+        here = pl.ds(y * half, half)
+        q = q_ref[here].reshape(slab, HEAD_DIM)
+        c = c_ref[here].reshape(slab, HEAD_DIM)
+        s = lax.dot_general(
+            jnp.concatenate([q, class_ref[...]], axis=1),
+            jnp.concatenate([k_all[window], bias_ref[y]], axis=1),
+            nt,
+            preferred_element_type=jnp.float32,
+        )
+        m = jnp.max(s, axis=1, keepdims=True)
+        e = jnp.exp2((s - m) * scale2)
+        p = e * (1.0 / jnp.sum(e, axis=1, keepdims=True))
+        w = p.astype(jnp.bfloat16)
+        o = jnp.dot(w, v_all[window], preferred_element_type=jnp.float32).astype(jnp.bfloat16)
+        delta = jnp.sum(c.astype(jnp.float32) * o.astype(jnp.float32), axis=1, keepdims=True)
+        dp = lax.dot_general(c, v_all[window], nt, preferred_element_type=jnp.float32)
+        ds = (p * (dp - delta)).astype(jnp.bfloat16)
+        dq = jnp.dot(ds, k_all[window], preferred_element_type=jnp.float32) * scale
+        odq_ref[here, 0] = o.reshape(half, rows, HEAD_DIM)
+        odq_ref[here, 1] = dq.astype(jnp.bfloat16).reshape(half, rows, HEAD_DIM)
+        dk = lax.dot_general(ds, q, tn, preferred_element_type=jnp.float32)
+        dv = lax.dot_general(w, c, tn, preferred_element_type=jnp.float32)
+        if y == 0:
+            dk_all[window] = dk
+            dv_all[window] = dv
+        else:
+            dk_all[slab : 3 * slab] += dk[: 2 * slab]
+            dv_all[slab : 3 * slab] += dv[: 2 * slab]
+            dk_all[3 * slab :] = dk[2 * slab :]
+            dv_all[3 * slab :] = dv[2 * slab :]
     prev_ref[:, 0] = (dk_all[:plane] * scale).astype(jnp.bfloat16).reshape(kp_ref.shape)
     prev_ref[:, 1] = dv_all[:plane].astype(jnp.bfloat16).reshape(kp_ref.shape)
     cur_ref[:, 0] = (dk_all[plane:] * scale).reshape(kp_ref.shape)
@@ -170,7 +165,7 @@
         grid=(count,),
         out_shape=[
             hbm(shape, jnp.bfloat16),
-            jax.ShapeDtypeStruct(shape, jnp.float32),
+            hbm(shape, jnp.float32),
             hbm(shape, jnp.bfloat16),
         ],
         in_specs=[
@@ -181,8 +176,6 @@
         scratch_shapes=[
             pltpu.VMEM((2 * plane, HEAD_DIM), jnp.bfloat16),
             pltpu.VMEM((2 * plane, HEAD_DIM), jnp.bfloat16),
-            pltpu.VMEM((HEAD_DIM, 2 * plane), jnp.bfloat16),
-            pltpu.VMEM((HEAD_DIM, 2 * plane), jnp.bfloat16),
             pltpu.VMEM((2 * plane, HEAD_DIM), jnp.float32),
             pltpu.VMEM((2 * plane, HEAD_DIM), jnp.float32),
         ],
@@ -193,7 +186,7 @@
             transcendentals=products,
         ),
         name="attention",
-    )(bias, classes, *[place[0] for place, _ in operands])
+    )(*in_hbm([bias, classes]), *[place[0] for place, _ in operands])
 
 
 def mask_operands(frame_blocks, tile_lists, z, bands, frame_rows, frame_cols):
@@ -268,8 +261,13 @@
     pairs = {"kv": (k, v), "qc": (q, c)}
     sent = pack(pairs, members, heads, [layout(inward[0])])
     sent += pack(pairs, members, heads, [layout(items) for items in inward[1:]])
+    bias, classes = mask_operands(
+        frame_blocks, tile_lists, z, bands, queries.shape[1] * bands, queries.shape[2]
+    )
     place, shifted = {}, []
     for items, buffer in zip(inward, sent):
+        if items is inward[-1]:
+            buffer = after(buffer, (bias, classes))
         buffer = exchange(buffer)
         slot = 0
         for name, i in items:
@@ -280,9 +278,6 @@
                     moved = after(moved, shifted[-1])
                 shifted.append(lax.ppermute(moved, "plane", up))
             slot += 2 * counts[i]
-    bias, classes = mask_operands(
-        frame_blocks, tile_lists, z, bands, queries.shape[1] * bands, queries.shape[2]
-    )
     made, owed = {}, []
     for i, count in enumerate(counts):
         odq, dkv, dkv_prev = attention(

time: 197 us -> 192 us (0.975)
  local copies, waits for them, and re-layouts: 17.3 us -> 6.3 us
  waiting for transfers between devices: 65.7 us -> 68.4 us
    unnamed x46 -> x18, local copies, waits for them, and re-layouts: 13.5 us -> 2.37 us
    pallas_call x3, Pallas kernels: 49.1 us -> 45 us  [attention(): pl.pallas_call(attention_body, grid=(count,), out_shape=[hbm(shape, jnp.b...]
    pallas_call x2, Pallas kernels: 3.42 us -> 6.43 us  [unpack(): pl.pallas_call(body, grid=(STEPS,), out_shape=[jax.ShapeDtypeStruct((toke...]
    pallas_call x2, Pallas kernels: 3.93 us -> 6.73 us  [pack(): pl.pallas_call(body, grid=(STEPS,), out_shape=[hbm((members, *shape), arr...]
    all_to_all x7, waiting for transfers between devices: 49.9 us -> 52.7 us  [exchange(): lax.all_to_all(array, group, split_axis=0, concat_axis=0, tiled=True)]
  transfers between devices with their start and end apart: 13 -> 13, of which waited for: 6 -> 7; matrix products, arithmetic and copies ran while one was open for 6% -> 7% of each run, Pallas kernels for 27% -> 28%
where the time goes in v5:
time: 192 us; the launch traced here: 190 us
  waiting for transfers between devices  68.4 us (36%)
  Pallas kernels  58.2 us (30%)
  starting transfers between devices  47 us (24%)
  other arithmetic  8.82 us (5%)
  local copies, waits for them, and re-layouts  6.3 us (3%)
    all_to_all x7, waiting for transfers between devices, exchange(): lax.all_to_all(array, group, split_axis=0, concat_axis=0, tiled=True)  52.7 us
    pallas_call x3, Pallas kernels, attention(): pl.pallas_call(attention_body, grid=(count,), out_shape=[hbm(shape, jnp.b...  45 us
    all_to_all x7, starting transfers between devices, exchange(): lax.all_to_all(array, group, split_axis=0, concat_axis=0, tiled=True)  29.1 us
    ppermute x3, waiting for transfers between devices, on_device(): owed.append((dkv, lax.ppermute(dkv_prev, 'plane', down)))  15.7 us
    ppermute x3, starting transfers between devices, on_device(): shifted.append(lax.ppermute(moved, 'plane', up))  13.8 us
    pallas_call x2, Pallas kernels, pack(): pl.pallas_call(body, grid=(STEPS,), out_shape=[hbm((members, *shape), arr...  6.73 us
    pallas_call x2, Pallas kernels, unpack(): pl.pallas_call(body, grid=(STEPS,), out_shape=[jax.ShapeDtypeStruct((toke...  6.43 us
    ppermute x3, starting transfers between devices, on_device(): owed.append((dkv, lax.ppermute(dkv_prev, 'plane', down)))  4 us
  transfers between devices with their start and end apart: 13, of which 7 were waited for; matrix products, arithmetic and copies ran while one was open for 7% of the time, Pallas kernels for 28%

profile of v5, /device:TPU:0, one launch (start us, length us, event | category | flops | bytes accessed | tf_op | source)
XLA Modules:
  0.0 189.7 jit_solution(3746770674822053510)
XLA Ops:
  0.6 2.6 %pack.3 = bf16[8,4,128,128]{3,2,1,0:T(8,128)(2,1)} custom-call(bf16[128,5120]{1,0:T(8,128)(2,1)} %bitcast.18, bf16[128,5120]{1,0:T(8,128)(2,1)} %bitcast.20), custom_call_target="tpu_custom_call" | custom-call | bytes 5242880 | tf_op jit(solution)/shard_map/pack/pallas_call | solution.py:53
  3.2 5.3 %all-to-all-start = ((bf16[8,4,128,128]{3,2,1,0:T(8,128)(2,1)}), bf16[8,4,128,128]{3,2,1,0:T(8,128)(2,1)S(1)}, u32[]{:S(2)}, u32[]{:S(2)}) async-start(bf16[8,4,128,128]{3,2,1,0:T(8,128)(2,1)} %pack.3), calls=%async_computation | async-start | bytes 2097152 | tf_op jit(solution)/shard_map/all_to_all | solution.py:255
  8.8 4.2 %pack.2 = (bf16[8,8,128,128]{3,2,1,0:T(8,128)(2,1)}, bf16[8,8,128,128]{3,2,1,0:T(8,128)(2,1)}) custom-call(bf16[128,5120]{1,0:T(8,128)(2,1)} %bitcast.19, bf16[128,5120]{1,0:T(8,128)(2,1)} %bitcast.21, bf16[128,5120]{1,0:T(8,128)(2,1)} %bitcast.22, bf16[128,5120]{1,0:T(8,128)(2,1)} %bitcast.23), custom_call_target="tpu_custom_call" | custom-call | bytes 10485760 | tf_op jit(solution)/shard_map/pack/pallas_call | solution.py:53
  13.1 10.8 %all-to-all-done.kc_ref.vc_ref = bf16[8,4,128,128]{3,2,1,0:T(8,128)(2,1)S(1)} async-done(((bf16[8,4,128,128]{3,2,1,0:T(8,128)(2,1)}), bf16[8,4,128,128]{3,2,1,0:T(8,128)(2,1)S(1)}, u32[]{:S(2)}, u32[]{:S(2)}) %all-to-all-start) | async-done | bytes 1048608 | tf_op jit(solution)/shard_map/all_to_all | solution.py:255
  23.9 3.6 %all-to-all-start.1 = ((bf16[8,8,128,128]{3,2,1,0:T(8,128)(2,1)}), bf16[8,8,128,128]{3,2,1,0:T(8,128)(2,1)S(1)}, u32[]{:S(2)}, u32[]{:S(2)}) async-start(bf16[8,8,128,128]{3,2,1,0:T(8,128)(2,1)} %get-tuple-element.31), calls=%async_computation.1 | async-start | bytes 4194304 | tf_op jit(solution)/shard_map/all_to_all | solution.py:255
  28.9 4.5 %collective-permute-start = (bf16[8,4,128,128]{3,2,1,0:T(8,128)(2,1)S(1)}, bf16[8,4,128,128]{3,2,1,0:T(8,128)(2,1)}, u32[]{:S(2)}, u32[]{:S(2)}) collective-permute-start(bf16[8,4,128,128]{3,2,1,0:T(8,128)(2,1)S(1)} %all-to-all-done.kc_ref.vc_ref), channel_id=1, source_target_pairs={{0,8},{8,16},{16,24},{1,9},{9,17},{17,25},{2,10},{10,18},{18,26},{... | collective-permute-start | bytes 3145736 | tf_op jit(solution)/shard_map/ppermute | solution.py:279
  33.4 2.0 %fusion.16.class_ref = bf16[512,128]{1,0:T(8,128)(2,1)} fusion(s32[512]{0:T(512)S(1)} %get-tuple-element.58, s32[512]{0:T(512)S(1)} %get-tuple-element.64, s32[512]{0:T(512)S(1)} %get-tuple-element.59, s32[512]{0:T(512)S(1)} %get-tuple-element.61, s32[512]{0:T(512)S(1)} %get-tuple-element.60, s32[512]{0:T(512)S(1)} %get-tuple-element.65, ...), kind=kLoop, calls=%fused_computation.40 | loop fusion | flops 3276800 | bytes 144896 | tf_op jit(solution)/shard_map/convert_element_type | solution.py:225
  36.4 17.8 %all-to-all-done.1.q_ref.c_ref.kc_ref.vc_ref = bf16[8,8,128,128]{3,2,1,0:T(8,128)(2,1)S(1)} async-done(((bf16[8,8,128,128]{3,2,1,0:T(8,128)(2,1)}), bf16[8,8,128,128]{3,2,1,0:T(8,128)(2,1)S(1)}, u32[]{:S(2)}, u32[]{:S(2)}) %all-to-all-start.1) | async-done | bytes 2097184 | tf_op jit(solution)/shard_map/all_to_all | solution.py:255
  54.1 4.3 %all-to-all-start.2 = ((bf16[8,8,128,128]{3,2,1,0:T(8,128)(2,1)}), bf16[8,8,128,128]{3,2,1,0:T(8,128)(2,1)}, u32[]{:S(2)}, u32[]{:S(2)}) async-start(bf16[8,8,128,128]{3,2,1,0:T(8,128)(2,1)} %get-tuple-element.35), calls=%async_computation.2 | async-start | bytes 4194304 | tf_op jit(solution)/shard_map/all_to_all | solution.py:255
  59.6 4.6 %collective-permute-start.1 = (bf16[8,4,128,128]{3,2,1,0:T(8,128)(2,1)}, bf16[8,4,128,128]{3,2,1,0:T(8,128)(2,1)}, u32[]{:S(2)}, u32[]{:S(2)}) collective-permute-start(bf16[8,4,128,128]{3,2,1,0:T(8,128)(2,1)} %slice.20), channel_id=1, source_target_pairs={{0,8},{8,16},{16,24},{1,9},{9,17},{17,25},{2,10},{10,18},{18,26},{... | collective-permute-start | bytes 3145736 | tf_op jit(solution)/shard_map/ppermute | solution.py:279
  64.1 17.4 %attention.3 = (bf16[8,4,128,128]{3,2,1,0:T(8,128)(2,1)}, f32[8,4,128,128]{3,2,1,0:T(8,128)}, bf16[8,4,128,128]{3,2,1,0:T(8,128)(2,1)}) custom-call(bf16[2,1536,128]{2,1,0:T(8,128)(2,1)} %bitcast.24, bf16[512,128]{1,0:T(8,128)(2,1)} %fusion.16.class_ref, bf16[8,8,128,128]{3,2,1,0:T(8,128)(2,1)S(1)} %all-to-all-done.1.q_ref.c_ref.kc_ref.vc_ref, ...), custom_call_target="tpu_custom_call" | custom-call | flops 9663676416 | bytes 9437184 | tf_op jit(solution)/shard_map/attention/pallas_call | solution.py:163
  81.5 3.6 %all-to-all-done.2.q_ref.c_ref.kc_ref.vc_ref = bf16[8,8,128,128]{3,2,1,0:T(8,128)(2,1)} async-done(((bf16[8,8,128,128]{3,2,1,0:T(8,128)(2,1)}), bf16[8,8,128,128]{3,2,1,0:T(8,128)(2,1)}, u32[]{:S(2)}, u32[]{:S(2)}) %all-to-all-start.2) | async-done | bytes 2097184 | tf_op jit(solution)/shard_map/all_to_all | solution.py:255
  85.1 4.3 %all-to-all-start.3 = ((bf16[8,4,128,128]{3,2,1,0:T(8,128)(2,1)}), bf16[8,4,128,128]{3,2,1,0:T(8,128)(2,1)}, u32[]{:S(2)}, u32[]{:S(2)}) async-start(bf16[8,4,128,128]{3,2,1,0:T(8,128)(2,1)} %get-tuple-element.36), calls=%async_computation.3 | async-start | bytes 2097152 | tf_op jit(solution)/shard_map/all_to_all | solution.py:255
  91.8 4.8 %collective-permute-start.2 = (bf16[8,2,128,128]{3,2,1,0:T(8,128)(2,1)S(1)}, bf16[8,2,128,128]{3,2,1,0:T(8,128)(2,1)S(1)}, u32[]{:S(2)}, u32[]{:S(2)}) collective-permute-start(bf16[8,2,128,128]{3,2,1,0:T(8,128)(2,1)S(1)} %slice.21), channel_id=1, source_target_pairs={{0,8},{8,16},{16,24},{1,9},{9,17},{17,25},{2,10},{10,18},{18,26},{... | collective-permute-start | bytes 1572872 | tf_op jit(solution)/shard_map/ppermute | solution.py:279
  96.6 17.5 %attention.4 = (bf16[8,4,128,128]{3,2,1,0:T(8,128)(2,1)}, f32[8,4,128,128]{3,2,1,0:T(8,128)}, bf16[8,4,128,128]{3,2,1,0:T(8,128)(2,1)}) custom-call(bf16[2,1536,128]{2,1,0:T(8,128)(2,1)} %bitcast.25, bf16[512,128]{1,0:T(8,128)(2,1)} %fusion.16.class_ref, bf16[8,8,128,128]{3,2,1,0:T(8,128)(2,1)} %all-to-all-done.2.q_ref.c_ref.kc_ref.vc_ref, ...), custom_call_target="tpu_custom_call" | custom-call | flops 9663676416 | bytes 9437184 | tf_op jit(solution)/shard_map/attention/pallas_call | solution.py:163
  115.4 4.5 %all-to-all-start.4 = ((bf16[8,4,128,128]{3,2,1,0:T(8,128)(2,1)}), bf16[8,4,128,128]{3,2,1,0:T(8,128)(2,1)}, u32[]{:S(2)}, u32[]{:S(2)}) async-start(bf16[8,4,128,128]{3,2,1,0:T(8,128)(2,1)} %get-tuple-element.39), calls=%async_computation.4 | async-start | bytes 2097152 | tf_op jit(solution)/shard_map/all_to_all | solution.py:255
  119.9 10.1 %attention.5 = (bf16[8,2,128,128]{3,2,1,0:T(8,128)(2,1)}, f32[8,2,128,128]{3,2,1,0:T(8,128)}, bf16[8,2,128,128]{3,2,1,0:T(8,128)(2,1)}) custom-call(bf16[2,1536,128]{2,1,0:T(8,128)(2,1)} %bitcast.26, bf16[512,128]{1,0:T(8,128)(2,1)} %fusion.16.class_ref, bf16[8,8,128,128]{3,2,1,0:T(8,128)(2,1)} %all-to-all-done.2.q_ref.c_ref.kc_ref.vc_ref, ...), custom_call_target="tpu_custom_call" | custom-call | flops 4831838208 | bytes 4718592 | tf_op jit(solution)/shard_map/attention/pallas_call | solution.py:163
  133.0 2.1 %all-to-all-done.4.refs_1_ = bf16[8,4,128,128]{3,2,1,0:T(8,128)(2,1)} async-done(((bf16[8,4,128,128]{3,2,1,0:T(8,128)(2,1)}), bf16[8,4,128,128]{3,2,1,0:T(8,128)(2,1)}, u32[]{:S(2)}, u32[]{:S(2)}) %all-to-all-start.4) | async-done | bytes 1048608 | tf_op jit(solution)/shard_map/all_to_all | solution.py:255
  135.1 3.6 %all-to-all-start.5 = ((bf16[8,6,128,128]{3,2,1,0:T(8,128)(2,1)}), bf16[8,6,128,128]{3,2,1,0:T(8,128)(2,1)S(1)}, u32[]{:S(2)}, u32[]{:S(2)}) async-start(bf16[8,6,128,128]{3,2,1,0:T(8,128)(2,1)} %pad_maximum_fusion), calls=%async_computation.5 | async-start | bytes 3145728 | tf_op jit(solution)/shard_map/all_to_all | solution.py:255
  140.1 15.7 %collective-permute-done.5 = bf16[8,2,128,128]{3,2,1,0:T(8,128)(2,1)S(1)} collective-permute-done((bf16[8,2,128,128]{3,2,1,0:T(8,128)(2,1)S(1)}, bf16[8,2,128,128]{3,2,1,0:T(8,128)(2,1)S(1)}, u32[]{:S(2)}, u32[]{:S(2)}) %collective-permute-start.5) | collective-permute-done | bytes 524320 | tf_op jit(solution)/shard_map/ppermute | solution.py:287
  160.8 3.6 %all-to-all-start.6 = ((bf16[8,6,128,128]{3,2,1,0:T(8,128)(2,1)}), bf16[8,6,128,128]{3,2,1,0:T(8,128)(2,1)S(1)}, u32[]{:S(2)}, u32[]{:S(2)}) async-start(bf16[8,6,128,128]{3,2,1,0:T(8,128)(2,1)} %pad_maximum_fusion.1), calls=%async_computation.6 | async-start | bytes 3145728 | tf_op jit(solution)/shard_map/all_to_all | solution.py:255
  164.4 3.3 %unpack.2 = (bf16[128,5120]{1,0:T(8,128)(2,1)}, bf16[128,5120]{1,0:T(8,128)(2,1)}) custom-call(bf16[8,4,128,128]{3,2,1,0:T(8,128)(2,1)} %all-to-all-done.3.refs_0_, bf16[8,4,128,128]{3,2,1,0:T(8,128)(2,1)} %all-to-all-done.4.refs_1_, bf16[8,6,128,128]{3,2,1,0:T(8,128)(2,1)} %copy-done.1), custom_call_target="tpu_custom_call" | custom-call | bytes 5242880 | tf_op jit(solution)/shard_map/unpack/pallas_call | solution.py:80
  167.7 17.7 %all-to-all-done.6.refs_1_ = bf16[8,6,128,128]{3,2,1,0:T(8,128)(2,1)S(1)} async-done(((bf16[8,6,128,128]{3,2,1,0:T(8,128)(2,1)}), bf16[8,6,128,128]{3,2,1,0:T(8,128)(2,1)S(1)}, u32[]{:S(2)}, u32[]{:S(2)}) %all-to-all-start.6) | async-done | bytes 1572896 | tf_op jit(solution)/shard_map/all_to_all | solution.py:255
  186.5 3.1 %unpack.3 = (bf16[128,5120]{1,0:T(8,128)(2,1)}, bf16[128,5120]{1,0:T(8,128)(2,1)}) custom-call(bf16[8,6,128,128]{3,2,1,0:T(8,128)(2,1)} %copy-done.1, bf16[8,6,128,128]{3,2,1,0:T(8,128)(2,1)} %copy-done.2), custom_call_target="tpu_custom_call" | custom-call | bytes 5242880 | tf_op jit(solution)/shard_map/unpack/pallas_call | solution.py:80
  (66 shorter events, 17.9 us)
Async XLA Ops:
  0.6 12.4 %copy-start = (s32[8,2,2,10]{3,2,1,0:T(2,128)S(1)}, s32[8,2,2,10]{3,2,1,0:T(2,128)}, u32[]{:S(2)}) copy-start(s32[8,2,2,10]{3,2,1,0:T(2,128)} %param.11) | copy-start | bytes 3844
  3.2 5.3 %copy-start.7 = (s32[16]{0:T(128)S(1)}, s32[16]{0:T(128)}, u32[]{:S(2)}) copy-start(s32[16]{0:T(128)} %param.10) | copy-start | bytes 196
  3.2 20.7 %all-to-all-start = ((bf16[8,4,128,128]{3,2,1,0:T(8,128)(2,1)}), bf16[8,4,128,128]{3,2,1,0:T(8,128)(2,1)S(1)}, u32[]{:S(2)}, u32[]{:S(2)}) async-start(bf16[8,4,128,128]{3,2,1,0:T(8,128)(2,1)} %pack.3), calls=%async_computation | async-start | bytes 2097152 | tf_op jit(solution)/shard_map/all_to_all | solution.py:255
  23.9 30.2 %all-to-all-start.1 = ((bf16[8,8,128,128]{3,2,1,0:T(8,128)(2,1)}), bf16[8,8,128,128]{3,2,1,0:T(8,128)(2,1)S(1)}, u32[]{:S(2)}, u32[]{:S(2)}) async-start(bf16[8,8,128,128]{3,2,1,0:T(8,128)(2,1)} %get-tuple-element.31), calls=%async_computation.1 | async-start | bytes 4194304 | tf_op jit(solution)/shard_map/all_to_all | solution.py:255
  28.9 30.6 %collective-permute-start = (bf16[8,4,128,128]{3,2,1,0:T(8,128)(2,1)S(1)}, bf16[8,4,128,128]{3,2,1,0:T(8,128)(2,1)}, u32[]{:S(2)}, u32[]{:S(2)}) collective-permute-start(bf16[8,4,128,128]{3,2,1,0:T(8,128)(2,1)S(1)} %all-to-all-done.kc_ref.vc_ref), channel_id=1, source_target_pairs={{0,8},{8,16},{16,24},{1,9},{9,17},{17,25},{2,10},{10,18},{18,26},{... | collective-permute-start | bytes 3145736 | tf_op jit(solution)/shard_map/ppermute | solution.py:279
  54.1 31.0 %all-to-all-start.2 = ((bf16[8,8,128,128]{3,2,1,0:T(8,128)(2,1)}), bf16[8,8,128,128]{3,2,1,0:T(8,128)(2,1)}, u32[]{:S(2)}, u32[]{:S(2)}) async-start(bf16[8,8,128,128]{3,2,1,0:T(8,128)(2,1)} %get-tuple-element.35), calls=%async_computation.2 | async-start | bytes 4194304 | tf_op jit(solution)/shard_map/all_to_all | solution.py:255
  59.6 32.2 %collective-permute-start.1 = (bf16[8,4,128,128]{3,2,1,0:T(8,128)(2,1)}, bf16[8,4,128,128]{3,2,1,0:T(8,128)(2,1)}, u32[]{:S(2)}, u32[]{:S(2)}) collective-permute-start(bf16[8,4,128,128]{3,2,1,0:T(8,128)(2,1)} %slice.20), channel_id=1, source_target_pairs={{0,8},{8,16},{16,24},{1,9},{9,17},{17,25},{2,10},{10,18},{18,26},{... | collective-permute-start | bytes 3145736 | tf_op jit(solution)/shard_map/ppermute | solution.py:279
  85.1 30.3 %all-to-all-start.3 = ((bf16[8,4,128,128]{3,2,1,0:T(8,128)(2,1)}), bf16[8,4,128,128]{3,2,1,0:T(8,128)(2,1)}, u32[]{:S(2)}, u32[]{:S(2)}) async-start(bf16[8,4,128,128]{3,2,1,0:T(8,128)(2,1)} %get-tuple-element.36), calls=%async_computation.3 | async-start | bytes 2097152 | tf_op jit(solution)/shard_map/all_to_all | solution.py:255
  89.4 40.6 %collective-permute-start.3 = (bf16[8,4,128,128]{3,2,1,0:T(8,128)(2,1)}, bf16[8,4,128,128]{3,2,1,0:T(8,128)(2,1)}, u32[]{:S(2)}, u32[]{:S(2)}) collective-permute-start(bf16[8,4,128,128]{3,2,1,0:T(8,128)(2,1)} %get-tuple-element.43), channel_id=1, source_target_pairs={{8,0},{16,8},{24,16},{9,1},{17,9},{25,17},{10,2},{18,10},{26,18},{... | collective-permute-start | bytes 3145736 | tf_op jit(solution)/shard_map/ppermute | solution.py:287
  91.8 28.1 %collective-permute-start.2 = (bf16[8,2,128,128]{3,2,1,0:T(8,128)(2,1)S(1)}, bf16[8,2,128,128]{3,2,1,0:T(8,128)(2,1)S(1)}, u32[]{:S(2)}, u32[]{:S(2)}) collective-permute-start(bf16[8,2,128,128]{3,2,1,0:T(8,128)(2,1)S(1)} %slice.21), channel_id=1, source_target_pairs={{0,8},{8,16},{16,24},{1,9},{9,17},{17,25},{2,10},{10,18},{18,26},{... | collective-permute-start | bytes 1572872 | tf_op jit(solution)/shard_map/ppermute | solution.py:279
  114.1 41.9 %collective-permute-start.4 = (bf16[8,4,128,128]{3,2,1,0:T(8,128)(2,1)}, bf16[8,4,128,128]{3,2,1,0:T(8,128)(2,1)}, u32[]{:S(2)}, u32[]{:S(2)}) collective-permute-start(bf16[8,4,128,128]{3,2,1,0:T(8,128)(2,1)} %get-tuple-element.50), channel_id=1, source_target_pairs={{8,0},{16,8},{24,16},{9,1},{17,9},{25,17},{10,2},{18,10},{26,18},{... | collective-permute-start | bytes 3145736 | tf_op jit(solution)/shard_map/ppermute | solution.py:287
  115.4 19.7 %all-to-all-start.4 = ((bf16[8,4,128,128]{3,2,1,0:T(8,128)(2,1)}), bf16[8,4,128,128]{3,2,1,0:T(8,128)(2,1)}, u32[]{:S(2)}, u32[]{:S(2)}) async-start(bf16[8,4,128,128]{3,2,1,0:T(8,128)(2,1)} %get-tuple-element.39), calls=%async_computation.4 | async-start | bytes 2097152 | tf_op jit(solution)/shard_map/all_to_all | solution.py:255
  119.9 10.1 %copy-start.4 = (f32[8,4,128,128]{3,2,1,0:T(8,128)S(1)}, f32[8,4,128,128]{3,2,1,0:T(8,128)}, u32[]{:S(2)}) copy-start(f32[8,4,128,128]{3,2,1,0:T(8,128)} %get-tuple-element.42) | copy-start | bytes 6291460
  130.0 1.6 copy-start.6
  133.0 5.7 %copy-start.8 = (bf16[8,2,128,128]{3,2,1,0:T(8,128)(2,1)S(1)}, bf16[8,2,128,128]{3,2,1,0:T(8,128)(2,1)}, u32[]{:S(2)}) copy-start(bf16[8,2,128,128]{3,2,1,0:T(8,128)(2,1)} %get-tuple-element.52) | copy-start | bytes 1572868
  133.0 22.9 %copy-start.5 = (f32[8,2,128,128]{3,2,1,0:T(8,128)S(1)}, f32[8,2,128,128]{3,2,1,0:T(8,128)}, u32[]{:S(2)}) copy-start(f32[8,2,128,128]{3,2,1,0:T(8,128)} %get-tuple-element.44) | copy-start | bytes 3145732
  135.1 24.5 %all-to-all-start.5 = ((bf16[8,6,128,128]{3,2,1,0:T(8,128)(2,1)}), bf16[8,6,128,128]{3,2,1,0:T(8,128)(2,1)S(1)}, u32[]{:S(2)}, u32[]{:S(2)}) async-start(bf16[8,6,128,128]{3,2,1,0:T(8,128)(2,1)} %pad_maximum_fusion), calls=%async_computation.5 | async-start | bytes 3145728 | tf_op jit(solution)/shard_map/all_to_all | solution.py:255
  138.7 17.3 %copy-start.3 = (f32[8,4,128,128]{3,2,1,0:T(8,128)S(1)}, f32[8,4,128,128]{3,2,1,0:T(8,128)}, u32[]{:S(2)}) copy-start(f32[8,4,128,128]{3,2,1,0:T(8,128)} %get-tuple-element.49) | copy-start | bytes 6291460
  138.7 17.1 %collective-permute-start.5 = (bf16[8,2,128,128]{3,2,1,0:T(8,128)(2,1)S(1)}, bf16[8,2,128,128]{3,2,1,0:T(8,128)(2,1)S(1)}, u32[]{:S(2)}, u32[]{:S(2)}) collective-permute-start(bf16[8,2,128,128]{3,2,1,0:T(8,128)(2,1)S(1)} %copy-done.8), channel_id=1, source_target_pairs={{8,0},{16,8},{24,16},{9,1},{17,9},{25,17},{10,2},{18,10},{26,18},{... | collective-permute-start | bytes 1572872 | tf_op jit(solution)/shard_map/ppermute | solution.py:287
  159.6 1.2 copy-start.1
  160.8 24.5 %all-to-all-start.6 = ((bf16[8,6,128,128]{3,2,1,0:T(8,128)(2,1)}), bf16[8,6,128,128]{3,2,1,0:T(8,128)(2,1)S(1)}, u32[]{:S(2)}, u32[]{:S(2)}) async-start(bf16[8,6,128,128]{3,2,1,0:T(8,128)(2,1)} %pad_maximum_fusion.1), calls=%async_computation.6 | async-start | bytes 3145728 | tf_op jit(solution)/shard_map/all_to_all | solution.py:255
  185.4 1.2 copy-start.2

commit v6 on v5

--- a/solution.py
+++ b/solution.py
@@ -17,7 +17,7 @@
 K_NB = 10
 MASKED = -1e30
 CHUNKS = (2, 2, 1)
-INWARD = ((("kv", 0),), (("kv", 1), ("qc", 0)), (("qc", 1), ("qc", 2), ("kv", 2)))
+INWARD = ((("kv", 0),), (("kv", 1), ("qc", 0), ("kv", 2)), (("qc", 1), ("qc", 2)))
 OUTWARD = ((("o", 0),), (("o", 1),), (("o", 2), ("d", 0)), (("d", 1), ("d", 2)))
 VMEM_LIMIT = 32 * 1024 * 1024
 
@@ -90,7 +90,7 @@
             flops=0, bytes_accessed=8 * tokens * width, transcendentals=0
         ),
         name="unpack",
-    )(*in_hbm(buffers))
+    )(*buffers)
 
 
 def attention_body(
@@ -109,38 +109,81 @@
     v_all[plane:] = vc_ref[...].reshape(plane, HEAD_DIM)
     nt = (((1,), (1,)), ((), ()))
     tn = (((0,), (0,)), ((), ()))
-    for y in range(2):
-        window = slice(y * slab, (y + 3) * slab)
-        here = pl.ds(y * half, half)
-        q = q_ref[here].reshape(slab, HEAD_DIM)
-        c = c_ref[here].reshape(slab, HEAD_DIM)
+    block = half // 2 * rows
+    tile = 2 * HEAD_DIM
+    tiles = range(3 * slab // tile)
+    blocks = [(y, piece) for y in range(2) for piece in range(2)]
+
+    def queries_of(j):
+        y, piece = blocks[j]
+        here = pl.ds(y * half + piece * (half // 2), half // 2)
+        return q_ref[here].reshape(block, HEAD_DIM), c_ref[here].reshape(block, HEAD_DIM)
+
+    def keys_of(j, t):
+        start = blocks[j][0] * slab + t * tile
+        return slice(start, start + tile)
+
+    def scores(j, t):
+        y, piece = blocks[j]
+        q, c = queries_of(j)
         s = lax.dot_general(
-            jnp.concatenate([q, class_ref[...]], axis=1),
-            jnp.concatenate([k_all[window], bias_ref[y]], axis=1),
+            jnp.concatenate([q, class_ref[piece * block : (piece + 1) * block]], axis=1),
+            jnp.concatenate(
+                [k_all[keys_of(j, t)], bias_ref[y, t * tile : (t + 1) * tile]], axis=1
+            ),
             nt,
             preferred_element_type=jnp.float32,
         )
-        m = jnp.max(s, axis=1, keepdims=True)
-        e = jnp.exp2((s - m) * scale2)
-        p = e * (1.0 / jnp.sum(e, axis=1, keepdims=True))
-        w = p.astype(jnp.bfloat16)
-        o = jnp.dot(w, v_all[window], preferred_element_type=jnp.float32).astype(jnp.bfloat16)
-        delta = jnp.sum(c.astype(jnp.float32) * o.astype(jnp.float32), axis=1, keepdims=True)
-        dp = lax.dot_general(c, v_all[window], nt, preferred_element_type=jnp.float32)
-        ds = (p * (dp - delta)).astype(jnp.bfloat16)
-        dq = jnp.dot(ds, k_all[window], preferred_element_type=jnp.float32) * scale
-        odq_ref[here, 0] = o.reshape(half, rows, HEAD_DIM)
-        odq_ref[here, 1] = dq.astype(jnp.bfloat16).reshape(half, rows, HEAD_DIM)
+        dp = lax.dot_general(
+            c, v_all[keys_of(j, t)], nt, preferred_element_type=jnp.float32
+        )
+        return s, dp
+
+    def key_grads(j, t, w, ds):
+        q, c = queries_of(j)
         dk = lax.dot_general(ds, q, tn, preferred_element_type=jnp.float32)
         dv = lax.dot_general(w, c, tn, preferred_element_type=jnp.float32)
-        if y == 0:
-            dk_all[window] = dk
-            dv_all[window] = dv
+        keys = keys_of(j, t)
+        if j == 0 or (j == 2 and keys.start >= 3 * slab):
+            dk_all[keys] = dk
+            dv_all[keys] = dv
         else:
-            dk_all[slab : 3 * slab] += dk[: 2 * slab]
-            dv_all[slab : 3 * slab] += dv[: 2 * slab]
-            dk_all[3 * slab :] = dk[2 * slab :]
-            dv_all[3 * slab :] = dv[2 * slab :]
+            dk_all[keys] += dk
+            dv_all[keys] += dv
+
+    ready = [scores(0, t) for t in tiles]
+    owed = None
+    for j, (y, piece) in enumerate(blocks):
+        window = slice(y * slab, (y + 3) * slab)
+        here = pl.ds(y * half + piece * (half // 2), half // 2)
+        _, c = queries_of(j)
+        m = functools.reduce(jnp.maximum, [s for s, _ in ready])
+        m = jnp.max(m, axis=1, keepdims=True)
+        coming, e = [], []
+        for t in tiles:
+            if j + 1 < len(blocks):
+                coming.append(scores(j + 1, t))
+            e.append(jnp.exp2((ready[t][0] - m) * scale2))
+        r = 1.0 / jnp.sum(functools.reduce(jnp.add, e), axis=1, keepdims=True)
+        p, w = [], []
+        for t in tiles:
+            if owed is not None:
+                key_grads(j - 1, t, owed[0][t], owed[1][t])
+            p.append(e[t] * r)
+            w.append(p[t].astype(jnp.bfloat16))
+        o = jnp.dot(
+            jnp.concatenate(w, axis=1), v_all[window], preferred_element_type=jnp.float32
+        ).astype(jnp.bfloat16)
+        delta = jnp.sum(c.astype(jnp.float32) * o.astype(jnp.float32), axis=1, keepdims=True)
+        ds = [(p[t] * (ready[t][1] - delta)).astype(jnp.bfloat16) for t in tiles]
+        dq = jnp.dot(
+            jnp.concatenate(ds, axis=1), k_all[window], preferred_element_type=jnp.float32
+        )
+        odq_ref[here, 0] = o.reshape(half // 2, rows, HEAD_DIM)
+        odq_ref[here, 1] = (dq * scale).astype(jnp.bfloat16).reshape(half // 2, rows, HEAD_DIM)
+        ready, owed = coming, (w, ds)
+    for t in tiles:
+        key_grads(len(blocks) - 1, t, owed[0][t], owed[1][t])
     prev_ref[:, 0] = (dk_all[:plane] * scale).astype(jnp.bfloat16).reshape(kp_ref.shape)
     prev_ref[:, 1] = dv_all[:plane].astype(jnp.bfloat16).reshape(kp_ref.shape)
     cur_ref[:, 0] = (dk_all[plane:] * scale).reshape(kp_ref.shape)

time: 192 us -> 187 us (0.974)
  Pallas kernels: 58.2 us -> 51.4 us
  waiting for transfers between devices: 68.4 us -> 72.4 us
    pallas_call x3, Pallas kernels: 45 us -> 40 us  [attention(): pl.pallas_call(attention_body, grid=(count,), out_shape=[hbm(shape, jnp.b...]
    all_to_all x7, waiting for transfers between devices: 52.7 us -> 56.3 us  [exchange(): lax.all_to_all(array, group, split_axis=0, concat_axis=0, tiled=True)]
  transfers between devices with their start and end apart: 13 -> 13, of which waited for: 7 -> 7; matrix products, arithmetic and copies ran while one was open for 7% -> 7% of each run, Pallas kernels for 28% -> 25%
where the time goes in v6:
time: 187 us; the launch traced here: 185 us
  waiting for transfers between devices  72.4 us (39%)
  Pallas kernels  51.4 us (27%)
  starting transfers between devices  46.7 us (25%)
  other arithmetic  8.77 us (5%)
  local copies, waits for them, and re-layouts  4.63 us (2%)
    all_to_all x7, waiting for transfers between devices, exchange(): lax.all_to_all(array, group, split_axis=0, concat_axis=0, tiled=True)  56.3 us
    pallas_call x3, Pallas kernels, attention(): pl.pallas_call(attention_body, grid=(count,), out_shape=[hbm(shape, jnp.b...  40 us
    all_to_all x7, starting transfers between devices, exchange(): lax.all_to_all(array, group, split_axis=0, concat_axis=0, tiled=True)  29.1 us
    ppermute x3, waiting for transfers between devices, on_device(): owed.append((dkv, lax.ppermute(dkv_prev, 'plane', down)))  15.7 us
    ppermute x3, starting transfers between devices, on_device(): shifted.append(lax.ppermute(moved, 'plane', up))  13.6 us
    pallas_call x2, Pallas kernels, pack(): pl.pallas_call(body, grid=(STEPS,), out_shape=[hbm((members, *shape), arr...  6.74 us
    pallas_call x2, Pallas kernels, unpack(): pl.pallas_call(body, grid=(STEPS,), out_shape=[jax.ShapeDtypeStruct((toke...  4.63 us
    ppermute x3, starting transfers between devices, on_device(): owed.append((dkv, lax.ppermute(dkv_prev, 'plane', down)))  4 us
  transfers between devices with their start and end apart: 13, of which 7 were waited for; matrix products, arithmetic and copies ran while one was open for 7% of the time, Pallas kernels for 25%

profile of v6, /device:TPU:0, one launch (start us, length us, event | category | flops | bytes accessed | tf_op | source)
XLA Modules:
  0.0 184.8 jit_solution(13891620802685721020)
XLA Ops:
  0.6 2.6 %pack.3 = bf16[8,4,128,128]{3,2,1,0:T(8,128)(2,1)} custom-call(bf16[128,5120]{1,0:T(8,128)(2,1)} %bitcast.18, bf16[128,5120]{1,0:T(8,128)(2,1)} %bitcast.20), custom_call_target="tpu_custom_call" | custom-call | bytes 5242880 | tf_op jit(solution)/shard_map/pack/pallas_call | solution.py:53
  3.2 5.3 %all-to-all-start = ((bf16[8,4,128,128]{3,2,1,0:T(8,128)(2,1)}), bf16[8,4,128,128]{3,2,1,0:T(8,128)(2,1)S(1)}, u32[]{:S(2)}, u32[]{:S(2)}) async-start(bf16[8,4,128,128]{3,2,1,0:T(8,128)(2,1)} %pack.3), calls=%async_computation | async-start | bytes 2097152 | tf_op jit(solution)/shard_map/all_to_all | solution.py:298
  8.8 4.2 %pack.2 = (bf16[8,10,128,128]{3,2,1,0:T(8,128)(2,1)}, bf16[8,6,128,128]{3,2,1,0:T(8,128)(2,1)}) custom-call(bf16[128,5120]{1,0:T(8,128)(2,1)} %bitcast.19, bf16[128,5120]{1,0:T(8,128)(2,1)} %bitcast.21, bf16[128,5120]{1,0:T(8,128)(2,1)} %bitcast.22, bf16[128,5120]{1,0:T(8,128)(2,1)} %bitcast.23), custom_call_target="tpu_custom_call" | custom-call | bytes 10485760 | tf_op jit(solution)/shard_map/pack/pallas_call | solution.py:53
  13.0 10.9 %all-to-all-done.kc_ref.vc_ref = bf16[8,4,128,128]{3,2,1,0:T(8,128)(2,1)S(1)} async-done(((bf16[8,4,128,128]{3,2,1,0:T(8,128)(2,1)}), bf16[8,4,128,128]{3,2,1,0:T(8,128)(2,1)S(1)}, u32[]{:S(2)}, u32[]{:S(2)}) %all-to-all-start) | async-done | bytes 1048608 | tf_op jit(solution)/shard_map/all_to_all | solution.py:298
  24.9 3.6 %all-to-all-start.1 = ((bf16[8,10,128,128]{3,2,1,0:T(8,128)(2,1)}), bf16[8,10,128,128]{3,2,1,0:T(8,128)(2,1)S(1)}, u32[]{:S(2)}, u32[]{:S(2)}) async-start(bf16[8,10,128,128]{3,2,1,0:T(8,128)(2,1)} %get-tuple-element.31), calls=%async_computation.1 | async-start | bytes 5242880 | tf_op jit(solution)/shard_map/all_to_all | solution.py:298
  30.0 4.5 %collective-permute-start = (bf16[8,4,128,128]{3,2,1,0:T(8,128)(2,1)}, bf16[8,4,128,128]{3,2,1,0:T(8,128)(2,1)}, u32[]{:S(2)}, u32[]{:S(2)}) collective-permute-start(bf16[8,4,128,128]{3,2,1,0:T(8,128)(2,1)} %copy-done.1), channel_id=1, source_target_pairs={{0,8},{8,16},{16,24},{1,9},{9,17},{17,25},{2,10},{10,18},{18,26},{... | collective-permute-start | bytes 3145736 | tf_op jit(solution)/shard_map/ppermute | solution.py:322
  34.6 2.0 %fusion.16.class_ref = bf16[512,128]{1,0:T(8,128)(2,1)} fusion(s32[512]{0:T(512)S(1)} %get-tuple-element.58, s32[512]{0:T(512)S(1)} %get-tuple-element.64, s32[512]{0:T(512)S(1)} %get-tuple-element.59, s32[512]{0:T(512)S(1)} %get-tuple-element.61, s32[512]{0:T(512)S(1)} %get-tuple-element.60, s32[512]{0:T(512)S(1)} %get-tuple-element.65, ...), kind=kLoop, calls=%fused_computation.40 | loop fusion | flops 3276800 | bytes 144896 | tf_op jit(solution)/shard_map/convert_element_type | solution.py:268
  37.5 23.2 %all-to-all-done.1.q_ref.c_ref.kc_ref.vc_ref = bf16[8,10,128,128]{3,2,1,0:T(8,128)(2,1)S(1)} async-done(((bf16[8,10,128,128]{3,2,1,0:T(8,128)(2,1)}), bf16[8,10,128,128]{3,2,1,0:T(8,128)(2,1)S(1)}, u32[]{:S(2)}, u32[]{:S(2)}) %all-to-all-start.1) | async-done | bytes 2621472 | tf_op jit(solution)/shard_map/all_to_all | solution.py:298
  60.7 4.3 %all-to-all-start.2 = ((bf16[8,6,128,128]{3,2,1,0:T(8,128)(2,1)}), bf16[8,6,128,128]{3,2,1,0:T(8,128)(2,1)}, u32[]{:S(2)}, u32[]{:S(2)}) async-start(bf16[8,6,128,128]{3,2,1,0:T(8,128)(2,1)} %get-tuple-element.35), calls=%async_computation.2 | async-start | bytes 3145728 | tf_op jit(solution)/shard_map/all_to_all | solution.py:298
  66.1 4.5 %collective-permute-start.1 = (bf16[8,4,128,128]{3,2,1,0:T(8,128)(2,1)}, bf16[8,4,128,128]{3,2,1,0:T(8,128)(2,1)}, u32[]{:S(2)}, u32[]{:S(2)}) collective-permute-start(bf16[8,4,128,128]{3,2,1,0:T(8,128)(2,1)} %slice.20), channel_id=1, source_target_pairs={{0,8},{8,16},{16,24},{1,9},{9,17},{17,25},{2,10},{10,18},{18,26},{... | collective-permute-start | bytes 3145736 | tf_op jit(solution)/shard_map/ppermute | solution.py:322
  70.6 15.5 %attention.3 = (bf16[8,4,128,128]{3,2,1,0:T(8,128)(2,1)}, f32[8,4,128,128]{3,2,1,0:T(8,128)}, bf16[8,4,128,128]{3,2,1,0:T(8,128)(2,1)}) custom-call(bf16[2,1536,128]{2,1,0:T(8,128)(2,1)} %bitcast.24, bf16[512,128]{1,0:T(8,128)(2,1)} %fusion.16.class_ref, bf16[8,10,128,128]{3,2,1,0:T(8,128)(2,1)S(1)} %all-to-all-done.1.q_ref.c_ref.kc_ref.vc_ref, ...), custom_call_target="tpu_custom_call" | custom-call | flops 9663676416 | bytes 9437184 | tf_op jit(solution)/shard_map/attention/pallas_call | solution.py:206
  86.1 4.3 %all-to-all-start.3 = ((bf16[8,4,128,128]{3,2,1,0:T(8,128)(2,1)}), bf16[8,4,128,128]{3,2,1,0:T(8,128)(2,1)}, u32[]{:S(2)}, u32[]{:S(2)}) async-start(bf16[8,4,128,128]{3,2,1,0:T(8,128)(2,1)} %get-tuple-element.36), calls=%async_computation.3 | async-start | bytes 2097152 | tf_op jit(solution)/shard_map/all_to_all | solution.py:298
  92.8 4.6 %collective-permute-start.2 = (bf16[8,2,128,128]{3,2,1,0:T(8,128)(2,1)}, bf16[8,2,128,128]{3,2,1,0:T(8,128)(2,1)S(1)}, u32[]{:S(2)}, u32[]{:S(2)}) collective-permute-start(bf16[8,2,128,128]{3,2,1,0:T(8,128)(2,1)} %slice.21), channel_id=1, source_target_pairs={{0,8},{8,16},{16,24},{1,9},{9,17},{17,25},{2,10},{10,18},{18,26},{... | collective-permute-start | bytes 1572872 | tf_op jit(solution)/shard_map/ppermute | solution.py:322
  97.4 15.6 %attention.4 = (bf16[8,4,128,128]{3,2,1,0:T(8,128)(2,1)}, f32[8,4,128,128]{3,2,1,0:T(8,128)}, bf16[8,4,128,128]{3,2,1,0:T(8,128)(2,1)}) custom-call(bf16[2,1536,128]{2,1,0:T(8,128)(2,1)} %bitcast.25, bf16[512,128]{1,0:T(8,128)(2,1)} %fusion.16.class_ref, bf16[8,6,128,128]{3,2,1,0:T(8,128)(2,1)} %all-to-all-done.2.q_ref.c_ref, ...), custom_call_target="tpu_custom_call" | custom-call | flops 9663676416 | bytes 9437184 | tf_op jit(solution)/shard_map/attention/pallas_call | solution.py:206
  114.3 4.5 %all-to-all-start.4 = ((bf16[8,4,128,128]{3,2,1,0:T(8,128)(2,1)}), bf16[8,4,128,128]{3,2,1,0:T(8,128)(2,1)}, u32[]{:S(2)}, u32[]{:S(2)}) async-start(bf16[8,4,128,128]{3,2,1,0:T(8,128)(2,1)} %get-tuple-element.39), calls=%async_computation.4 | async-start | bytes 2097152 | tf_op jit(solution)/shard_map/all_to_all | solution.py:298
  118.8 8.9 %attention.5 = (bf16[8,2,128,128]{3,2,1,0:T(8,128)(2,1)}, f32[8,2,128,128]{3,2,1,0:T(8,128)}, bf16[8,2,128,128]{3,2,1,0:T(8,128)(2,1)}) custom-call(bf16[2,1536,128]{2,1,0:T(8,128)(2,1)} %bitcast.26, bf16[512,128]{1,0:T(8,128)(2,1)} %fusion.16.class_ref, bf16[8,6,128,128]{3,2,1,0:T(8,128)(2,1)} %all-to-all-done.2.q_ref.c_ref, ...), custom_call_target="tpu_custom_call" | custom-call | flops 4831838208 | bytes 4718592 | tf_op jit(solution)/shard_map/attention/pallas_call | solution.py:206
  127.8 1.6 add_convert_fusion.1
  130.7 3.3 %all-to-all-done.4.refs_1_ = bf16[8,4,128,128]{3,2,1,0:T(8,128)(2,1)} async-done(((bf16[8,4,128,128]{3,2,1,0:T(8,128)(2,1)}), bf16[8,4,128,128]{3,2,1,0:T(8,128)(2,1)}, u32[]{:S(2)}, u32[]{:S(2)}) %all-to-all-start.4) | async-done | bytes 1048608 | tf_op jit(solution)/shard_map/all_to_all | solution.py:298
  134.0 3.6 %all-to-all-start.5 = ((bf16[8,6,128,128]{3,2,1,0:T(8,128)(2,1)}), bf16[8,6,128,128]{3,2,1,0:T(8,128)(2,1)S(1)}, u32[]{:S(2)}, u32[]{:S(2)}) async-start(bf16[8,6,128,128]{3,2,1,0:T(8,128)(2,1)} %pad_maximum_fusion), calls=%async_computation.5 | async-start | bytes 3145728 | tf_op jit(solution)/shard_map/all_to_all | solution.py:298
  139.0 15.7 %collective-permute-done.5 = bf16[8,2,128,128]{3,2,1,0:T(8,128)(2,1)S(1)} collective-permute-done((bf16[8,2,128,128]{3,2,1,0:T(8,128)(2,1)S(1)}, bf16[8,2,128,128]{3,2,1,0:T(8,128)(2,1)S(1)}, u32[]{:S(2)}, u32[]{:S(2)}) %collective-permute-start.5) | collective-permute-done | bytes 524320 | tf_op jit(solution)/shard_map/ppermute | solution.py:330
  158.5 3.6 %all-to-all-start.6 = ((bf16[8,6,128,128]{3,2,1,0:T(8,128)(2,1)}), bf16[8,6,128,128]{3,2,1,0:T(8,128)(2,1)S(1)}, u32[]{:S(2)}, u32[]{:S(2)}) async-start(bf16[8,6,128,128]{3,2,1,0:T(8,128)(2,1)} %pad_maximum_fusion.1), calls=%async_computation.6 | async-start | bytes 3145728 | tf_op jit(solution)/shard_map/all_to_all | solution.py:298
  162.1 2.9 %unpack.2 = (bf16[128,5120]{1,0:T(8,128)(2,1)}, bf16[128,5120]{1,0:T(8,128)(2,1)}) custom-call(bf16[8,4,128,128]{3,2,1,0:T(8,128)(2,1)} %all-to-all-done.3.refs_0_, bf16[8,4,128,128]{3,2,1,0:T(8,128)(2,1)} %all-to-all-done.4.refs_1_, bf16[8,6,128,128]{3,2,1,0:T(8,128)(2,1)S(1)} %all-to-all-done.5.refs_2_.refs_0_), custom_call_target="tpu_custom_call" | custom-call | bytes 5242880 | tf_op jit(solution)/shard_map/unpack/pallas_call | solution.py:80
  165.1 18.0 %all-to-all-done.6.refs_1_ = bf16[8,6,128,128]{3,2,1,0:T(8,128)(2,1)S(1)} async-done(((bf16[8,6,128,128]{3,2,1,0:T(8,128)(2,1)}), bf16[8,6,128,128]{3,2,1,0:T(8,128)(2,1)S(1)}, u32[]{:S(2)}, u32[]{:S(2)}) %all-to-all-start.6) | async-done | bytes 1572896 | tf_op jit(solution)/shard_map/all_to_all | solution.py:298
  183.1 1.7 unpack.3
  (66 shorter events, 15.0 us)
Async XLA Ops:
  0.6 28.1 %copy-start = (s32[8,2,2,10]{3,2,1,0:T(2,128)S(1)}, s32[8,2,2,10]{3,2,1,0:T(2,128)}, u32[]{:S(2)}) copy-start(s32[8,2,2,10]{3,2,1,0:T(2,128)} %param.11) | copy-start | bytes 3844
  3.2 5.3 %copy-start.7 = (s32[16]{0:T(128)S(1)}, s32[16]{0:T(128)}, u32[]{:S(2)}) copy-start(s32[16]{0:T(128)} %param.10) | copy-start | bytes 196
  3.2 20.7 %all-to-all-start = ((bf16[8,4,128,128]{3,2,1,0:T(8,128)(2,1)}), bf16[8,4,128,128]{3,2,1,0:T(8,128)(2,1)S(1)}, u32[]{:S(2)}, u32[]{:S(2)}) async-start(bf16[8,4,128,128]{3,2,1,0:T(8,128)(2,1)} %pack.3), calls=%async_computation | async-start | bytes 2097152 | tf_op jit(solution)/shard_map/all_to_all | solution.py:298
  23.9 1.0 copy-start.1
  24.9 35.8 %all-to-all-start.1 = ((bf16[8,10,128,128]{3,2,1,0:T(8,128)(2,1)}), bf16[8,10,128,128]{3,2,1,0:T(8,128)(2,1)S(1)}, u32[]{:S(2)}, u32[]{:S(2)}) async-start(bf16[8,10,128,128]{3,2,1,0:T(8,128)(2,1)} %get-tuple-element.31), calls=%async_computation.1 | async-start | bytes 5242880 | tf_op jit(solution)/shard_map/all_to_all | solution.py:298
  30.0 36.1 %collective-permute-start = (bf16[8,4,128,128]{3,2,1,0:T(8,128)(2,1)}, bf16[8,4,128,128]{3,2,1,0:T(8,128)(2,1)}, u32[]{:S(2)}, u32[]{:S(2)}) collective-permute-start(bf16[8,4,128,128]{3,2,1,0:T(8,128)(2,1)} %copy-done.1), channel_id=1, source_target_pairs={{0,8},{8,16},{16,24},{1,9},{9,17},{17,25},{2,10},{10,18},{18,26},{... | collective-permute-start | bytes 3145736 | tf_op jit(solution)/shard_map/ppermute | solution.py:322
  60.7 25.3 %all-to-all-start.2 = ((bf16[8,6,128,128]{3,2,1,0:T(8,128)(2,1)}), bf16[8,6,128,128]{3,2,1,0:T(8,128)(2,1)}, u32[]{:S(2)}, u32[]{:S(2)}) async-start(bf16[8,6,128,128]{3,2,1,0:T(8,128)(2,1)} %get-tuple-element.35), calls=%async_computation.2 | async-start | bytes 3145728 | tf_op jit(solution)/shard_map/all_to_all | solution.py:298
  65.0 5.6 %copy-start.2 = (bf16[8,4,128,128]{3,2,1,0:T(8,128)(2,1)S(1)}, bf16[8,4,128,128]{3,2,1,0:T(8,128)(2,1)}, u32[]{:S(2)}) copy-start(bf16[8,4,128,128]{3,2,1,0:T(8,128)(2,1)} %copy-done.1) | copy-start | bytes 3145732
  66.1 26.7 %collective-permute-start.1 = (bf16[8,4,128,128]{3,2,1,0:T(8,128)(2,1)}, bf16[8,4,128,128]{3,2,1,0:T(8,128)(2,1)}, u32[]{:S(2)}, u32[]{:S(2)}) collective-permute-start(bf16[8,4,128,128]{3,2,1,0:T(8,128)(2,1)} %slice.20), channel_id=1, source_target_pairs={{0,8},{8,16},{16,24},{1,9},{9,17},{17,25},{2,10},{10,18},{18,26},{... | collective-permute-start | bytes 3145736 | tf_op jit(solution)/shard_map/ppermute | solution.py:322
  86.1 28.2 %all-to-all-start.3 = ((bf16[8,4,128,128]{3,2,1,0:T(8,128)(2,1)}), bf16[8,4,128,128]{3,2,1,0:T(8,128)(2,1)}, u32[]{:S(2)}, u32[]{:S(2)}) async-start(bf16[8,4,128,128]{3,2,1,0:T(8,128)(2,1)} %get-tuple-element.36), calls=%async_computation.3 | async-start | bytes 2097152 | tf_op jit(solution)/shard_map/all_to_all | solution.py:298
  90.3 37.4 %collective-permute-start.3 = (bf16[8,4,128,128]{3,2,1,0:T(8,128)(2,1)}, bf16[8,4,128,128]{3,2,1,0:T(8,128)(2,1)}, u32[]{:S(2)}, u32[]{:S(2)}) collective-permute-start(bf16[8,4,128,128]{3,2,1,0:T(8,128)(2,1)} %get-tuple-element.43), channel_id=1, source_target_pairs={{8,0},{16,8},{24,16},{9,1},{17,9},{25,17},{10,2},{18,10},{26,18},{... | collective-permute-start | bytes 3145736 | tf_op jit(solution)/shard_map/ppermute | solution.py:330
  92.8 26.0 %collective-permute-start.2 = (bf16[8,2,128,128]{3,2,1,0:T(8,128)(2,1)}, bf16[8,2,128,128]{3,2,1,0:T(8,128)(2,1)S(1)}, u32[]{:S(2)}, u32[]{:S(2)}) collective-permute-start(bf16[8,2,128,128]{3,2,1,0:T(8,128)(2,1)} %slice.21), channel_id=1, source_target_pairs={{0,8},{8,16},{16,24},{1,9},{9,17},{17,25},{2,10},{10,18},{18,26},{... | collective-permute-start | bytes 1572872 | tf_op jit(solution)/shard_map/ppermute | solution.py:322
  113.0 41.9 %collective-permute-start.4 = (bf16[8,4,128,128]{3,2,1,0:T(8,128)(2,1)}, bf16[8,4,128,128]{3,2,1,0:T(8,128)(2,1)}, u32[]{:S(2)}, u32[]{:S(2)}) collective-permute-start(bf16[8,4,128,128]{3,2,1,0:T(8,128)(2,1)} %get-tuple-element.50), channel_id=1, source_target_pairs={{8,0},{16,8},{24,16},{9,1},{17,9},{25,17},{10,2},{18,10},{26,18},{... | collective-permute-start | bytes 3145736 | tf_op jit(solution)/shard_map/ppermute | solution.py:330
  114.3 19.7 %all-to-all-start.4 = ((bf16[8,4,128,128]{3,2,1,0:T(8,128)(2,1)}), bf16[8,4,128,128]{3,2,1,0:T(8,128)(2,1)}, u32[]{:S(2)}, u32[]{:S(2)}) async-start(bf16[8,4,128,128]{3,2,1,0:T(8,128)(2,1)} %get-tuple-element.39), calls=%async_computation.4 | async-start | bytes 2097152 | tf_op jit(solution)/shard_map/all_to_all | solution.py:298
  118.8 9.0 %copy-start.4 = (f32[8,4,128,128]{3,2,1,0:T(8,128)S(1)}, f32[8,4,128,128]{3,2,1,0:T(8,128)}, u32[]{:S(2)}) copy-start(f32[8,4,128,128]{3,2,1,0:T(8,128)} %get-tuple-element.42) | copy-start | bytes 6291460
  127.8 1.6 copy-start.6
  130.7 6.9 %copy-start.8 = (bf16[8,2,128,128]{3,2,1,0:T(8,128)(2,1)S(1)}, bf16[8,2,128,128]{3,2,1,0:T(8,128)(2,1)}, u32[]{:S(2)}) copy-start(bf16[8,2,128,128]{3,2,1,0:T(8,128)(2,1)} %get-tuple-element.52) | copy-start | bytes 1572868
  130.7 24.1 %copy-start.5 = (f32[8,2,128,128]{3,2,1,0:T(8,128)S(1)}, f32[8,2,128,128]{3,2,1,0:T(8,128)}, u32[]{:S(2)}) copy-start(f32[8,2,128,128]{3,2,1,0:T(8,128)} %get-tuple-element.44) | copy-start | bytes 3145732
  134.0 24.5 %all-to-all-start.5 = ((bf16[8,6,128,128]{3,2,1,0:T(8,128)(2,1)}), bf16[8,6,128,128]{3,2,1,0:T(8,128)(2,1)S(1)}, u32[]{:S(2)}, u32[]{:S(2)}) async-start(bf16[8,6,128,128]{3,2,1,0:T(8,128)(2,1)} %pad_maximum_fusion), calls=%async_computation.5 | async-start | bytes 3145728 | tf_op jit(solution)/shard_map/all_to_all | solution.py:298
  137.6 17.3 %copy-start.3 = (f32[8,4,128,128]{3,2,1,0:T(8,128)S(1)}, f32[8,4,128,128]{3,2,1,0:T(8,128)}, u32[]{:S(2)}) copy-start(f32[8,4,128,128]{3,2,1,0:T(8,128)} %get-tuple-element.49) | copy-start | bytes 6291460
  137.6 17.1 %collective-permute-start.5 = (bf16[8,2,128,128]{3,2,1,0:T(8,128)(2,1)S(1)}, bf16[8,2,128,128]{3,2,1,0:T(8,128)(2,1)S(1)}, u32[]{:S(2)}, u32[]{:S(2)}) collective-permute-start(bf16[8,2,128,128]{3,2,1,0:T(8,128)(2,1)S(1)} %copy-done.8), channel_id=1, source_target_pairs={{8,0},{16,8},{24,16},{9,1},{17,9},{25,17},{10,2},{18,10},{26,18},{... | collective-permute-start | bytes 1572872 | tf_op jit(solution)/shard_map/ppermute | solution.py:330
  158.5 24.5 %all-to-all-start.6 = ((bf16[8,6,128,128]{3,2,1,0:T(8,128)(2,1)}), bf16[8,6,128,128]{3,2,1,0:T(8,128)(2,1)S(1)}, u32[]{:S(2)}, u32[]{:S(2)}) async-start(bf16[8,6,128,128]{3,2,1,0:T(8,128)(2,1)} %pad_maximum_fusion.1), calls=%async_computation.6 | async-start | bytes 3145728 | tf_op jit(solution)/shard_map/all_to_all | solution.py:298

commit v7 on v6

--- a/solution.py
+++ b/solution.py
@@ -17,8 +17,15 @@
 K_NB = 10
 MASKED = -1e30
 CHUNKS = (2, 2, 1)
-INWARD = ((("kv", 0),), (("kv", 1), ("qc", 0), ("kv", 2)), (("qc", 1), ("qc", 2)))
-OUTWARD = ((("o", 0),), (("o", 1),), (("o", 2), ("d", 0)), (("d", 1), ("d", 2)))
+ORDER = (
+    (("kv", 0),),
+    (("kv", 1), ("qc", 0)),
+    (("kv", 2), ("qc", 1)),
+    (("qc", 2), ("o", 0)),
+    (("o", 1),),
+    (("o", 2), ("d", 0)),
+    (("d", 1), ("d", 2)),
+)
 VMEM_LIMIT = 32 * 1024 * 1024
 
 
@@ -125,8 +132,8 @@
 
     def scores(j, t):
         y, piece = blocks[j]
-        q, c = queries_of(j)
-        s = lax.dot_general(
+        q, _ = queries_of(j)
+        return lax.dot_general(
             jnp.concatenate([q, class_ref[piece * block : (piece + 1) * block]], axis=1),
             jnp.concatenate(
                 [k_all[keys_of(j, t)], bias_ref[y, t * tile : (t + 1) * tile]], axis=1
@@ -134,10 +141,6 @@
             nt,
             preferred_element_type=jnp.float32,
         )
-        dp = lax.dot_general(
-            c, v_all[keys_of(j, t)], nt, preferred_element_type=jnp.float32
-        )
-        return s, dp
 
     def key_grads(j, t, w, ds):
         q, c = queries_of(j)
@@ -151,31 +154,39 @@
             dk_all[keys] += dk
             dv_all[keys] += dv
 
-    ready = [scores(0, t) for t in tiles]
+    ready, top = [], None
+    for t in tiles:
+        ready.append(scores(0, t))
+        top = ready[t] if top is None else jnp.maximum(top, ready[t])
     owed = None
     for j, (y, piece) in enumerate(blocks):
         window = slice(y * slab, (y + 3) * slab)
         here = pl.ds(y * half + piece * (half // 2), half // 2)
         _, c = queries_of(j)
-        m = functools.reduce(jnp.maximum, [s for s, _ in ready])
-        m = jnp.max(m, axis=1, keepdims=True)
-        coming, e = [], []
+        m = jnp.max(top, axis=1, keepdims=True)
+        coming, e, top, total = [], [], None, None
         for t in tiles:
             if j + 1 < len(blocks):
                 coming.append(scores(j + 1, t))
-            e.append(jnp.exp2((ready[t][0] - m) * scale2))
-        r = 1.0 / jnp.sum(functools.reduce(jnp.add, e), axis=1, keepdims=True)
-        p, w = [], []
+                top = coming[t] if top is None else jnp.maximum(top, coming[t])
+            e.append(jnp.exp2((ready[t] - m) * scale2))
+            total = e[t] if total is None else total + e[t]
+        r = 1.0 / jnp.sum(total, axis=1, keepdims=True)
+        w = []
         for t in tiles:
             if owed is not None:
                 key_grads(j - 1, t, owed[0][t], owed[1][t])
-            p.append(e[t] * r)
-            w.append(p[t].astype(jnp.bfloat16))
+            w.append((e[t] * r).astype(jnp.bfloat16))
         o = jnp.dot(
             jnp.concatenate(w, axis=1), v_all[window], preferred_element_type=jnp.float32
         ).astype(jnp.bfloat16)
         delta = jnp.sum(c.astype(jnp.float32) * o.astype(jnp.float32), axis=1, keepdims=True)
-        ds = [(p[t] * (ready[t][1] - delta)).astype(jnp.bfloat16) for t in tiles]
+        ds = []
+        for t in tiles:
+            dp = lax.dot_general(
+                c, v_all[keys_of(j, t)], nt, preferred_element_type=jnp.float32
+            )
+            ds.append((e[t] * r * (dp - delta)).astype(jnp.bfloat16))
         dq = jnp.dot(
             jnp.concatenate(ds, axis=1), k_all[window], preferred_element_type=jnp.float32
         )
@@ -282,67 +293,72 @@
     down = [(i + 1, i) for i in range(planes - 1)]
 
     if sum(CHUNKS) == heads:
-        counts, inward, outward = CHUNKS, INWARD, OUTWARD
+        counts, order = CHUNKS, ORDER
     else:
         counts = (heads,)
-        inward, outward = ((("kv", 0),), (("qc", 0),)), ((("o", 0),), (("d", 0),))
+        order = ((("kv", 0),), (("qc", 0),), (("o", 0),), (("d", 0),))
     firsts = [sum(counts[:i]) for i in range(len(counts))]
-    last = []
+    arrived, place, shifted, owed, made = [], {}, [], [], {}
 
     def after(array, other):
         return lax.optimization_barrier((array, other))[0]
 
-    def exchange(array):
-        if last:
-            array = after(array, last[-1])
-        last.append(lax.all_to_all(array, group, split_axis=0, concat_axis=0, tiled=True))
-        return last[-1]
-
     def layout(items):
         return [(name, firsts[i] + h) for name, i in items for h in range(counts[i])]
 
+    def work_on(i):
+        odq, dkv, dkv_prev = attention(
+            bias, classes, counts[i], place["qc", i], place["kv", i], (shifted[i], 0)
+        )
+        made["o", i] = odq
+        owed.append((dkv, lax.ppermute(dkv_prev, "plane", down)))
+
+    def returned(i):
+        dkv, dkv_next = owed[i]
+        if i + 1 < len(owed):
+            dkv_next = after(dkv_next, owed[-1][0])
+        return (dkv + dkv_next.astype(jnp.float32)).astype(jnp.bfloat16)
+
     pairs = {"kv": (k, v), "qc": (q, c)}
+    inward = [[item for item in items if item[0] in pairs] for items in order]
     sent = pack(pairs, members, heads, [layout(inward[0])])
-    sent += pack(pairs, members, heads, [layout(items) for items in inward[1:]])
+    sent += pack(pairs, members, heads, [layout(items) for items in inward[1:] if items])
     bias, classes = mask_operands(
         frame_blocks, tile_lists, z, bands, queries.shape[1] * bands, queries.shape[2]
     )
-    place, shifted = {}, []
-    for items, buffer in zip(inward, sent):
-        if items is inward[-1]:
+    for step, items in enumerate(order):
+        parts = [sent[step]] if inward[step] else []
+        for name, i in items[len(inward[step]) :]:
+            if name == "o":
+                while ("o", i) not in made:
+                    work_on(len(owed))
+                parts.append(made["o", i])
+            else:
+                parts.append(returned(i))
+        buffer = jnp.concatenate(parts, axis=1) if len(parts) > 1 else parts[0]
+        if step == 2:
             buffer = after(buffer, (bias, classes))
-        buffer = exchange(buffer)
+        if arrived:
+            buffer = after(buffer, arrived[-1])
+        buffer = lax.all_to_all(buffer, group, split_axis=0, concat_axis=0, tiled=True)
+        arrived.append(buffer)
         slot = 0
         for name, i in items:
             place[name, i] = (buffer, slot)
             if name == "kv":
                 moved = buffer[:, slot : slot + 2 * counts[i]]
-                if shifted:
-                    moved = after(moved, shifted[-1])
                 shifted.append(lax.ppermute(moved, "plane", up))
             slot += 2 * counts[i]
-    made, owed = {}, []
-    for i, count in enumerate(counts):
-        odq, dkv, dkv_prev = attention(
-            bias, classes, count, place["qc", i], place["kv", i], (shifted[i], 0)
-        )
-        made["o", i] = odq
-        owed.append((dkv, lax.ppermute(dkv_prev, "plane", down)))
-    for i, (dkv, dkv_next) in enumerate(owed):
-        if i + 1 < len(owed):
-            dkv_next = after(dkv_next, owed[-1][0])
-        made["d", i] = (dkv + dkv_next.astype(jnp.float32)).astype(jnp.bfloat16)
-    back, found = [], {}
-    for items in outward:
-        parts = [made[item] for item in items]
-        back.append(exchange(jnp.concatenate(parts, axis=1) if len(parts) > 1 else parts[0]))
-        for slot, (name, head) in enumerate(layout(items)):
-            found[name, head] = (len(back) - 1, 2 * slot)
     outputs = []
     for name in ("o", "d"):
-        used = sorted({found[name, head][0] for head in range(heads)})
-        places = [(used.index(found[name, h][0]), found[name, h][1]) for h in range(heads)]
-        outputs += unpack([back[i] for i in used], places, members, heads)
+        used, places = [], []
+        for i, count in enumerate(counts):
+            buffer, slot = place[name, i]
+            if not any(buffer is other for other in used):
+                used.append(buffer)
+            index = [buffer is other for other in used].index(True)
+            places += [(index, slot + 2 * h) for h in range(count)]
+        outputs += unpack(used, places, members, heads)
     return tuple(array.reshape(queries.shape) for array in outputs)
 
 

time: 187 us -> 183 us (0.979)
  waiting for transfers between devices: 72.4 us -> 65 us
  local copies, waits for them, and re-layouts: 4.63 us -> 9.95 us
  Pallas kernels: 51.4 us -> 47.1 us
  other arithmetic: 8.77 us -> 12.1 us
    all_to_all x7, waiting for transfers between devices: 56.3 us -> 51.6 us  [on_device(): lax.all_to_all(buffer, group, split_axis=0, concat_axis=0, tiled=True)]
    unnamed x18 -> x26, local copies, waits for them, and re-layouts: 1.01 us -> 5.22 us
    pallas_call x3, Pallas kernels: 40 us -> 37 us  [attention(): pl.pallas_call(attention_body, grid=(count,), out_shape=[hbm(shape, jnp.b...]
    concatenate x2 -> x3, other arithmetic: 2.62 us -> 5.21 us  [on_device(): buffer = jnp.concatenate(parts, axis=1) if len(parts) > 1 else parts[0]]
    ppermute x3, waiting for transfers between devices: 15.7 us -> 13.4 us  [work_on(): owed.append((dkv, lax.ppermute(dkv_prev, 'plane', down)))]
  transfers between devices with their start and end apart: 13 -> 13, of which waited for: 7 -> 7; matrix products, arithmetic and copies ran while one was open for 7% -> 9% of each run, Pallas kernels for 25% -> 24%
where the time goes in v7:
time: 183 us; the launch traced here: 182 us
  waiting for transfers between devices  65 us (36%)
  Pallas kernels  47.1 us (26%)
  starting transfers between devices  46.5 us (25%)
  other arithmetic  12.1 us (7%)
  local copies, waits for them, and re-layouts  9.95 us (5%)
    all_to_all x7, waiting for transfers between devices, on_device(): lax.all_to_all(buffer, group, split_axis=0, concat_axis=0, tiled=True)  51.6 us
    pallas_call x3, Pallas kernels, attention(): pl.pallas_call(attention_body, grid=(count,), out_shape=[hbm(shape, jnp.b...  37 us
    all_to_all x7, starting transfers between devices, on_device(): lax.all_to_all(buffer, group, split_axis=0, concat_axis=0, tiled=True)  28.7 us
    ppermute x3, starting transfers between devices, on_device(): shifted.append(lax.ppermute(moved, 'plane', up))  13.9 us
    ppermute x3, waiting for transfers between devices, work_on(): owed.append((dkv, lax.ppermute(dkv_prev, 'plane', down)))  13.4 us
    pallas_call x2, Pallas kernels, pack(): pl.pallas_call(body, grid=(STEPS,), out_shape=[hbm((members, *shape), arr...  6.73 us
    unnamed x26, local copies, waits for them, and re-layouts  5.22 us
    concatenate x3, other arithmetic, on_device(): buffer = jnp.concatenate(parts, axis=1) if len(parts) > 1 else parts[0]  5.21 us
  transfers between devices with their start and end apart: 13, of which 7 were waited for; matrix products, arithmetic and copies ran while one was open for 9% of the time, Pallas kernels for 24%

profile of v7, /device:TPU:0, one launch (start us, length us, event | category | flops | bytes accessed | tf_op | source)
XLA Modules:
  0.0 181.6 jit_solution(11469581519479421018)
XLA Ops:
  0.6 2.6 %pack.3 = bf16[8,4,128,128]{3,2,1,0:T(8,128)(2,1)} custom-call(bf16[128,5120]{1,0:T(8,128)(2,1)} %bitcast.18, bf16[128,5120]{1,0:T(8,128)(2,1)} %bitcast.20), custom_call_target="tpu_custom_call" | custom-call | bytes 5242880 | tf_op jit(solution)/shard_map/pack/pallas_call | solution.py:60
  3.2 5.3 %all-to-all-start = ((bf16[8,4,128,128]{3,2,1,0:T(8,128)(2,1)}), bf16[8,4,128,128]{3,2,1,0:T(8,128)(2,1)S(1)}, u32[]{:S(2)}, u32[]{:S(2)}) async-start(bf16[8,4,128,128]{3,2,1,0:T(8,128)(2,1)} %pack.3), calls=%async_computation | async-start | bytes 2097152 | tf_op jit(solution)/shard_map/all_to_all | solution.py:343
  8.8 4.1 %pack.2 = (bf16[8,8,128,128]{3,2,1,0:T(8,128)(2,1)}, bf16[8,6,128,128]{3,2,1,0:T(8,128)(2,1)}, bf16[8,2,128,128]{3,2,1,0:T(8,128)(2,1)}) custom-call(bf16[128,5120]{1,0:T(8,128)(2,1)} %bitcast.19, bf16[128,5120]{1,0:T(8,128)(2,1)} %bitcast.21, bf16[128,5120]{1,0:T(8,128)(2,1)} %bitcast.22, bf16[128,5120]{1,0:T(8,128)(2,1)} %bitcast.23), custom_call_target="tpu_custom_call" | custom-call | bytes 10485760 | tf_op jit(solution)/shard_map/pack/pallas_call | solution.py:60
  13.1 10.8 %all-to-all-done.kc_ref.vc_ref = bf16[8,4,128,128]{3,2,1,0:T(8,128)(2,1)S(1)} async-done(((bf16[8,4,128,128]{3,2,1,0:T(8,128)(2,1)}), bf16[8,4,128,128]{3,2,1,0:T(8,128)(2,1)S(1)}, u32[]{:S(2)}, u32[]{:S(2)}) %all-to-all-start) | async-done | bytes 1048608 | tf_op jit(solution)/shard_map/all_to_all | solution.py:343
  23.9 3.6 %all-to-all-start.1 = ((bf16[8,8,128,128]{3,2,1,0:T(8,128)(2,1)}), bf16[8,8,128,128]{3,2,1,0:T(8,128)(2,1)S(1)}, u32[]{:S(2)}, u32[]{:S(2)}) async-start(bf16[8,8,128,128]{3,2,1,0:T(8,128)(2,1)} %get-tuple-element.31), calls=%async_computation.1 | async-start | bytes 4194304 | tf_op jit(solution)/shard_map/all_to_all | solution.py:343
  28.9 4.6 %collective-permute-start = (bf16[8,4,128,128]{3,2,1,0:T(8,128)(2,1)S(1)}, bf16[8,4,128,128]{3,2,1,0:T(8,128)(2,1)}, u32[]{:S(2)}, u32[]{:S(2)}) collective-permute-start(bf16[8,4,128,128]{3,2,1,0:T(8,128)(2,1)S(1)} %all-to-all-done.kc_ref.vc_ref), channel_id=1, source_target_pairs={{0,8},{8,16},{16,24},{1,9},{9,17},{17,25},{2,10},{10,18},{18,26},{... | collective-permute-start | bytes 3145736 | tf_op jit(solution)/shard_map/ppermute | solution.py:350
  33.6 2.0 %fusion.16.class_ref = bf16[512,128]{1,0:T(8,128)(2,1)} fusion(s32[512]{0:T(512)S(1)} %get-tuple-element.56, s32[512]{0:T(512)S(1)} %get-tuple-element.62, s32[512]{0:T(512)S(1)} %get-tuple-element.57, s32[512]{0:T(512)S(1)} %get-tuple-element.59, s32[512]{0:T(512)S(1)} %get-tuple-element.58, s32[512]{0:T(512)S(1)} %get-tuple-element.63, ...), kind=kLoop, calls=%fused_computation.41 | loop fusion | flops 3276800 | bytes 144896 | tf_op jit(solution)/shard_map/convert_element_type | solution.py:279
  36.5 17.6 %all-to-all-done.1.q_ref.c_ref.kc_ref.vc_ref = bf16[8,8,128,128]{3,2,1,0:T(8,128)(2,1)S(1)} async-done(((bf16[8,8,128,128]{3,2,1,0:T(8,128)(2,1)}), bf16[8,8,128,128]{3,2,1,0:T(8,128)(2,1)S(1)}, u32[]{:S(2)}, u32[]{:S(2)}) %all-to-all-start.1) | async-done | bytes 2097184 | tf_op jit(solution)/shard_map/all_to_all | solution.py:343
  54.1 4.3 %all-to-all-start.2 = ((bf16[8,6,128,128]{3,2,1,0:T(8,128)(2,1)}), bf16[8,6,128,128]{3,2,1,0:T(8,128)(2,1)}, u32[]{:S(2)}, u32[]{:S(2)}) async-start(bf16[8,6,128,128]{3,2,1,0:T(8,128)(2,1)} %get-tuple-element.35), calls=%async_computation.2 | async-start | bytes 3145728 | tf_op jit(solution)/shard_map/all_to_all | solution.py:343
  59.5 4.6 %collective-permute-start.1 = (bf16[8,4,128,128]{3,2,1,0:T(8,128)(2,1)}, bf16[8,4,128,128]{3,2,1,0:T(8,128)(2,1)}, u32[]{:S(2)}, u32[]{:S(2)}) collective-permute-start(bf16[8,4,128,128]{3,2,1,0:T(8,128)(2,1)} %slice.20), channel_id=1, source_target_pairs={{0,8},{8,16},{16,24},{1,9},{9,17},{17,25},{2,10},{10,18},{18,26},{... | collective-permute-start | bytes 3145736 | tf_op jit(solution)/shard_map/ppermute | solution.py:350
  64.1 14.3 %attention.3 = (bf16[8,4,128,128]{3,2,1,0:T(8,128)(2,1)}, f32[8,4,128,128]{3,2,1,0:T(8,128)}, bf16[8,4,128,128]{3,2,1,0:T(8,128)(2,1)}) custom-call(bf16[2,1536,128]{2,1,0:T(8,128)(2,1)} %bitcast.24, bf16[512,128]{1,0:T(8,128)(2,1)} %fusion.16.class_ref, bf16[8,8,128,128]{3,2,1,0:T(8,128)(2,1)S(1)} %all-to-all-done.1.q_ref.c_ref.kc_ref.vc_ref, ...), custom_call_target="tpu_custom_call" | custom-call | flops 9663676416 | bytes 9437184 | tf_op jit(solution)/shard_map/attention/pallas_call | solution.py:217
  78.4 2.6 %pad_maximum_fusion = bf16[8,6,128,128]{3,2,1,0:T(8,128)(2,1)} fusion(bf16[8,4,128,128]{3,2,1,0:T(8,128)(2,1)} %get-tuple-element.32, bf16[8,2,128,128]{3,2,1,0:T(8,128)(2,1)S(1)} %copy-done.9), kind=kLoop, calls=%fused_computation.2 | loop fusion | flops 786432 | bytes 3145728 | tf_op jit(solution)/shard_map/concatenate | solution.py:338
  81.0 4.1 %all-to-all-start.3 = ((bf16[8,6,128,128]{3,2,1,0:T(8,128)(2,1)}), bf16[8,6,128,128]{3,2,1,0:T(8,128)(2,1)S(1)}, u32[]{:S(2)}, u32[]{:S(2)}) async-start(bf16[8,6,128,128]{3,2,1,0:T(8,128)(2,1)} %pad_maximum_fusion), calls=%async_computation.3 | async-start | bytes 3145728 | tf_op jit(solution)/shard_map/all_to_all | solution.py:343
  88.3 4.7 %collective-permute-start.2 = (bf16[8,2,128,128]{3,2,1,0:T(8,128)(2,1)}, bf16[8,2,128,128]{3,2,1,0:T(8,128)(2,1)S(1)}, u32[]{:S(2)}, u32[]{:S(2)}) collective-permute-start(bf16[8,2,128,128]{3,2,1,0:T(8,128)(2,1)} %slice.21), channel_id=1, source_target_pairs={{0,8},{8,16},{16,24},{1,9},{9,17},{17,25},{2,10},{10,18},{18,26},{... | collective-permute-start | bytes 1572872 | tf_op jit(solution)/shard_map/ppermute | solution.py:350
  94.6 14.3 %attention.4 = (bf16[8,4,128,128]{3,2,1,0:T(8,128)(2,1)}, f32[8,4,128,128]{3,2,1,0:T(8,128)}, bf16[8,4,128,128]{3,2,1,0:T(8,128)(2,1)}) custom-call(bf16[2,1536,128]{2,1,0:T(8,128)(2,1)} %bitcast.25, bf16[512,128]{1,0:T(8,128)(2,1)} %fusion.16.class_ref, bf16[8,6,128,128]{3,2,1,0:T(8,128)(2,1)} %all-to-all-done.2.q_ref.c_ref.kc_ref.vc_ref, ...), custom_call_target="tpu_custom_call" | custom-call | flops 9663676416 | bytes 9437184 | tf_op jit(solution)/shard_map/attention/pallas_call | solution.py:217
  110.2 4.2 %all-to-all-start.4 = ((bf16[8,4,128,128]{3,2,1,0:T(8,128)(2,1)}), bf16[8,4,128,128]{3,2,1,0:T(8,128)(2,1)S(1)}, u32[]{:S(2)}, u32[]{:S(2)}) async-start(bf16[8,4,128,128]{3,2,1,0:T(8,128)(2,1)} %get-tuple-element.38), calls=%async_computation.4 | async-start | bytes 2097152 | tf_op jit(solution)/shard_map/all_to_all | solution.py:343
  114.5 8.4 %attention.5 = (bf16[8,2,128,128]{3,2,1,0:T(8,128)(2,1)}, f32[8,2,128,128]{3,2,1,0:T(8,128)}, bf16[8,2,128,128]{3,2,1,0:T(8,128)(2,1)}) custom-call(bf16[2,1536,128]{2,1,0:T(8,128)(2,1)} %bitcast.26, bf16[512,128]{1,0:T(8,128)(2,1)} %fusion.16.class_ref, bf16[8,6,128,128]{3,2,1,0:T(8,128)(2,1)S(1)} %all-to-all-done.3.q_ref.c_ref.refs_0_, ...), custom_call_target="tpu_custom_call" | custom-call | flops 4831838208 | bytes 4718592 | tf_op jit(solution)/shard_map/attention/pallas_call | solution.py:217
  125.8 4.1 %all-to-all-done.4.refs_1_ = bf16[8,4,128,128]{3,2,1,0:T(8,128)(2,1)S(1)} async-done(((bf16[8,4,128,128]{3,2,1,0:T(8,128)(2,1)}), bf16[8,4,128,128]{3,2,1,0:T(8,128)(2,1)S(1)}, u32[]{:S(2)}, u32[]{:S(2)}) %all-to-all-start.4) | async-done | bytes 1048608 | tf_op jit(solution)/shard_map/all_to_all | solution.py:343
  130.8 3.6 %all-to-all-start.5 = ((bf16[8,6,128,128]{3,2,1,0:T(8,128)(2,1)}), bf16[8,6,128,128]{3,2,1,0:T(8,128)(2,1)S(1)}, u32[]{:S(2)}, u32[]{:S(2)}) async-start(bf16[8,6,128,128]{3,2,1,0:T(8,128)(2,1)} %pad_maximum_fusion.1), calls=%async_computation.5 | async-start | bytes 3145728 | tf_op jit(solution)/shard_map/all_to_all | solution.py:343
  136.2 2.3 %add_convert_fusion = bf16[8,4,128,128]{3,2,1,0:T(8,128)(2,1)S(1)} fusion(f32[8,4,128,128]{3,2,1,0:T(8,128)} %get-tuple-element.47, bf16[8,4,128,128]{3,2,1,0:T(8,128)(2,1)} %collective-permute-done.4), kind=kLoop, calls=%fused_computation | loop fusion | flops 1572864 | bytes 4194304 | tf_op jit(solution)/shard_map/convert_element_type | solution.py:320
  138.4 13.0 %collective-permute-done.5 = bf16[8,2,128,128]{3,2,1,0:T(8,128)(2,1)S(1)} collective-permute-done((bf16[8,2,128,128]{3,2,1,0:T(8,128)(2,1)S(1)}, bf16[8,2,128,128]{3,2,1,0:T(8,128)(2,1)S(1)}, u32[]{:S(2)}, u32[]{:S(2)}) %collective-permute-start.5) | collective-permute-done | bytes 524320 | tf_op jit(solution)/shard_map/ppermute | solution.py:314
  152.9 2.5 %all-to-all-done.5.refs_2_.refs_0_ = bf16[8,6,128,128]{3,2,1,0:T(8,128)(2,1)S(1)} async-done(((bf16[8,6,128,128]{3,2,1,0:T(8,128)(2,1)}), bf16[8,6,128,128]{3,2,1,0:T(8,128)(2,1)S(1)}, u32[]{:S(2)}, u32[]{:S(2)}) %all-to-all-start.5) | async-done | bytes 1572896 | tf_op jit(solution)/shard_map/all_to_all | solution.py:343
  155.4 3.6 %all-to-all-start.6 = ((bf16[8,6,128,128]{3,2,1,0:T(8,128)(2,1)}), bf16[8,6,128,128]{3,2,1,0:T(8,128)(2,1)S(1)}, u32[]{:S(2)}, u32[]{:S(2)}) async-start(bf16[8,6,128,128]{3,2,1,0:T(8,128)(2,1)} %pad_maximum_fusion.2), calls=%async_computation.6 | async-start | bytes 3145728 | tf_op jit(solution)/shard_map/all_to_all | solution.py:343
  163.3 16.6 %all-to-all-done.6.refs_1_ = bf16[8,6,128,128]{3,2,1,0:T(8,128)(2,1)S(1)} async-done(((bf16[8,6,128,128]{3,2,1,0:T(8,128)(2,1)}), bf16[8,6,128,128]{3,2,1,0:T(8,128)(2,1)S(1)}, u32[]{:S(2)}, u32[]{:S(2)}) %all-to-all-start.6) | async-done | bytes 1572896 | tf_op jit(solution)/shard_map/all_to_all | solution.py:343
  (75 shorter events, 22.9 us)
Async XLA Ops:
  0.6 12.4 %copy-start = (s32[8,2,2,10]{3,2,1,0:T(2,128)S(1)}, s32[8,2,2,10]{3,2,1,0:T(2,128)}, u32[]{:S(2)}) copy-start(s32[8,2,2,10]{3,2,1,0:T(2,128)} %param.11) | copy-start | bytes 3844
  3.2 5.3 %copy-start.11 = (s32[16]{0:T(128)S(1)}, s32[16]{0:T(128)}, u32[]{:S(2)}) copy-start(s32[16]{0:T(128)} %param.10) | copy-start | bytes 196
  3.2 20.7 %all-to-all-start = ((bf16[8,4,128,128]{3,2,1,0:T(8,128)(2,1)}), bf16[8,4,128,128]{3,2,1,0:T(8,128)(2,1)S(1)}, u32[]{:S(2)}, u32[]{:S(2)}) async-start(bf16[8,4,128,128]{3,2,1,0:T(8,128)(2,1)} %pack.3), calls=%async_computation | async-start | bytes 2097152 | tf_op jit(solution)/shard_map/all_to_all | solution.py:343
  23.9 30.2 %all-to-all-start.1 = ((bf16[8,8,128,128]{3,2,1,0:T(8,128)(2,1)}), bf16[8,8,128,128]{3,2,1,0:T(8,128)(2,1)S(1)}, u32[]{:S(2)}, u32[]{:S(2)}) async-start(bf16[8,8,128,128]{3,2,1,0:T(8,128)(2,1)} %get-tuple-element.31), calls=%async_computation.1 | async-start | bytes 4194304 | tf_op jit(solution)/shard_map/all_to_all | solution.py:343
  28.9 35.2 %collective-permute-start = (bf16[8,4,128,128]{3,2,1,0:T(8,128)(2,1)S(1)}, bf16[8,4,128,128]{3,2,1,0:T(8,128)(2,1)}, u32[]{:S(2)}, u32[]{:S(2)}) collective-permute-start(bf16[8,4,128,128]{3,2,1,0:T(8,128)(2,1)S(1)} %all-to-all-done.kc_ref.vc_ref), channel_id=1, source_target_pairs={{0,8},{8,16},{16,24},{1,9},{9,17},{17,25},{2,10},{10,18},{18,26},{... | collective-permute-start | bytes 3145736 | tf_op jit(solution)/shard_map/ppermute | solution.py:350
  54.1 10.0 %copy-start.3 = (bf16[8,8,128,128]{3,2,1,0:T(8,128)(2,1)}, bf16[8,8,128,128]{3,2,1,0:T(8,128)(2,1)S(1)}, u32[]{:S(2)}) copy-start(bf16[8,8,128,128]{3,2,1,0:T(8,128)(2,1)S(1)} %all-to-all-done.1.q_ref.c_ref.kc_ref.vc_ref) | copy-start | bytes 6291460
  54.1 26.8 %all-to-all-start.2 = ((bf16[8,6,128,128]{3,2,1,0:T(8,128)(2,1)}), bf16[8,6,128,128]{3,2,1,0:T(8,128)(2,1)}, u32[]{:S(2)}, u32[]{:S(2)}) async-start(bf16[8,6,128,128]{3,2,1,0:T(8,128)(2,1)} %get-tuple-element.35), calls=%async_computation.2 | async-start | bytes 3145728 | tf_op jit(solution)/shard_map/all_to_all | solution.py:343
  59.5 18.8 %copy-start.9 = (bf16[8,2,128,128]{3,2,1,0:T(8,128)(2,1)S(1)}, bf16[8,2,128,128]{3,2,1,0:T(8,128)(2,1)}, u32[]{:S(2)}) copy-start(bf16[8,2,128,128]{3,2,1,0:T(8,128)(2,1)} %get-tuple-element.29) | copy-start | bytes 1572868
  59.5 33.5 %collective-permute-start.1 = (bf16[8,4,128,128]{3,2,1,0:T(8,128)(2,1)}, bf16[8,4,128,128]{3,2,1,0:T(8,128)(2,1)}, u32[]{:S(2)}, u32[]{:S(2)}) collective-permute-start(bf16[8,4,128,128]{3,2,1,0:T(8,128)(2,1)} %slice.20), channel_id=1, source_target_pairs={{0,8},{8,16},{16,24},{1,9},{9,17},{17,25},{2,10},{10,18},{18,26},{... | collective-permute-start | bytes 3145736 | tf_op jit(solution)/shard_map/ppermute | solution.py:350
  81.0 29.3 %all-to-all-start.3 = ((bf16[8,6,128,128]{3,2,1,0:T(8,128)(2,1)}), bf16[8,6,128,128]{3,2,1,0:T(8,128)(2,1)S(1)}, u32[]{:S(2)}, u32[]{:S(2)}) async-start(bf16[8,6,128,128]{3,2,1,0:T(8,128)(2,1)} %pad_maximum_fusion), calls=%async_computation.3 | async-start | bytes 3145728 | tf_op jit(solution)/shard_map/all_to_all | solution.py:343
  85.1 37.8 %collective-permute-start.3 = (bf16[8,4,128,128]{3,2,1,0:T(8,128)(2,1)}, bf16[8,4,128,128]{3,2,1,0:T(8,128)(2,1)}, u32[]{:S(2)}, u32[]{:S(2)}) collective-permute-start(bf16[8,4,128,128]{3,2,1,0:T(8,128)(2,1)} %get-tuple-element.41), channel_id=1, source_target_pairs={{8,0},{16,8},{24,16},{9,1},{17,9},{25,17},{10,2},{18,10},{26,18},{... | collective-permute-start | bytes 3145736 | tf_op jit(solution)/shard_map/ppermute | solution.py:314
  88.3 26.2 %collective-permute-start.2 = (bf16[8,2,128,128]{3,2,1,0:T(8,128)(2,1)}, bf16[8,2,128,128]{3,2,1,0:T(8,128)(2,1)S(1)}, u32[]{:S(2)}, u32[]{:S(2)}) collective-permute-start(bf16[8,2,128,128]{3,2,1,0:T(8,128)(2,1)} %slice.21), channel_id=1, source_target_pairs={{0,8},{8,16},{16,24},{1,9},{9,17},{17,25},{2,10},{10,18},{18,26},{... | collective-permute-start | bytes 1572872 | tf_op jit(solution)/shard_map/ppermute | solution.py:350
  93.0 1.6 copy-start.4
  108.9 27.2 %collective-permute-start.4 = (bf16[8,4,128,128]{3,2,1,0:T(8,128)(2,1)}, bf16[8,4,128,128]{3,2,1,0:T(8,128)(2,1)}, u32[]{:S(2)}, u32[]{:S(2)}) collective-permute-start(bf16[8,4,128,128]{3,2,1,0:T(8,128)(2,1)} %get-tuple-element.48), channel_id=1, source_target_pairs={{8,0},{16,8},{24,16},{9,1},{17,9},{25,17},{10,2},{18,10},{26,18},{... | collective-permute-start | bytes 3145736 | tf_op jit(solution)/shard_map/ppermute | solution.py:314
  110.2 12.6 %copy-start.1 = (bf16[8,6,128,128]{3,2,1,0:T(8,128)(2,1)}, bf16[8,6,128,128]{3,2,1,0:T(8,128)(2,1)S(1)}, u32[]{:S(2)}) copy-start(bf16[8,6,128,128]{3,2,1,0:T(8,128)(2,1)S(1)} %all-to-all-done.3.q_ref.c_ref.refs_0_) | copy-start | bytes 4718596
  110.2 19.6 %all-to-all-start.4 = ((bf16[8,4,128,128]{3,2,1,0:T(8,128)(2,1)}), bf16[8,4,128,128]{3,2,1,0:T(8,128)(2,1)S(1)}, u32[]{:S(2)}, u32[]{:S(2)}) async-start(bf16[8,4,128,128]{3,2,1,0:T(8,128)(2,1)} %get-tuple-element.38), calls=%async_computation.4 | async-start | bytes 2097152 | tf_op jit(solution)/shard_map/all_to_all | solution.py:343
  114.5 8.4 %copy-start.7 = (f32[8,4,128,128]{3,2,1,0:T(8,128)S(1)}, f32[8,4,128,128]{3,2,1,0:T(8,128)}, u32[]{:S(2)}) copy-start(f32[8,4,128,128]{3,2,1,0:T(8,128)} %get-tuple-element.40) | copy-start | bytes 6291460
  122.9 1.6 copy-start.10
  125.8 8.6 %copy-start.12 = (bf16[8,2,128,128]{3,2,1,0:T(8,128)(2,1)S(1)}, bf16[8,2,128,128]{3,2,1,0:T(8,128)(2,1)}, u32[]{:S(2)}) copy-start(bf16[8,2,128,128]{3,2,1,0:T(8,128)(2,1)} %get-tuple-element.50) | copy-start | bytes 1572868
  130.8 24.5 %all-to-all-start.5 = ((bf16[8,6,128,128]{3,2,1,0:T(8,128)(2,1)}), bf16[8,6,128,128]{3,2,1,0:T(8,128)(2,1)S(1)}, u32[]{:S(2)}, u32[]{:S(2)}) async-start(bf16[8,6,128,128]{3,2,1,0:T(8,128)(2,1)} %pad_maximum_fusion.1), calls=%async_computation.5 | async-start | bytes 3145728 | tf_op jit(solution)/shard_map/all_to_all | solution.py:343
  134.4 17.0 %collective-permute-start.5 = (bf16[8,2,128,128]{3,2,1,0:T(8,128)(2,1)S(1)}, bf16[8,2,128,128]{3,2,1,0:T(8,128)(2,1)S(1)}, u32[]{:S(2)}, u32[]{:S(2)}) collective-permute-start(bf16[8,2,128,128]{3,2,1,0:T(8,128)(2,1)S(1)} %copy-done.12), channel_id=1, source_target_pairs={{8,0},{16,8},{24,16},{9,1},{17,9},{25,17},{10,2},{18,10},{26,18},{... | collective-permute-start | bytes 1572872 | tf_op jit(solution)/shard_map/ppermute | solution.py:314
  136.2 15.3 %copy-start.8 = (f32[8,2,128,128]{3,2,1,0:T(8,128)S(1)}, f32[8,2,128,128]{3,2,1,0:T(8,128)}, u32[]{:S(2)}) copy-start(f32[8,2,128,128]{3,2,1,0:T(8,128)} %get-tuple-element.42) | copy-start | bytes 3145732
  155.4 24.5 %all-to-all-start.6 = ((bf16[8,6,128,128]{3,2,1,0:T(8,128)(2,1)}), bf16[8,6,128,128]{3,2,1,0:T(8,128)(2,1)S(1)}, u32[]{:S(2)}, u32[]{:S(2)}) async-start(bf16[8,6,128,128]{3,2,1,0:T(8,128)(2,1)} %pad_maximum_fusion.2), calls=%async_computation.6 | async-start | bytes 3145728 | tf_op jit(solution)/shard_map/all_to_all | solution.py:343
  159.0 1.4 copy-start.2
  (2 other events, 2.2 us)

commit v8 on v7

--- a/solution.py
+++ b/solution.py
@@ -40,7 +40,7 @@
     return [pltpu.with_memory_space_constraint(array, pltpu.HBM) for array in arrays]
 
 
-def pack(pairs, members, heads, layouts):
+def pack(pairs, members, heads, layouts, rooms):
     names = sorted({name for layout in layouts for name, _ in layout})
     arrays = [array for name in names for array in pairs[name]]
     tokens, width = arrays[0].shape
@@ -60,7 +60,9 @@
     return pl.pallas_call(
         body,
         grid=(STEPS,),
-        out_shape=[hbm((members, *shape), arrays[0].dtype) for shape in shapes],
+        out_shape=[
+            hbm((members, room, tokens, HEAD_DIM), arrays[0].dtype) for room in rooms
+        ],
         in_specs=[pl.BlockSpec((tokens, width // STEPS), lambda i: (0, i))] * len(arrays),
         out_specs=[pl.BlockSpec((here, *shape), lambda i: (i, 0, 0, 0)) for shape in shapes],
         compiler_params=pltpu.CompilerParams(vmem_limit_bytes=VMEM_LIMIT),
@@ -102,8 +104,9 @@
 
 def attention_body(
     bias_ref, class_ref, q_ref, c_ref, kc_ref, vc_ref, kp_ref, vp_ref,
-    odq_ref, cur_ref, prev_ref, k_all, v_all, dk_all, dv_all,
+    *refs,
 ):
+    odq_ref, cur_ref, prev_ref, k_all, v_all, dk_all, dv_all = refs[-7:]
     parts, rows = q_ref.shape[0], q_ref.shape[1]
     plane = parts * rows
     slab = plane // 2
@@ -201,7 +204,7 @@
     cur_ref[:, 1] = dv_all[plane:].reshape(kp_ref.shape)
 
 
-def attention(bias, classes, count, qc, kv, kv_prev):
+def attention(bias, classes, count, qc, kv, kv_prev, target):
     parts, _, rows, _ = qc[0].shape
     plane = parts * rows
     products = count * 2 * (plane // 2) * 3 * (plane // 2)
@@ -213,20 +216,26 @@
 
     shape = (parts, 2 * count, rows, HEAD_DIM)
     both = pl.BlockSpec((parts, 2, rows, HEAD_DIM), lambda h: (0, h, 0, 0))
+    into = both
+    if target is not None:
+        skip = target[1] // 2
+        into = pl.BlockSpec((parts, 2, rows, HEAD_DIM), lambda h: (0, skip + h, 0, 0))
     operands = [(place, a) for place in (qc, kv, kv_prev) for a in range(2)]
     return pl.pallas_call(
         attention_body,
         grid=(count,),
         out_shape=[
-            hbm(shape, jnp.bfloat16),
+            hbm(shape if target is None else target[0].shape, jnp.bfloat16),
             hbm(shape, jnp.float32),
             hbm(shape, jnp.bfloat16),
         ],
         in_specs=[
             pl.BlockSpec(bias.shape, lambda h: (0, 0, 0)),
             pl.BlockSpec(classes.shape, lambda h: (0, 0)),
-        ] + [one(place, a) for place, a in operands],
-        out_specs=[both, both, both],
+        ] + [one(place, a) for place, a in operands]
+        + ([] if target is None else [pl.BlockSpec(memory_space=pl.ANY)]),
+        out_specs=[into, both, both],
+        input_output_aliases={} if target is None else {2 + len(operands): 0},
         scratch_shapes=[
             pltpu.VMEM((2 * plane, HEAD_DIM), jnp.bfloat16),
             pltpu.VMEM((2 * plane, HEAD_DIM), jnp.bfloat16),
@@ -240,7 +249,11 @@
             transcendentals=products,
         ),
         name="attention",
-    )(*in_hbm([bias, classes]), *[place[0] for place, _ in operands])
+    )(
+        *in_hbm([bias, classes] + [place[0] for place, _ in operands[:4]]),
+        *[place[0] for place, _ in operands[4:]],
+        *([] if target is None else [target[0]]),
+    )
 
 
 def mask_operands(frame_blocks, tile_lists, z, bands, frame_rows, frame_cols):
@@ -306,9 +319,9 @@
     def layout(items):
         return [(name, firsts[i] + h) for name, i in items for h in range(counts[i])]
 
-    def work_on(i):
+    def work_on(i, target):
         odq, dkv, dkv_prev = attention(
-            bias, classes, counts[i], place["qc", i], place["kv", i], (shifted[i], 0)
+            bias, classes, counts[i], place["qc", i], place["kv", i], (shifted[i], 0), target
         )
         made["o", i] = odq
         owed.append((dkv, lax.ppermute(dkv_prev, "plane", down)))
@@ -321,20 +334,37 @@
 
     pairs = {"kv": (k, v), "qc": (q, c)}
     inward = [[item for item in items if item[0] in pairs] for items in order]
-    sent = pack(pairs, members, heads, [layout(inward[0])])
-    sent += pack(pairs, members, heads, [layout(items) for items in inward[1:] if items])
+    rooms = [sum(2 * counts[i] for _, i in items) for items in order]
+    later = [step for step in range(1, len(order)) if inward[step]]
+    sent = dict(zip([0], pack(pairs, members, heads, [layout(inward[0])], rooms[:1])))
+    sent.update(
+        zip(
+            later,
+            pack(
+                pairs, members, heads,
+                [layout(inward[step]) for step in later], [rooms[step] for step in later],
+            ),
+        )
+    )
     bias, classes = mask_operands(
         frame_blocks, tile_lists, z, bands, queries.shape[1] * bands, queries.shape[2]
     )
     for step, items in enumerate(order):
-        parts = [sent[step]] if inward[step] else []
+        packed, slot, parts = sent.get(step), 2 * len(layout(inward[step])), []
         for name, i in items[len(inward[step]) :]:
             if name == "o":
-                while ("o", i) not in made:
-                    work_on(len(owed))
-                parts.append(made["o", i])
+                while len(owed) <= i:
+                    ours = packed is not None and len(owed) == i
+                    work_on(len(owed), (packed, slot) if ours else None)
+                if packed is None:
+                    parts.append(made["o", i])
+                else:
+                    packed = made["o", i]
             else:
                 parts.append(returned(i))
+            slot += 2 * counts[i]
+        if packed is not None:
+            parts.insert(0, packed)
         buffer = jnp.concatenate(parts, axis=1) if len(parts) > 1 else parts[0]
         if step == 2:
             buffer = after(buffer, (bias, classes))

time: 183 us -> 181 us (0.989)
  waiting for transfers between devices: 65 us -> 67.9 us
  starting transfers between devices: 46.5 us -> 43.8 us
  other arithmetic: 12.1 us -> 9.47 us
    all_to_all x7, waiting for transfers between devices: 51.6 us -> 54.5 us  [on_device(): lax.all_to_all(buffer, group, split_axis=0, concat_axis=0, tiled=True)]
    concatenate x3 -> x2, other arithmetic: 5.21 us -> 2.63 us  [on_device(): buffer = jnp.concatenate(parts, axis=1) if len(parts) > 1 else parts[0]]
    ppermute x3, starting transfers between devices: 13.9 us -> 11.9 us  [on_device(): shifted.append(lax.ppermute(moved, 'plane', up))]
    unnamed x26 -> x24, local copies, waits for them, and re-layouts: 5.22 us -> 4.6 us
  transfers between devices with their start and end apart: 13 -> 13, of which waited for: 7 -> 8; matrix products, arithmetic and copies ran while one was open for 9% -> 8% of each run, Pallas kernels for 24% -> 24%
where the time goes in v8:
time: 181 us; the launch traced here: 179 us
  waiting for transfers between devices  67.9 us (38%)
  Pallas kernels  47.5 us (26%)
  starting transfers between devices  43.8 us (24%)
  other arithmetic  9.47 us (5%)
  local copies, waits for them, and re-layouts  9.3 us (5%)
    all_to_all x7, waiting for transfers between devices, on_device(): lax.all_to_all(buffer, group, split_axis=0, concat_axis=0, tiled=True)  54.5 us
    pallas_call x3, Pallas kernels, attention(): pl.pallas_call(attention_body, grid=(count,), out_shape=[hbm(shape if tar...  37.3 us
    all_to_all x7, starting transfers between devices, on_device(): lax.all_to_all(buffer, group, split_axis=0, concat_axis=0, tiled=True)  28 us
    ppermute x3, waiting for transfers between devices, work_on(): owed.append((dkv, lax.ppermute(dkv_prev, 'plane', down)))  13.5 us
    ppermute x3, starting transfers between devices, on_device(): shifted.append(lax.ppermute(moved, 'plane', up))  11.9 us
    pallas_call x2, Pallas kernels, pack(): pl.pallas_call(body, grid=(STEPS,), out_shape=[hbm((members, room, tokens...  6.76 us
    unnamed x24, local copies, waits for them, and re-layouts  4.6 us
    convert_element_type x3, other arithmetic, returned(): return (dkv + dkv_next.astype(jnp.float32)).astype(jnp.bfloat16)  3.94 us
  transfers between devices with their start and end apart: 13, of which 8 were waited for; matrix products, arithmetic and copies ran while one was open for 8% of the time, Pallas kernels for 24%

profile of v8, /device:TPU:0, one launch (start us, length us, event | category | flops | bytes accessed | tf_op | source)
XLA Modules:
  0.0 179.0 jit_solution(447120588141196952)
XLA Ops:
  0.6 2.6 %pack.3 = bf16[8,4,128,128]{3,2,1,0:T(8,128)(2,1)} custom-call(bf16[128,5120]{1,0:T(8,128)(2,1)} %bitcast.18, bf16[128,5120]{1,0:T(8,128)(2,1)} %bitcast.20), custom_call_target="tpu_custom_call" | custom-call | bytes 5242880 | tf_op jit(solution)/shard_map/pack/pallas_call | solution.py:60
  3.2 5.3 %all-to-all-start = ((bf16[8,4,128,128]{3,2,1,0:T(8,128)(2,1)}), bf16[8,4,128,128]{3,2,1,0:T(8,128)(2,1)S(1)}, u32[]{:S(2)}, u32[]{:S(2)}) async-start(bf16[8,4,128,128]{3,2,1,0:T(8,128)(2,1)} %pack.3), calls=%async_computation | async-start | bytes 2097152 | tf_op jit(solution)/shard_map/all_to_all | solution.py:373
  8.8 4.2 %pack.2 = (bf16[8,8,128,128]{3,2,1,0:T(8,128)(2,1)}, bf16[8,6,128,128]{3,2,1,0:T(8,128)(2,1)}, bf16[8,6,128,128]{3,2,1,0:T(8,128)(2,1)}) custom-call(bf16[128,5120]{1,0:T(8,128)(2,1)} %bitcast.19, bf16[128,5120]{1,0:T(8,128)(2,1)} %bitcast.21, bf16[128,5120]{1,0:T(8,128)(2,1)} %bitcast.22, bf16[128,5120]{1,0:T(8,128)(2,1)} %bitcast.23), custom_call_target="tpu_custom_call" | custom-call | bytes 10485760 | tf_op jit(solution)/shard_map/pack/pallas_call | solution.py:60
  13.1 10.8 %all-to-all-done.kc_ref.vc_ref = bf16[8,4,128,128]{3,2,1,0:T(8,128)(2,1)S(1)} async-done(((bf16[8,4,128,128]{3,2,1,0:T(8,128)(2,1)}), bf16[8,4,128,128]{3,2,1,0:T(8,128)(2,1)S(1)}, u32[]{:S(2)}, u32[]{:S(2)}) %all-to-all-start) | async-done | bytes 1048608 | tf_op jit(solution)/shard_map/all_to_all | solution.py:373
  24.9 3.6 %all-to-all-start.1 = ((bf16[8,8,128,128]{3,2,1,0:T(8,128)(2,1)}), bf16[8,8,128,128]{3,2,1,0:T(8,128)(2,1)S(1)}, u32[]{:S(2)}, u32[]{:S(2)}) async-start(bf16[8,8,128,128]{3,2,1,0:T(8,128)(2,1)} %get-tuple-element.30), calls=%async_computation.1 | async-start | bytes 4194304 | tf_op jit(solution)/shard_map/all_to_all | solution.py:373
  29.9 3.6 %collective-permute-start = (bf16[8,4,128,128]{3,2,1,0:T(8,128)(2,1)}, bf16[8,4,128,128]{3,2,1,0:T(8,128)(2,1)S(1)}, u32[]{:S(2)}, u32[]{:S(2)}) collective-permute-start(bf16[8,4,128,128]{3,2,1,0:T(8,128)(2,1)} %copy-done.7), channel_id=1, source_target_pairs={{0,8},{8,16},{16,24},{1,9},{9,17},{17,25},{2,10},{10,18},{18,26},{... | collective-permute-start | bytes 3145736 | tf_op jit(solution)/shard_map/ppermute | solution.py:380
  33.5 2.0 %fusion.16.class_ref = bf16[512,128]{1,0:T(8,128)(2,1)} fusion(s32[512]{0:T(512)S(1)} %get-tuple-element.56, s32[512]{0:T(512)S(1)} %get-tuple-element.62, s32[512]{0:T(512)S(1)} %get-tuple-element.57, s32[512]{0:T(512)S(1)} %get-tuple-element.59, s32[512]{0:T(512)S(1)} %get-tuple-element.58, s32[512]{0:T(512)S(1)} %get-tuple-element.63, ...), kind=kLoop, calls=%fused_computation.40 | loop fusion | flops 3276800 | bytes 144896 | tf_op jit(solution)/shard_map/convert_element_type | solution.py:292
  36.5 18.6 %all-to-all-done.1.q_ref.c_ref.kc_ref.vc_ref = bf16[8,8,128,128]{3,2,1,0:T(8,128)(2,1)S(1)} async-done(((bf16[8,8,128,128]{3,2,1,0:T(8,128)(2,1)}), bf16[8,8,128,128]{3,2,1,0:T(8,128)(2,1)S(1)}, u32[]{:S(2)}, u32[]{:S(2)}) %all-to-all-start.1) | async-done | bytes 2097184 | tf_op jit(solution)/shard_map/all_to_all | solution.py:373
  55.1 4.3 %all-to-all-start.2 = ((bf16[8,6,128,128]{3,2,1,0:T(8,128)(2,1)}), bf16[8,6,128,128]{3,2,1,0:T(8,128)(2,1)}, u32[]{:S(2)}, u32[]{:S(2)}) async-start(bf16[8,6,128,128]{3,2,1,0:T(8,128)(2,1)} %get-tuple-element.35), calls=%async_computation.2 | async-start | bytes 3145728 | tf_op jit(solution)/shard_map/all_to_all | solution.py:373
  60.5 3.5 %collective-permute-start.1 = (bf16[8,4,128,128]{3,2,1,0:T(8,128)(2,1)}, bf16[8,4,128,128]{3,2,1,0:T(8,128)(2,1)S(1)}, u32[]{:S(2)}, u32[]{:S(2)}) collective-permute-start(bf16[8,4,128,128]{3,2,1,0:T(8,128)(2,1)} %slice.20), channel_id=1, source_target_pairs={{0,8},{8,16},{16,24},{1,9},{9,17},{17,25},{2,10},{10,18},{18,26},{... | collective-permute-start | bytes 3145736 | tf_op jit(solution)/shard_map/ppermute | solution.py:380
  64.0 14.4 %attention.3 = (bf16[8,6,128,128]{3,2,1,0:T(8,128)(2,1)}, f32[8,4,128,128]{3,2,1,0:T(8,128)}, bf16[8,4,128,128]{3,2,1,0:T(8,128)(2,1)}) custom-call(bf16[2,1536,128]{2,1,0:T(8,128)(2,1)} %bitcast.24, bf16[512,128]{1,0:T(8,128)(2,1)} %fusion.16.class_ref, bf16[8,8,128,128]{3,2,1,0:T(8,128)(2,1)} %copy-done.5, ...), custom_call_target="tpu_custom_call", output_to_operand_aliasing={{0}: (8, {})} | custom-call | flops 9663676416 | bytes 9437184 | tf_op jit(solution)/shard_map/attention/pallas_call | solution.py:224
  78.4 2.0 %all-to-all-done.2.q_ref.c_ref.kc_ref.vc_ref = bf16[8,6,128,128]{3,2,1,0:T(8,128)(2,1)} async-done(((bf16[8,6,128,128]{3,2,1,0:T(8,128)(2,1)}), bf16[8,6,128,128]{3,2,1,0:T(8,128)(2,1)}, u32[]{:S(2)}, u32[]{:S(2)}) %all-to-all-start.2) | async-done | bytes 1572896 | tf_op jit(solution)/shard_map/all_to_all | solution.py:373
  80.4 3.6 %all-to-all-start.3 = ((bf16[8,6,128,128]{3,2,1,0:T(8,128)(2,1)}), bf16[8,6,128,128]{3,2,1,0:T(8,128)(2,1)S(1)}, u32[]{:S(2)}, u32[]{:S(2)}) async-start(bf16[8,6,128,128]{3,2,1,0:T(8,128)(2,1)} %get-tuple-element.36), calls=%async_computation.3 | async-start | bytes 3145728 | tf_op jit(solution)/shard_map/all_to_all | solution.py:373
  87.2 4.8 %collective-permute-start.2 = (bf16[8,2,128,128]{3,2,1,0:T(8,128)(2,1)}, bf16[8,2,128,128]{3,2,1,0:T(8,128)(2,1)S(1)}, u32[]{:S(2)}, u32[]{:S(2)}) collective-permute-start(bf16[8,2,128,128]{3,2,1,0:T(8,128)(2,1)} %slice.21), channel_id=1, source_target_pairs={{0,8},{8,16},{16,24},{1,9},{9,17},{17,25},{2,10},{10,18},{18,26},{... | collective-permute-start | bytes 1572872 | tf_op jit(solution)/shard_map/ppermute | solution.py:380
  92.0 14.4 %attention.4 = (bf16[8,4,128,128]{3,2,1,0:T(8,128)(2,1)}, f32[8,4,128,128]{3,2,1,0:T(8,128)}, bf16[8,4,128,128]{3,2,1,0:T(8,128)(2,1)}) custom-call(bf16[2,1536,128]{2,1,0:T(8,128)(2,1)} %bitcast.25, bf16[512,128]{1,0:T(8,128)(2,1)} %fusion.16.class_ref, bf16[8,6,128,128]{3,2,1,0:T(8,128)(2,1)} %all-to-all-done.2.q_ref.c_ref.kc_ref.vc_ref, ...), custom_call_target="tpu_custom_call" | custom-call | flops 9663676416 | bytes 9437184 | tf_op jit(solution)/shard_map/attention/pallas_call | solution.py:224
  107.7 4.1 %all-to-all-start.4 = ((bf16[8,4,128,128]{3,2,1,0:T(8,128)(2,1)}), bf16[8,4,128,128]{3,2,1,0:T(8,128)(2,1)S(1)}, u32[]{:S(2)}, u32[]{:S(2)}) async-start(bf16[8,4,128,128]{3,2,1,0:T(8,128)(2,1)} %get-tuple-element.38), calls=%async_computation.4 | async-start | bytes 2097152 | tf_op jit(solution)/shard_map/all_to_all | solution.py:373
  111.8 8.5 %attention.5 = (bf16[8,2,128,128]{3,2,1,0:T(8,128)(2,1)}, f32[8,2,128,128]{3,2,1,0:T(8,128)}, bf16[8,2,128,128]{3,2,1,0:T(8,128)(2,1)}) custom-call(bf16[2,1536,128]{2,1,0:T(8,128)(2,1)} %bitcast.26, bf16[512,128]{1,0:T(8,128)(2,1)} %fusion.16.class_ref, bf16[8,6,128,128]{3,2,1,0:T(8,128)(2,1)} %copy-done.1, bf16[8,6,128,128]{3,2,1,0:T(8,128)(2,1)} %copy-done.1, ...), custom_call_target="tpu_custom_call" | custom-call | flops 4831838208 | bytes 4718592 | tf_op jit(solution)/shard_map/attention/pallas_call | solution.py:224
  123.2 4.0 %all-to-all-done.4.refs_1_ = bf16[8,4,128,128]{3,2,1,0:T(8,128)(2,1)S(1)} async-done(((bf16[8,4,128,128]{3,2,1,0:T(8,128)(2,1)}), bf16[8,4,128,128]{3,2,1,0:T(8,128)(2,1)S(1)}, u32[]{:S(2)}, u32[]{:S(2)}) %all-to-all-start.4) | async-done | bytes 1048608 | tf_op jit(solution)/shard_map/all_to_all | solution.py:373
  128.2 3.6 %all-to-all-start.5 = ((bf16[8,6,128,128]{3,2,1,0:T(8,128)(2,1)}), bf16[8,6,128,128]{3,2,1,0:T(8,128)(2,1)S(1)}, u32[]{:S(2)}, u32[]{:S(2)}) async-start(bf16[8,6,128,128]{3,2,1,0:T(8,128)(2,1)} %pad_maximum_fusion), calls=%async_computation.5 | async-start | bytes 3145728 | tf_op jit(solution)/shard_map/all_to_all | solution.py:373
  134.2 2.2 %add_convert_fusion = bf16[8,4,128,128]{3,2,1,0:T(8,128)(2,1)S(1)} fusion(f32[8,4,128,128]{3,2,1,0:T(8,128)} %get-tuple-element.47, bf16[8,4,128,128]{3,2,1,0:T(8,128)(2,1)} %collective-permute-done.4), kind=kLoop, calls=%fused_computation | loop fusion | flops 1572864 | bytes 4194304 | tf_op jit(solution)/shard_map/convert_element_type | solution.py:333
  136.4 12.4 %collective-permute-done.5 = bf16[8,2,128,128]{3,2,1,0:T(8,128)(2,1)S(1)} collective-permute-done((bf16[8,2,128,128]{3,2,1,0:T(8,128)(2,1)S(1)}, bf16[8,2,128,128]{3,2,1,0:T(8,128)(2,1)S(1)}, u32[]{:S(2)}, u32[]{:S(2)}) %collective-permute-start.5) | collective-permute-done | bytes 524320 | tf_op jit(solution)/shard_map/ppermute | solution.py:327
  150.3 2.5 %all-to-all-done.5.refs_2_.refs_0_ = bf16[8,6,128,128]{3,2,1,0:T(8,128)(2,1)S(1)} async-done(((bf16[8,6,128,128]{3,2,1,0:T(8,128)(2,1)}), bf16[8,6,128,128]{3,2,1,0:T(8,128)(2,1)S(1)}, u32[]{:S(2)}, u32[]{:S(2)}) %all-to-all-start.5) | async-done | bytes 1572896 | tf_op jit(solution)/shard_map/all_to_all | solution.py:373
  152.7 3.6 %all-to-all-start.6 = ((bf16[8,6,128,128]{3,2,1,0:T(8,128)(2,1)}), bf16[8,6,128,128]{3,2,1,0:T(8,128)(2,1)S(1)}, u32[]{:S(2)}, u32[]{:S(2)}) async-start(bf16[8,6,128,128]{3,2,1,0:T(8,128)(2,1)} %pad_maximum_fusion.1), calls=%async_computation.6 | async-start | bytes 3145728 | tf_op jit(solution)/shard_map/all_to_all | solution.py:373
  160.7 16.6 %all-to-all-done.6.refs_1_ = bf16[8,6,128,128]{3,2,1,0:T(8,128)(2,1)S(1)} async-done(((bf16[8,6,128,128]{3,2,1,0:T(8,128)(2,1)}), bf16[8,6,128,128]{3,2,1,0:T(8,128)(2,1)S(1)}, u32[]{:S(2)}, u32[]{:S(2)}) %all-to-all-start.6) | async-done | bytes 1572896 | tf_op jit(solution)/shard_map/all_to_all | solution.py:373
  (72 shorter events, 22.9 us)
Async XLA Ops:
  0.6 12.4 %copy-start = (s32[8,2,2,10]{3,2,1,0:T(2,128)S(1)}, s32[8,2,2,10]{3,2,1,0:T(2,128)}, u32[]{:S(2)}) copy-start(s32[8,2,2,10]{3,2,1,0:T(2,128)} %param.11) | copy-start | bytes 3844
  3.2 5.3 %copy-start.10 = (s32[16]{0:T(128)S(1)}, s32[16]{0:T(128)}, u32[]{:S(2)}) copy-start(s32[16]{0:T(128)} %param.10) | copy-start | bytes 196
  3.2 20.7 %all-to-all-start = ((bf16[8,4,128,128]{3,2,1,0:T(8,128)(2,1)}), bf16[8,4,128,128]{3,2,1,0:T(8,128)(2,1)S(1)}, u32[]{:S(2)}, u32[]{:S(2)}) async-start(bf16[8,4,128,128]{3,2,1,0:T(8,128)(2,1)} %pack.3), calls=%async_computation | async-start | bytes 2097152 | tf_op jit(solution)/shard_map/all_to_all | solution.py:373
  23.9 1.0 copy-start.7
  24.9 30.2 %all-to-all-start.1 = ((bf16[8,8,128,128]{3,2,1,0:T(8,128)(2,1)}), bf16[8,8,128,128]{3,2,1,0:T(8,128)(2,1)S(1)}, u32[]{:S(2)}, u32[]{:S(2)}) async-start(bf16[8,8,128,128]{3,2,1,0:T(8,128)(2,1)} %get-tuple-element.30), calls=%async_computation.1 | async-start | bytes 4194304 | tf_op jit(solution)/shard_map/all_to_all | solution.py:373
  29.9 34.1 %collective-permute-start = (bf16[8,4,128,128]{3,2,1,0:T(8,128)(2,1)}, bf16[8,4,128,128]{3,2,1,0:T(8,128)(2,1)S(1)}, u32[]{:S(2)}, u32[]{:S(2)}) collective-permute-start(bf16[8,4,128,128]{3,2,1,0:T(8,128)(2,1)} %copy-done.7), channel_id=1, source_target_pairs={{0,8},{8,16},{16,24},{1,9},{9,17},{17,25},{2,10},{10,18},{18,26},{... | collective-permute-start | bytes 3145736 | tf_op jit(solution)/shard_map/ppermute | solution.py:380
  55.1 4.3 %copy-start.5 = (bf16[8,8,128,128]{3,2,1,0:T(8,128)(2,1)}, bf16[8,8,128,128]{3,2,1,0:T(8,128)(2,1)S(1)}, u32[]{:S(2)}) copy-start(bf16[8,8,128,128]{3,2,1,0:T(8,128)(2,1)S(1)} %all-to-all-done.1.q_ref.c_ref.kc_ref.vc_ref) | copy-start | bytes 6291460
  55.1 25.3 %all-to-all-start.2 = ((bf16[8,6,128,128]{3,2,1,0:T(8,128)(2,1)}), bf16[8,6,128,128]{3,2,1,0:T(8,128)(2,1)}, u32[]{:S(2)}, u32[]{:S(2)}) async-start(bf16[8,6,128,128]{3,2,1,0:T(8,128)(2,1)} %get-tuple-element.35), calls=%async_computation.2 | async-start | bytes 3145728 | tf_op jit(solution)/shard_map/all_to_all | solution.py:373
  60.5 31.6 %collective-permute-start.1 = (bf16[8,4,128,128]{3,2,1,0:T(8,128)(2,1)}, bf16[8,4,128,128]{3,2,1,0:T(8,128)(2,1)S(1)}, u32[]{:S(2)}, u32[]{:S(2)}) collective-permute-start(bf16[8,4,128,128]{3,2,1,0:T(8,128)(2,1)} %slice.20), channel_id=1, source_target_pairs={{0,8},{8,16},{16,24},{1,9},{9,17},{17,25},{2,10},{10,18},{18,26},{... | collective-permute-start | bytes 3145736 | tf_op jit(solution)/shard_map/ppermute | solution.py:380
  80.4 27.2 %all-to-all-start.3 = ((bf16[8,6,128,128]{3,2,1,0:T(8,128)(2,1)}), bf16[8,6,128,128]{3,2,1,0:T(8,128)(2,1)S(1)}, u32[]{:S(2)}, u32[]{:S(2)}) async-start(bf16[8,6,128,128]{3,2,1,0:T(8,128)(2,1)} %get-tuple-element.36), calls=%async_computation.3 | async-start | bytes 3145728 | tf_op jit(solution)/shard_map/all_to_all | solution.py:373
  84.0 36.3 %collective-permute-start.3 = (bf16[8,4,128,128]{3,2,1,0:T(8,128)(2,1)}, bf16[8,4,128,128]{3,2,1,0:T(8,128)(2,1)}, u32[]{:S(2)}, u32[]{:S(2)}) collective-permute-start(bf16[8,4,128,128]{3,2,1,0:T(8,128)(2,1)} %get-tuple-element.41), channel_id=1, source_target_pairs={{8,0},{16,8},{24,16},{9,1},{17,9},{25,17},{10,2},{18,10},{26,18},{... | collective-permute-start | bytes 3145736 | tf_op jit(solution)/shard_map/ppermute | solution.py:327
  87.2 24.6 %collective-permute-start.2 = (bf16[8,2,128,128]{3,2,1,0:T(8,128)(2,1)}, bf16[8,2,128,128]{3,2,1,0:T(8,128)(2,1)S(1)}, u32[]{:S(2)}, u32[]{:S(2)}) collective-permute-start(bf16[8,2,128,128]{3,2,1,0:T(8,128)(2,1)} %slice.21), channel_id=1, source_target_pairs={{0,8},{8,16},{16,24},{1,9},{9,17},{17,25},{2,10},{10,18},{18,26},{... | collective-permute-start | bytes 1572872 | tf_op jit(solution)/shard_map/ppermute | solution.py:380
  106.4 27.8 %collective-permute-start.4 = (bf16[8,4,128,128]{3,2,1,0:T(8,128)(2,1)}, bf16[8,4,128,128]{3,2,1,0:T(8,128)(2,1)}, u32[]{:S(2)}, u32[]{:S(2)}) collective-permute-start(bf16[8,4,128,128]{3,2,1,0:T(8,128)(2,1)} %get-tuple-element.48), channel_id=1, source_target_pairs={{8,0},{16,8},{24,16},{9,1},{17,9},{25,17},{10,2},{18,10},{26,18},{... | collective-permute-start | bytes 3145736 | tf_op jit(solution)/shard_map/ppermute | solution.py:327
  107.7 4.1 %copy-start.1 = (bf16[8,6,128,128]{3,2,1,0:T(8,128)(2,1)}, bf16[8,6,128,128]{3,2,1,0:T(8,128)(2,1)S(1)}, u32[]{:S(2)}) copy-start(bf16[8,6,128,128]{3,2,1,0:T(8,128)(2,1)S(1)} %all-to-all-done.3.q_ref.c_ref.refs_0_) | copy-start | bytes 4718596
  107.7 19.5 %all-to-all-start.4 = ((bf16[8,4,128,128]{3,2,1,0:T(8,128)(2,1)}), bf16[8,4,128,128]{3,2,1,0:T(8,128)(2,1)S(1)}, u32[]{:S(2)}, u32[]{:S(2)}) async-start(bf16[8,4,128,128]{3,2,1,0:T(8,128)(2,1)} %get-tuple-element.38), calls=%async_computation.4 | async-start | bytes 2097152 | tf_op jit(solution)/shard_map/all_to_all | solution.py:373
  111.8 8.5 %copy-start.6 = (f32[8,4,128,128]{3,2,1,0:T(8,128)S(1)}, f32[8,4,128,128]{3,2,1,0:T(8,128)}, u32[]{:S(2)}) copy-start(f32[8,4,128,128]{3,2,1,0:T(8,128)} %get-tuple-element.40) | copy-start | bytes 6291460
  120.3 1.6 copy-start.9
  123.2 8.5 %copy-start.11 = (bf16[8,2,128,128]{3,2,1,0:T(8,128)(2,1)S(1)}, bf16[8,2,128,128]{3,2,1,0:T(8,128)(2,1)}, u32[]{:S(2)}) copy-start(bf16[8,2,128,128]{3,2,1,0:T(8,128)(2,1)} %get-tuple-element.50) | copy-start | bytes 1572868
  128.2 24.5 %all-to-all-start.5 = ((bf16[8,6,128,128]{3,2,1,0:T(8,128)(2,1)}), bf16[8,6,128,128]{3,2,1,0:T(8,128)(2,1)S(1)}, u32[]{:S(2)}, u32[]{:S(2)}) async-start(bf16[8,6,128,128]{3,2,1,0:T(8,128)(2,1)} %pad_maximum_fusion), calls=%async_computation.5 | async-start | bytes 3145728 | tf_op jit(solution)/shard_map/all_to_all | solution.py:373
  131.8 17.0 %collective-permute-start.5 = (bf16[8,2,128,128]{3,2,1,0:T(8,128)(2,1)S(1)}, bf16[8,2,128,128]{3,2,1,0:T(8,128)(2,1)S(1)}, u32[]{:S(2)}, u32[]{:S(2)}) collective-permute-start(bf16[8,2,128,128]{3,2,1,0:T(8,128)(2,1)S(1)} %copy-done.11), channel_id=1, source_target_pairs={{8,0},{16,8},{24,16},{9,1},{17,9},{25,17},{10,2},{18,10},{26,18},{... | collective-permute-start | bytes 1572872 | tf_op jit(solution)/shard_map/ppermute | solution.py:327
  134.2 14.6 %copy-start.8 = (f32[8,2,128,128]{3,2,1,0:T(8,128)S(1)}, f32[8,2,128,128]{3,2,1,0:T(8,128)}, u32[]{:S(2)}) copy-start(f32[8,2,128,128]{3,2,1,0:T(8,128)} %get-tuple-element.42) | copy-start | bytes 3145732
  152.7 24.5 %all-to-all-start.6 = ((bf16[8,6,128,128]{3,2,1,0:T(8,128)(2,1)}), bf16[8,6,128,128]{3,2,1,0:T(8,128)(2,1)S(1)}, u32[]{:S(2)}, u32[]{:S(2)}) async-start(bf16[8,6,128,128]{3,2,1,0:T(8,128)(2,1)} %pad_maximum_fusion.1), calls=%async_computation.6 | async-start | bytes 3145728 | tf_op jit(solution)/shard_map/all_to_all | solution.py:373
  156.3 1.4 copy-start.2
  157.7 1.2 copy-start.4
  (1 other events, 1.0 us)

commit v9 on v8

--- a/solution.py
+++ b/solution.py
@@ -120,7 +120,7 @@
     nt = (((1,), (1,)), ((), ()))
     tn = (((0,), (0,)), ((), ()))
     block = half // 2 * rows
-    tile = 2 * HEAD_DIM
+    tile = slab
     tiles = range(3 * slab // tile)
     blocks = [(y, piece) for y in range(2) for piece in range(2)]
 
@@ -221,6 +221,8 @@
         skip = target[1] // 2
         into = pl.BlockSpec((parts, 2, rows, HEAD_DIM), lambda h: (0, skip + h, 0, 0))
     operands = [(place, a) for place in (qc, kv, kv_prev) for a in range(2)]
+    alone = kv[0].shape[1] == 2 * count
+    held = [(place, place is qc or (place is kv and not alone)) for place, _ in operands]
     return pl.pallas_call(
         attention_body,
         grid=(count,),
@@ -250,8 +252,8 @@
         ),
         name="attention",
     )(
-        *in_hbm([bias, classes] + [place[0] for place, _ in operands[:4]]),
-        *[place[0] for place, _ in operands[4:]],
+        *in_hbm([bias, classes]),
+        *[in_hbm([place[0]])[0] if pinned else place[0] for place, pinned in held],
         *([] if target is None else [target[0]]),
     )
 

time: 181 us -> 181 us (level)
    unnamed x24 -> x20, local copies, waits for them, and re-layouts: 4.6 us -> 3.63 us
  transfers between devices with their start and end apart: 13 -> 13, of which waited for: 8 -> 8; matrix products, arithmetic and copies ran while one was open for 8% -> 9% of each run, Pallas kernels for 24% -> 24%
where the time goes in v9:
time: 181 us; the launch traced here: 179 us
  waiting for transfers between devices  67 us (37%)
  Pallas kernels  46.9 us (26%)
  starting transfers between devices  45.2 us (25%)
  local copies, waits for them, and re-layouts  9.61 us (5%)
  other arithmetic  9.51 us (5%)
    all_to_all x7, waiting for transfers between devices, on_device(): lax.all_to_all(buffer, group, split_axis=0, concat_axis=0, tiled=True)  53.6 us
    pallas_call x3, Pallas kernels, attention(): pl.pallas_call(attention_body, grid=(count,), out_shape=[hbm(shape if tar...  36.7 us
    all_to_all x7, starting transfers between devices, on_device(): lax.all_to_all(buffer, group, split_axis=0, concat_axis=0, tiled=True)  28.8 us
    ppermute x3, waiting for transfers between devices, work_on(): owed.append((dkv, lax.ppermute(dkv_prev, 'plane', down)))  13.5 us
    ppermute x3, starting transfers between devices, on_device(): shifted.append(lax.ppermute(moved, 'plane', up))  12.5 us
    pallas_call x2, Pallas kernels, pack(): pl.pallas_call(body, grid=(STEPS,), out_shape=[hbm((members, room, tokens...  6.77 us
    slice x2, local copies, waits for them, and re-layouts, on_device(): moved = buffer[:, slot:slot + 2 * counts[i]]  4.2 us
    convert_element_type x3, other arithmetic, returned(): return (dkv + dkv_next.astype(jnp.float32)).astype(jnp.bfloat16)  3.97 us
  transfers between devices with their start and end apart: 13, of which 8 were waited for; matrix products, arithmetic and copies ran while one was open for 9% of the time, Pallas kernels for 24%

profile of v9, /device:TPU:0, one launch (start us, length us, event | category | flops | bytes accessed | tf_op | source)
XLA Modules:
  0.0 179.3 jit_solution(5480136494304782865)
XLA Ops:
  0.6 2.6 %pack.3 = bf16[8,4,128,128]{3,2,1,0:T(8,128)(2,1)} custom-call(bf16[128,5120]{1,0:T(8,128)(2,1)} %bitcast.18, bf16[128,5120]{1,0:T(8,128)(2,1)} %bitcast.20), custom_call_target="tpu_custom_call" | custom-call | bytes 5242880 | tf_op jit(solution)/shard_map/pack/pallas_call | solution.py:60
  3.2 5.3 %all-to-all-start = ((bf16[8,4,128,128]{3,2,1,0:T(8,128)(2,1)}), bf16[8,4,128,128]{3,2,1,0:T(8,128)(2,1)S(1)}, u32[]{:S(2)}, u32[]{:S(2)}) async-start(bf16[8,4,128,128]{3,2,1,0:T(8,128)(2,1)} %pack.3), calls=%async_computation | async-start | bytes 2097152 | tf_op jit(solution)/shard_map/all_to_all | solution.py:375
  8.8 4.2 %pack.2 = (bf16[8,8,128,128]{3,2,1,0:T(8,128)(2,1)}, bf16[8,6,128,128]{3,2,1,0:T(8,128)(2,1)}, bf16[8,6,128,128]{3,2,1,0:T(8,128)(2,1)}) custom-call(bf16[128,5120]{1,0:T(8,128)(2,1)} %bitcast.19, bf16[128,5120]{1,0:T(8,128)(2,1)} %bitcast.21, bf16[128,5120]{1,0:T(8,128)(2,1)} %bitcast.22, bf16[128,5120]{1,0:T(8,128)(2,1)} %bitcast.23), custom_call_target="tpu_custom_call" | custom-call | bytes 10485760 | tf_op jit(solution)/shard_map/pack/pallas_call | solution.py:60
  13.2 10.8 %all-to-all-done.kc_ref.vc_ref = bf16[8,4,128,128]{3,2,1,0:T(8,128)(2,1)S(1)} async-done(((bf16[8,4,128,128]{3,2,1,0:T(8,128)(2,1)}), bf16[8,4,128,128]{3,2,1,0:T(8,128)(2,1)S(1)}, u32[]{:S(2)}, u32[]{:S(2)}) %all-to-all-start) | async-done | bytes 1048608 | tf_op jit(solution)/shard_map/all_to_all | solution.py:375
  23.9 4.4 %all-to-all-start.1 = ((bf16[8,8,128,128]{3,2,1,0:T(8,128)(2,1)}), bf16[8,8,128,128]{3,2,1,0:T(8,128)(2,1)}, u32[]{:S(2)}, u32[]{:S(2)}) async-start(bf16[8,8,128,128]{3,2,1,0:T(8,128)(2,1)} %get-tuple-element.30), calls=%async_computation.1 | async-start | bytes 4194304 | tf_op jit(solution)/shard_map/all_to_all | solution.py:375
  29.7 3.6 %collective-permute-start = (bf16[8,4,128,128]{3,2,1,0:T(8,128)(2,1)S(1)}, bf16[8,4,128,128]{3,2,1,0:T(8,128)(2,1)S(1)}, u32[]{:S(2)}, u32[]{:S(2)}) collective-permute-start(bf16[8,4,128,128]{3,2,1,0:T(8,128)(2,1)S(1)} %all-to-all-done.kc_ref.vc_ref), channel_id=1, source_target_pairs={{0,8},{8,16},{16,24},{1,9},{9,17},{17,25},{2,10},{10,18},{18,26},{... | collective-permute-start | bytes 3145736 | tf_op jit(solution)/shard_map/ppermute | solution.py:382
  33.3 2.0 %fusion.16.class_ref = bf16[512,128]{1,0:T(8,128)(2,1)} fusion(s32[512]{0:T(512)S(1)} %get-tuple-element.56, s32[512]{0:T(512)S(1)} %get-tuple-element.62, s32[512]{0:T(512)S(1)} %get-tuple-element.57, s32[512]{0:T(512)S(1)} %get-tuple-element.59, s32[512]{0:T(512)S(1)} %get-tuple-element.58, s32[512]{0:T(512)S(1)} %get-tuple-element.63, ...), kind=kLoop, calls=%fused_computation.40 | loop fusion | flops 3276800 | bytes 144896 | tf_op jit(solution)/shard_map/convert_element_type | solution.py:294
  36.3 18.7 %all-to-all-done.1.q_ref.c_ref.kc_ref.vc_ref = bf16[8,8,128,128]{3,2,1,0:T(8,128)(2,1)} async-done(((bf16[8,8,128,128]{3,2,1,0:T(8,128)(2,1)}), bf16[8,8,128,128]{3,2,1,0:T(8,128)(2,1)}, u32[]{:S(2)}, u32[]{:S(2)}) %all-to-all-start.1) | async-done | bytes 2097184 | tf_op jit(solution)/shard_map/all_to_all | solution.py:375
  55.0 4.3 %all-to-all-start.2 = ((bf16[8,6,128,128]{3,2,1,0:T(8,128)(2,1)}), bf16[8,6,128,128]{3,2,1,0:T(8,128)(2,1)}, u32[]{:S(2)}, u32[]{:S(2)}) async-start(bf16[8,6,128,128]{3,2,1,0:T(8,128)(2,1)} %get-tuple-element.35), calls=%async_computation.2 | async-start | bytes 3145728 | tf_op jit(solution)/shard_map/all_to_all | solution.py:375
  59.3 2.3 %slice.20 = bf16[8,4,128,128]{3,2,1,0:T(8,128)(2,1)} slice(bf16[8,8,128,128]{3,2,1,0:T(8,128)(2,1)} %all-to-all-done.1.q_ref.c_ref.kc_ref.vc_ref), slice={[0:8], [0:4], [0:128], [0:128]} | slice | bytes 2097152 | tf_op jit(solution)/shard_map/slice | solution.py:381
  61.6 3.5 %collective-permute-start.1 = (bf16[8,4,128,128]{3,2,1,0:T(8,128)(2,1)}, bf16[8,4,128,128]{3,2,1,0:T(8,128)(2,1)S(1)}, u32[]{:S(2)}, u32[]{:S(2)}) collective-permute-start(bf16[8,4,128,128]{3,2,1,0:T(8,128)(2,1)} %slice.20), channel_id=1, source_target_pairs={{0,8},{8,16},{16,24},{1,9},{9,17},{17,25},{2,10},{10,18},{18,26},{... | collective-permute-start | bytes 3145736 | tf_op jit(solution)/shard_map/ppermute | solution.py:382
  65.2 14.0 %attention.3 = (bf16[8,6,128,128]{3,2,1,0:T(8,128)(2,1)}, f32[8,4,128,128]{3,2,1,0:T(8,128)}, bf16[8,4,128,128]{3,2,1,0:T(8,128)(2,1)}) custom-call(bf16[2,1536,128]{2,1,0:T(8,128)(2,1)} %bitcast.24, bf16[512,128]{1,0:T(8,128)(2,1)} %fusion.16.class_ref, ...), custom_call_target="tpu_custom_call", output_to_operand_aliasing={{0}: (8, {})} | custom-call | flops 9663676416 | bytes 9437184 | tf_op jit(solution)/shard_map/attention/pallas_call | solution.py:226
  80.3 3.6 %all-to-all-start.3 = ((bf16[8,6,128,128]{3,2,1,0:T(8,128)(2,1)}), bf16[8,6,128,128]{3,2,1,0:T(8,128)(2,1)S(1)}, u32[]{:S(2)}, u32[]{:S(2)}) async-start(bf16[8,6,128,128]{3,2,1,0:T(8,128)(2,1)} %get-tuple-element.36), calls=%async_computation.3 | async-start | bytes 3145728 | tf_op jit(solution)/shard_map/all_to_all | solution.py:375
  87.1 5.4 %collective-permute-start.2 = (bf16[8,2,128,128]{3,2,1,0:T(8,128)(2,1)}, bf16[8,2,128,128]{3,2,1,0:T(8,128)(2,1)}, u32[]{:S(2)}, u32[]{:S(2)}) collective-permute-start(bf16[8,2,128,128]{3,2,1,0:T(8,128)(2,1)} %slice.21), channel_id=1, source_target_pairs={{0,8},{8,16},{16,24},{1,9},{9,17},{17,25},{2,10},{10,18},{18,26},{... | collective-permute-start | bytes 1572872 | tf_op jit(solution)/shard_map/ppermute | solution.py:382
  92.5 14.1 %attention.4 = (bf16[8,4,128,128]{3,2,1,0:T(8,128)(2,1)}, f32[8,4,128,128]{3,2,1,0:T(8,128)}, bf16[8,4,128,128]{3,2,1,0:T(8,128)(2,1)}) custom-call(bf16[2,1536,128]{2,1,0:T(8,128)(2,1)} %bitcast.25, bf16[512,128]{1,0:T(8,128)(2,1)} %fusion.16.class_ref, bf16[8,6,128,128]{3,2,1,0:T(8,128)(2,1)} %all-to-all-done.2.q_ref.c_ref.kc_ref.vc_ref, ...), custom_call_target="tpu_custom_call" | custom-call | flops 9663676416 | bytes 9437184 | tf_op jit(solution)/shard_map/attention/pallas_call | solution.py:226
  108.0 4.1 %all-to-all-start.4 = ((bf16[8,4,128,128]{3,2,1,0:T(8,128)(2,1)}), bf16[8,4,128,128]{3,2,1,0:T(8,128)(2,1)S(1)}, u32[]{:S(2)}, u32[]{:S(2)}) async-start(bf16[8,4,128,128]{3,2,1,0:T(8,128)(2,1)} %get-tuple-element.38), calls=%async_computation.4 | async-start | bytes 2097152 | tf_op jit(solution)/shard_map/all_to_all | solution.py:375
  112.1 8.6 %attention.5 = (bf16[8,2,128,128]{3,2,1,0:T(8,128)(2,1)}, f32[8,2,128,128]{3,2,1,0:T(8,128)}, bf16[8,2,128,128]{3,2,1,0:T(8,128)(2,1)}) custom-call(bf16[2,1536,128]{2,1,0:T(8,128)(2,1)} %bitcast.26, bf16[512,128]{1,0:T(8,128)(2,1)} %fusion.16.class_ref, bf16[8,6,128,128]{3,2,1,0:T(8,128)(2,1)} %copy-done.1, bf16[8,6,128,128]{3,2,1,0:T(8,128)(2,1)} %copy-done.1, ...), custom_call_target="tpu_custom_call" | custom-call | flops 4831838208 | bytes 4718592 | tf_op jit(solution)/shard_map/attention/pallas_call | solution.py:226
  123.6 3.8 %all-to-all-done.4.refs_1_ = bf16[8,4,128,128]{3,2,1,0:T(8,128)(2,1)S(1)} async-done(((bf16[8,4,128,128]{3,2,1,0:T(8,128)(2,1)}), bf16[8,4,128,128]{3,2,1,0:T(8,128)(2,1)S(1)}, u32[]{:S(2)}, u32[]{:S(2)}) %all-to-all-start.4) | async-done | bytes 1048608 | tf_op jit(solution)/shard_map/all_to_all | solution.py:375
  128.4 3.6 %all-to-all-start.5 = ((bf16[8,6,128,128]{3,2,1,0:T(8,128)(2,1)}), bf16[8,6,128,128]{3,2,1,0:T(8,128)(2,1)S(1)}, u32[]{:S(2)}, u32[]{:S(2)}) async-start(bf16[8,6,128,128]{3,2,1,0:T(8,128)(2,1)} %pad_maximum_fusion), calls=%async_computation.5 | async-start | bytes 3145728 | tf_op jit(solution)/shard_map/all_to_all | solution.py:375
  134.0 2.2 %add_convert_fusion = bf16[8,4,128,128]{3,2,1,0:T(8,128)(2,1)S(1)} fusion(f32[8,4,128,128]{3,2,1,0:T(8,128)} %get-tuple-element.47, bf16[8,4,128,128]{3,2,1,0:T(8,128)(2,1)} %collective-permute-done.4), kind=kLoop, calls=%fused_computation | loop fusion | flops 1572864 | bytes 4194304 | tf_op jit(solution)/shard_map/convert_element_type | solution.py:335
  136.3 12.8 %collective-permute-done.5 = bf16[8,2,128,128]{3,2,1,0:T(8,128)(2,1)S(1)} collective-permute-done((bf16[8,2,128,128]{3,2,1,0:T(8,128)(2,1)S(1)}, bf16[8,2,128,128]{3,2,1,0:T(8,128)(2,1)S(1)}, u32[]{:S(2)}, u32[]{:S(2)}) %collective-permute-start.5) | collective-permute-done | bytes 524320 | tf_op jit(solution)/shard_map/ppermute | solution.py:329
  150.5 2.5 %all-to-all-done.5.refs_2_.refs_0_ = bf16[8,6,128,128]{3,2,1,0:T(8,128)(2,1)S(1)} async-done(((bf16[8,6,128,128]{3,2,1,0:T(8,128)(2,1)}), bf16[8,6,128,128]{3,2,1,0:T(8,128)(2,1)S(1)}, u32[]{:S(2)}, u32[]{:S(2)}) %all-to-all-start.5) | async-done | bytes 1572896 | tf_op jit(solution)/shard_map/all_to_all | solution.py:375
  153.0 3.6 %all-to-all-start.6 = ((bf16[8,6,128,128]{3,2,1,0:T(8,128)(2,1)}), bf16[8,6,128,128]{3,2,1,0:T(8,128)(2,1)S(1)}, u32[]{:S(2)}, u32[]{:S(2)}) async-start(bf16[8,6,128,128]{3,2,1,0:T(8,128)(2,1)} %pad_maximum_fusion.1), calls=%async_computation.6 | async-start | bytes 3145728 | tf_op jit(solution)/shard_map/all_to_all | solution.py:375
  160.9 16.6 %all-to-all-done.6.refs_1_ = bf16[8,6,128,128]{3,2,1,0:T(8,128)(2,1)S(1)} async-done(((bf16[8,6,128,128]{3,2,1,0:T(8,128)(2,1)}), bf16[8,6,128,128]{3,2,1,0:T(8,128)(2,1)S(1)}, u32[]{:S(2)}, u32[]{:S(2)}) %all-to-all-start.6) | async-done | bytes 1572896 | tf_op jit(solution)/shard_map/all_to_all | solution.py:375
  (68 shorter events, 21.7 us)
Async XLA Ops:
  0.6 12.4 %copy-start = (s32[8,2,2,10]{3,2,1,0:T(2,128)S(1)}, s32[8,2,2,10]{3,2,1,0:T(2,128)}, u32[]{:S(2)}) copy-start(s32[8,2,2,10]{3,2,1,0:T(2,128)} %param.11) | copy-start | bytes 3844
  3.2 5.3 %copy-start.8 = (s32[16]{0:T(128)S(1)}, s32[16]{0:T(128)}, u32[]{:S(2)}) copy-start(s32[16]{0:T(128)} %param.10) | copy-start | bytes 196
  3.2 20.7 %all-to-all-start = ((bf16[8,4,128,128]{3,2,1,0:T(8,128)(2,1)}), bf16[8,4,128,128]{3,2,1,0:T(8,128)(2,1)S(1)}, u32[]{:S(2)}, u32[]{:S(2)}) async-start(bf16[8,4,128,128]{3,2,1,0:T(8,128)(2,1)} %pack.3), calls=%async_computation | async-start | bytes 2097152 | tf_op jit(solution)/shard_map/all_to_all | solution.py:375
  23.9 31.0 %all-to-all-start.1 = ((bf16[8,8,128,128]{3,2,1,0:T(8,128)(2,1)}), bf16[8,8,128,128]{3,2,1,0:T(8,128)(2,1)}, u32[]{:S(2)}, u32[]{:S(2)}) async-start(bf16[8,8,128,128]{3,2,1,0:T(8,128)(2,1)} %get-tuple-element.30), calls=%async_computation.1 | async-start | bytes 4194304 | tf_op jit(solution)/shard_map/all_to_all | solution.py:375
  29.7 35.5 %collective-permute-start = (bf16[8,4,128,128]{3,2,1,0:T(8,128)(2,1)S(1)}, bf16[8,4,128,128]{3,2,1,0:T(8,128)(2,1)S(1)}, u32[]{:S(2)}, u32[]{:S(2)}) collective-permute-start(bf16[8,4,128,128]{3,2,1,0:T(8,128)(2,1)S(1)} %all-to-all-done.kc_ref.vc_ref), channel_id=1, source_target_pairs={{0,8},{8,16},{16,24},{1,9},{9,17},{17,25},{2,10},{10,18},{18,26},{... | collective-permute-start | bytes 3145736 | tf_op jit(solution)/shard_map/ppermute | solution.py:382
  55.0 25.3 %all-to-all-start.2 = ((bf16[8,6,128,128]{3,2,1,0:T(8,128)(2,1)}), bf16[8,6,128,128]{3,2,1,0:T(8,128)(2,1)}, u32[]{:S(2)}, u32[]{:S(2)}) async-start(bf16[8,6,128,128]{3,2,1,0:T(8,128)(2,1)} %get-tuple-element.35), calls=%async_computation.2 | async-start | bytes 3145728 | tf_op jit(solution)/shard_map/all_to_all | solution.py:375
  61.6 30.9 %collective-permute-start.1 = (bf16[8,4,128,128]{3,2,1,0:T(8,128)(2,1)}, bf16[8,4,128,128]{3,2,1,0:T(8,128)(2,1)S(1)}, u32[]{:S(2)}, u32[]{:S(2)}) collective-permute-start(bf16[8,4,128,128]{3,2,1,0:T(8,128)(2,1)} %slice.20), channel_id=1, source_target_pairs={{0,8},{8,16},{16,24},{1,9},{9,17},{17,25},{2,10},{10,18},{18,26},{... | collective-permute-start | bytes 3145736 | tf_op jit(solution)/shard_map/ppermute | solution.py:382
  80.3 27.6 %all-to-all-start.3 = ((bf16[8,6,128,128]{3,2,1,0:T(8,128)(2,1)}), bf16[8,6,128,128]{3,2,1,0:T(8,128)(2,1)S(1)}, u32[]{:S(2)}, u32[]{:S(2)}) async-start(bf16[8,6,128,128]{3,2,1,0:T(8,128)(2,1)} %get-tuple-element.36), calls=%async_computation.3 | async-start | bytes 3145728 | tf_op jit(solution)/shard_map/all_to_all | solution.py:375
  83.9 36.8 %collective-permute-start.3 = (bf16[8,4,128,128]{3,2,1,0:T(8,128)(2,1)}, bf16[8,4,128,128]{3,2,1,0:T(8,128)(2,1)}, u32[]{:S(2)}, u32[]{:S(2)}) collective-permute-start(bf16[8,4,128,128]{3,2,1,0:T(8,128)(2,1)} %get-tuple-element.41), channel_id=1, source_target_pairs={{8,0},{16,8},{24,16},{9,1},{17,9},{25,17},{10,2},{18,10},{26,18},{... | collective-permute-start | bytes 3145736 | tf_op jit(solution)/shard_map/ppermute | solution.py:329
  87.1 25.0 %collective-permute-start.2 = (bf16[8,2,128,128]{3,2,1,0:T(8,128)(2,1)}, bf16[8,2,128,128]{3,2,1,0:T(8,128)(2,1)}, u32[]{:S(2)}, u32[]{:S(2)}) collective-permute-start(bf16[8,2,128,128]{3,2,1,0:T(8,128)(2,1)} %slice.21), channel_id=1, source_target_pairs={{0,8},{8,16},{16,24},{1,9},{9,17},{17,25},{2,10},{10,18},{18,26},{... | collective-permute-start | bytes 1572872 | tf_op jit(solution)/shard_map/ppermute | solution.py:382
  106.7 27.4 %collective-permute-start.4 = (bf16[8,4,128,128]{3,2,1,0:T(8,128)(2,1)}, bf16[8,4,128,128]{3,2,1,0:T(8,128)(2,1)}, u32[]{:S(2)}, u32[]{:S(2)}) collective-permute-start(bf16[8,4,128,128]{3,2,1,0:T(8,128)(2,1)} %get-tuple-element.48), channel_id=1, source_target_pairs={{8,0},{16,8},{24,16},{9,1},{17,9},{25,17},{10,2},{18,10},{26,18},{... | collective-permute-start | bytes 3145736 | tf_op jit(solution)/shard_map/ppermute | solution.py:329
  108.0 4.1 %copy-start.1 = (bf16[8,6,128,128]{3,2,1,0:T(8,128)(2,1)}, bf16[8,6,128,128]{3,2,1,0:T(8,128)(2,1)S(1)}, u32[]{:S(2)}) copy-start(bf16[8,6,128,128]{3,2,1,0:T(8,128)(2,1)S(1)} %all-to-all-done.3.q_ref.c_ref.refs_0_) | copy-start | bytes 4718596
  108.0 19.5 %all-to-all-start.4 = ((bf16[8,4,128,128]{3,2,1,0:T(8,128)(2,1)}), bf16[8,4,128,128]{3,2,1,0:T(8,128)(2,1)S(1)}, u32[]{:S(2)}, u32[]{:S(2)}) async-start(bf16[8,4,128,128]{3,2,1,0:T(8,128)(2,1)} %get-tuple-element.38), calls=%async_computation.4 | async-start | bytes 2097152 | tf_op jit(solution)/shard_map/all_to_all | solution.py:375
  112.1 8.6 %copy-start.5 = (f32[8,4,128,128]{3,2,1,0:T(8,128)S(1)}, f32[8,4,128,128]{3,2,1,0:T(8,128)}, u32[]{:S(2)}) copy-start(f32[8,4,128,128]{3,2,1,0:T(8,128)} %get-tuple-element.40) | copy-start | bytes 6291460
  120.7 1.6 copy-start.7
  123.6 8.4 %copy-start.9 = (bf16[8,2,128,128]{3,2,1,0:T(8,128)(2,1)S(1)}, bf16[8,2,128,128]{3,2,1,0:T(8,128)(2,1)}, u32[]{:S(2)}) copy-start(bf16[8,2,128,128]{3,2,1,0:T(8,128)(2,1)} %get-tuple-element.50) | copy-start | bytes 1572868
  127.5 1.0 copy-start.3
  128.4 24.5 %all-to-all-start.5 = ((bf16[8,6,128,128]{3,2,1,0:T(8,128)(2,1)}), bf16[8,6,128,128]{3,2,1,0:T(8,128)(2,1)S(1)}, u32[]{:S(2)}, u32[]{:S(2)}) async-start(bf16[8,6,128,128]{3,2,1,0:T(8,128)(2,1)} %pad_maximum_fusion), calls=%async_computation.5 | async-start | bytes 3145728 | tf_op jit(solution)/shard_map/all_to_all | solution.py:375
  132.0 17.0 %collective-permute-start.5 = (bf16[8,2,128,128]{3,2,1,0:T(8,128)(2,1)S(1)}, bf16[8,2,128,128]{3,2,1,0:T(8,128)(2,1)S(1)}, u32[]{:S(2)}, u32[]{:S(2)}) collective-permute-start(bf16[8,2,128,128]{3,2,1,0:T(8,128)(2,1)S(1)} %copy-done.9), channel_id=1, source_target_pairs={{8,0},{16,8},{24,16},{9,1},{17,9},{25,17},{10,2},{18,10},{26,18},{... | collective-permute-start | bytes 1572872 | tf_op jit(solution)/shard_map/ppermute | solution.py:329
  134.0 15.0 %copy-start.6 = (f32[8,2,128,128]{3,2,1,0:T(8,128)S(1)}, f32[8,2,128,128]{3,2,1,0:T(8,128)}, u32[]{:S(2)}) copy-start(f32[8,2,128,128]{3,2,1,0:T(8,128)} %get-tuple-element.42) | copy-start | bytes 3145732
  153.0 24.5 %all-to-all-start.6 = ((bf16[8,6,128,128]{3,2,1,0:T(8,128)(2,1)}), bf16[8,6,128,128]{3,2,1,0:T(8,128)(2,1)S(1)}, u32[]{:S(2)}, u32[]{:S(2)}) async-start(bf16[8,6,128,128]{3,2,1,0:T(8,128)(2,1)} %pad_maximum_fusion.1), calls=%async_computation.6 | async-start | bytes 3145728 | tf_op jit(solution)/shard_map/all_to_all | solution.py:375
  156.6 1.4 copy-start.2
  158.0 1.2 copy-start.4

commit v10 on v9

--- a/solution.py
+++ b/solution.py
@@ -16,15 +16,15 @@
 TPS = 4
 K_NB = 10
 MASKED = -1e30
-CHUNKS = (2, 2, 1)
+CHUNKS = (2, 1, 2)
 ORDER = (
     (("kv", 0),),
     (("kv", 1), ("qc", 0)),
     (("kv", 2), ("qc", 1)),
     (("qc", 2), ("o", 0)),
-    (("o", 1),),
-    (("o", 2), ("d", 0)),
-    (("d", 1), ("d", 2)),
+    (("o", 1), ("d", 0)),
+    (("o", 2), ("d", 1)),
+    (("d", 2),),
 )
 VMEM_LIMIT = 32 * 1024 * 1024
 

time: 181 us -> 187 us (1.033)
  waiting for transfers between devices: 67 us -> 73.9 us
    all_to_all x7, waiting for transfers between devices: 53.6 us -> 40.7 us  [on_device(): lax.all_to_all(buffer, group, split_axis=0, concat_axis=0, tiled=True)]
    ppermute x3, waiting for transfers between devices: 0.01 us -> 12.6 us  [on_device(): shifted.append(lax.ppermute(moved, 'plane', up))]
    ppermute x3, waiting for transfers between devices: 13.5 us -> 20.6 us  [work_on(): owed.append((dkv, lax.ppermute(dkv_prev, 'plane', down)))]
  transfers between devices with their start and end apart: 13 -> 13, of which waited for: 8 -> 8; matrix products, arithmetic and copies ran while one was open for 9% -> 8% of each run, Pallas kernels for 24% -> 23%
where the time goes in v10:
time: 187 us; the launch traced here: 186 us
  waiting for transfers between devices  73.9 us (40%)
  Pallas kernels  47.7 us (26%)
  starting transfers between devices  45.8 us (24%)
  other arithmetic  9.06 us (5%)
  local copies, waits for them, and re-layouts  8.84 us (5%)
    all_to_all x7, waiting for transfers between devices, on_device(): lax.all_to_all(buffer, group, split_axis=0, concat_axis=0, tiled=True)  40.7 us
    pallas_call x3, Pallas kernels, attention(): pl.pallas_call(attention_body, grid=(count,), out_shape=[hbm(shape if tar...  36.3 us
    all_to_all x7, starting transfers between devices, on_device(): lax.all_to_all(buffer, group, split_axis=0, concat_axis=0, tiled=True)  29.7 us
    ppermute x3, waiting for transfers between devices, work_on(): owed.append((dkv, lax.ppermute(dkv_prev, 'plane', down)))  20.6 us
    ppermute x3, waiting for transfers between devices, on_device(): shifted.append(lax.ppermute(moved, 'plane', up))  12.6 us
    ppermute x3, starting transfers between devices, on_device(): shifted.append(lax.ppermute(moved, 'plane', up))  12 us
    pallas_call x2, Pallas kernels, pack(): pl.pallas_call(body, grid=(STEPS,), out_shape=[hbm((members, room, tokens...  6.89 us
    pallas_call x2, Pallas kernels, unpack(): pl.pallas_call(body, grid=(STEPS,), out_shape=[jax.ShapeDtypeStruct((toke...  4.46 us
  transfers between devices with their start and end apart: 13, of which 8 were waited for; matrix products, arithmetic and copies ran while one was open for 8% of the time, Pallas kernels for 23%

profile of v10, /device:TPU:0, one launch (start us, length us, event | category | flops | bytes accessed | tf_op | source)
XLA Modules:
  0.0 186.2 jit_solution(2913407318869036226)
XLA Ops:
  0.6 2.6 %pack.3 = bf16[8,4,128,128]{3,2,1,0:T(8,128)(2,1)} custom-call(bf16[128,5120]{1,0:T(8,128)(2,1)} %bitcast.18, bf16[128,5120]{1,0:T(8,128)(2,1)} %bitcast.20), custom_call_target="tpu_custom_call" | custom-call | bytes 5242880 | tf_op jit(solution)/shard_map/pack/pallas_call | solution.py:60
  3.2 5.3 %all-to-all-start = ((bf16[8,4,128,128]{3,2,1,0:T(8,128)(2,1)}), bf16[8,4,128,128]{3,2,1,0:T(8,128)(2,1)S(1)}, u32[]{:S(2)}, u32[]{:S(2)}) async-start(bf16[8,4,128,128]{3,2,1,0:T(8,128)(2,1)} %pack.3), calls=%async_computation | async-start | bytes 2097152 | tf_op jit(solution)/shard_map/all_to_all | solution.py:375
  8.9 4.3 %pack.2 = (bf16[8,6,128,128]{3,2,1,0:T(8,128)(2,1)}, bf16[8,6,128,128]{3,2,1,0:T(8,128)(2,1)}, bf16[8,8,128,128]{3,2,1,0:T(8,128)(2,1)}) custom-call(bf16[128,5120]{1,0:T(8,128)(2,1)} %bitcast.19, bf16[128,5120]{1,0:T(8,128)(2,1)} %bitcast.21, bf16[128,5120]{1,0:T(8,128)(2,1)} %bitcast.22, bf16[128,5120]{1,0:T(8,128)(2,1)} %bitcast.23), custom_call_target="tpu_custom_call" | custom-call | bytes 10485760 | tf_op jit(solution)/shard_map/pack/pallas_call | solution.py:60
  13.4 10.5 %all-to-all-done.kc_ref.vc_ref = bf16[8,4,128,128]{3,2,1,0:T(8,128)(2,1)S(1)} async-done(((bf16[8,4,128,128]{3,2,1,0:T(8,128)(2,1)}), bf16[8,4,128,128]{3,2,1,0:T(8,128)(2,1)S(1)}, u32[]{:S(2)}, u32[]{:S(2)}) %all-to-all-start) | async-done | bytes 1048608 | tf_op jit(solution)/shard_map/all_to_all | solution.py:375
  23.9 4.3 %all-to-all-start.1 = ((bf16[8,6,128,128]{3,2,1,0:T(8,128)(2,1)}), bf16[8,6,128,128]{3,2,1,0:T(8,128)(2,1)}, u32[]{:S(2)}, u32[]{:S(2)}) async-start(bf16[8,6,128,128]{3,2,1,0:T(8,128)(2,1)} %get-tuple-element.30), calls=%async_computation.1 | async-start | bytes 3145728 | tf_op jit(solution)/shard_map/all_to_all | solution.py:375
  29.5 3.5 %collective-permute-start = (bf16[8,4,128,128]{3,2,1,0:T(8,128)(2,1)S(1)}, bf16[8,4,128,128]{3,2,1,0:T(8,128)(2,1)S(1)}, u32[]{:S(2)}, u32[]{:S(2)}) collective-permute-start(bf16[8,4,128,128]{3,2,1,0:T(8,128)(2,1)S(1)} %all-to-all-done.kc_ref.vc_ref), channel_id=1, source_target_pairs={{0,8},{8,16},{16,24},{1,9},{9,17},{17,25},{2,10},{10,18},{18,26},{... | collective-permute-start | bytes 3145736 | tf_op jit(solution)/shard_map/ppermute | solution.py:382
  36.1 13.2 %all-to-all-done.1.q_ref.c_ref.kc_ref.vc_ref = bf16[8,6,128,128]{3,2,1,0:T(8,128)(2,1)} async-done(((bf16[8,6,128,128]{3,2,1,0:T(8,128)(2,1)}), bf16[8,6,128,128]{3,2,1,0:T(8,128)(2,1)}, u32[]{:S(2)}, u32[]{:S(2)}) %all-to-all-start.1) | async-done | bytes 1572896 | tf_op jit(solution)/shard_map/all_to_all | solution.py:375
  49.3 4.3 %all-to-all-start.2 = ((bf16[8,6,128,128]{3,2,1,0:T(8,128)(2,1)}), bf16[8,6,128,128]{3,2,1,0:T(8,128)(2,1)}, u32[]{:S(2)}, u32[]{:S(2)}) async-start(bf16[8,6,128,128]{3,2,1,0:T(8,128)(2,1)} %get-tuple-element.35), calls=%async_computation.2 | async-start | bytes 3145728 | tf_op jit(solution)/shard_map/all_to_all | solution.py:375
  55.9 14.0 %attention.3 = (bf16[8,8,128,128]{3,2,1,0:T(8,128)(2,1)}, f32[8,4,128,128]{3,2,1,0:T(8,128)}, bf16[8,4,128,128]{3,2,1,0:T(8,128)(2,1)}) custom-call(bf16[2,1536,128]{2,1,0:T(8,128)(2,1)} %bitcast.24, bf16[512,128]{1,0:T(8,128)(2,1)} %fusion.16.class_ref, ...), custom_call_target="tpu_custom_call", output_to_operand_aliasing={{0}: (8, {})} | custom-call | flops 9663676416 | bytes 9437184 | tf_op jit(solution)/shard_map/attention/pallas_call | solution.py:226
  69.8 4.8 %all-to-all-done.2.q_ref.c_ref.kc_ref.vc_ref = bf16[8,6,128,128]{3,2,1,0:T(8,128)(2,1)} async-done(((bf16[8,6,128,128]{3,2,1,0:T(8,128)(2,1)}), bf16[8,6,128,128]{3,2,1,0:T(8,128)(2,1)}, u32[]{:S(2)}, u32[]{:S(2)}) %all-to-all-start.2) | async-done | bytes 1572896 | tf_op jit(solution)/shard_map/all_to_all | solution.py:375
  74.6 3.6 %all-to-all-start.3 = ((bf16[8,8,128,128]{3,2,1,0:T(8,128)(2,1)}), bf16[8,8,128,128]{3,2,1,0:T(8,128)(2,1)S(1)}, u32[]{:S(2)}, u32[]{:S(2)}) async-start(bf16[8,8,128,128]{3,2,1,0:T(8,128)(2,1)} %get-tuple-element.36), calls=%async_computation.3 | async-start | bytes 4194304 | tf_op jit(solution)/shard_map/all_to_all | solution.py:375
  80.6 4.6 %collective-permute-start.1 = (bf16[8,2,128,128]{3,2,1,0:T(8,128)(2,1)S(1)}, bf16[8,2,128,128]{3,2,1,0:T(8,128)(2,1)S(1)}, u32[]{:S(2)}, u32[]{:S(2)}) collective-permute-start(bf16[8,2,128,128]{3,2,1,0:T(8,128)(2,1)S(1)} %slice.20), channel_id=1, source_target_pairs={{0,8},{8,16},{16,24},{1,9},{9,17},{17,25},{2,10},{10,18},{18,26},{... | collective-permute-start | bytes 1572872 | tf_op jit(solution)/shard_map/ppermute | solution.py:382
  87.6 3.8 %collective-permute-start.3 = (bf16[8,4,128,128]{3,2,1,0:T(8,128)(2,1)}, bf16[8,4,128,128]{3,2,1,0:T(8,128)(2,1)S(1)}, u32[]{:S(2)}, u32[]{:S(2)}) collective-permute-start(bf16[8,4,128,128]{3,2,1,0:T(8,128)(2,1)} %slice.21), channel_id=1, source_target_pairs={{0,8},{8,16},{16,24},{1,9},{9,17},{17,25},{2,10},{10,18},{18,26},{... | collective-permute-start | bytes 3145736 | tf_op jit(solution)/shard_map/ppermute | solution.py:382
  91.4 6.1 %collective-permute-done.1.kp_ref.vp_ref = bf16[8,2,128,128]{3,2,1,0:T(8,128)(2,1)S(1)} collective-permute-done((bf16[8,2,128,128]{3,2,1,0:T(8,128)(2,1)S(1)}, bf16[8,2,128,128]{3,2,1,0:T(8,128)(2,1)S(1)}, u32[]{:S(2)}, u32[]{:S(2)}) %collective-permute-start.1) | collective-permute-done | bytes 524320 | tf_op jit(solution)/shard_map/ppermute | solution.py:382
  97.5 8.3 %attention.4 = (bf16[8,2,128,128]{3,2,1,0:T(8,128)(2,1)}, f32[8,2,128,128]{3,2,1,0:T(8,128)}, bf16[8,2,128,128]{3,2,1,0:T(8,128)(2,1)}) custom-call(bf16[2,1536,128]{2,1,0:T(8,128)(2,1)} %bitcast.25, bf16[512,128]{1,0:T(8,128)(2,1)} %fusion.16.class_ref, bf16[8,6,128,128]{3,2,1,0:T(8,128)(2,1)} %all-to-all-done.2.q_ref.c_ref.kc_ref.vc_ref, ...), custom_call_target="tpu_custom_call" | custom-call | flops 4831838208 | bytes 4718592 | tf_op jit(solution)/shard_map/attention/pallas_call | solution.py:226
  109.5 4.1 %all-to-all-start.4 = ((bf16[8,6,128,128]{3,2,1,0:T(8,128)(2,1)}), bf16[8,6,128,128]{3,2,1,0:T(8,128)(2,1)S(1)}, u32[]{:S(2)}, u32[]{:S(2)}) async-start(bf16[8,6,128,128]{3,2,1,0:T(8,128)(2,1)} %pad_maximum_fusion), calls=%async_computation.4 | async-start | bytes 3145728 | tf_op jit(solution)/shard_map/all_to_all | solution.py:375
  115.0 4.2 %collective-permute-done.3.kp_ref.vp_ref = bf16[8,4,128,128]{3,2,1,0:T(8,128)(2,1)S(1)} collective-permute-done((bf16[8,4,128,128]{3,2,1,0:T(8,128)(2,1)}, bf16[8,4,128,128]{3,2,1,0:T(8,128)(2,1)S(1)}, u32[]{:S(2)}, u32[]{:S(2)}) %collective-permute-start.3) | collective-permute-done | bytes 1048608 | tf_op jit(solution)/shard_map/ppermute | solution.py:382
  119.2 14.1 %attention.5 = (bf16[8,4,128,128]{3,2,1,0:T(8,128)(2,1)}, f32[8,4,128,128]{3,2,1,0:T(8,128)}, bf16[8,4,128,128]{3,2,1,0:T(8,128)(2,1)}) custom-call(bf16[2,1536,128]{2,1,0:T(8,128)(2,1)} %bitcast.26, bf16[512,128]{1,0:T(8,128)(2,1)} %fusion.16.class_ref, bf16[8,8,128,128]{3,2,1,0:T(8,128)(2,1)} %copy-done.1, bf16[8,8,128,128]{3,2,1,0:T(8,128)(2,1)} %copy-done.1, ...), custom_call_target="tpu_custom_call" | custom-call | flops 9663676416 | bytes 9437184 | tf_op jit(solution)/shard_map/attention/pallas_call | solution.py:226
  136.2 3.9 %all-to-all-start.5 = ((bf16[8,6,128,128]{3,2,1,0:T(8,128)(2,1)}), bf16[8,6,128,128]{3,2,1,0:T(8,128)(2,1)S(1)}, u32[]{:S(2)}, u32[]{:S(2)}) async-start(bf16[8,6,128,128]{3,2,1,0:T(8,128)(2,1)} %pad_maximum_fusion.1), calls=%async_computation.5 | async-start | bytes 3145728 | tf_op jit(solution)/shard_map/all_to_all | solution.py:375
  140.1 20.5 %collective-permute-done.5 = bf16[8,4,128,128]{3,2,1,0:T(8,128)(2,1)} collective-permute-done((bf16[8,4,128,128]{3,2,1,0:T(8,128)(2,1)}, bf16[8,4,128,128]{3,2,1,0:T(8,128)(2,1)}, u32[]{:S(2)}, u32[]{:S(2)}) %collective-permute-start.5) | collective-permute-done | bytes 1048608 | tf_op jit(solution)/shard_map/ppermute | solution.py:329
  160.6 3.2 %add_convert_fusion = bf16[8,4,128,128]{3,2,1,0:T(8,128)(2,1)} fusion(f32[8,4,128,128]{3,2,1,0:T(8,128)} %get-tuple-element.45, bf16[8,4,128,128]{3,2,1,0:T(8,128)(2,1)} %collective-permute-done.5), kind=kLoop, calls=%fused_computation | loop fusion | flops 1572864 | bytes 4194304 | tf_op jit(solution)/shard_map/convert_element_type | solution.py:335
  163.7 4.3 %all-to-all-start.6 = ((bf16[8,4,128,128]{3,2,1,0:T(8,128)(2,1)}), bf16[8,4,128,128]{3,2,1,0:T(8,128)(2,1)}, u32[]{:S(2)}, u32[]{:S(2)}) async-start(bf16[8,4,128,128]{3,2,1,0:T(8,128)(2,1)} %add_convert_fusion), calls=%async_computation.6 | async-start | bytes 2097152 | tf_op jit(solution)/shard_map/all_to_all | solution.py:375
  171.3 12.1 %all-to-all-done.6.refs_2_ = bf16[8,4,128,128]{3,2,1,0:T(8,128)(2,1)} async-done(((bf16[8,4,128,128]{3,2,1,0:T(8,128)(2,1)}), bf16[8,4,128,128]{3,2,1,0:T(8,128)(2,1)}, u32[]{:S(2)}, u32[]{:S(2)}) %all-to-all-start.6) | async-done | bytes 1048608 | tf_op jit(solution)/shard_map/all_to_all | solution.py:375
  183.4 2.8 %unpack.3 = (bf16[128,5120]{1,0:T(8,128)(2,1)}, bf16[128,5120]{1,0:T(8,128)(2,1)}) custom-call(bf16[8,6,128,128]{3,2,1,0:T(8,128)(2,1)S(1)} %all-to-all-done.4.refs_1_.refs_0_, bf16[8,6,128,128]{3,2,1,0:T(8,128)(2,1)S(1)} %all-to-all-done.5.refs_2_.refs_1_, bf16[8,4,128,128]{3,2,1,0:T(8,128)(2,1)} %all-to-all-done.6.refs_2_), custom_call_target="tpu_custom_call" | custom-call | bytes 5242880 | tf_op jit(solution)/shard_map/unpack/pallas_call | solution.py:89
  (64 shorter events, 22.9 us)
Async XLA Ops:
  0.6 27.6 %copy-start = (s32[8,2,2,10]{3,2,1,0:T(2,128)S(1)}, s32[8,2,2,10]{3,2,1,0:T(2,128)}, u32[]{:S(2)}) copy-start(s32[8,2,2,10]{3,2,1,0:T(2,128)} %param.11) | copy-start | bytes 3844
  3.2 5.3 %copy-start.7 = (s32[16]{0:T(128)S(1)}, s32[16]{0:T(128)}, u32[]{:S(2)}) copy-start(s32[16]{0:T(128)} %param.10) | copy-start | bytes 196
  3.2 20.7 %all-to-all-start = ((bf16[8,4,128,128]{3,2,1,0:T(8,128)(2,1)}), bf16[8,4,128,128]{3,2,1,0:T(8,128)(2,1)S(1)}, u32[]{:S(2)}, u32[]{:S(2)}) async-start(bf16[8,4,128,128]{3,2,1,0:T(8,128)(2,1)} %pack.3), calls=%async_computation | async-start | bytes 2097152 | tf_op jit(solution)/shard_map/all_to_all | solution.py:375
  23.9 25.4 %all-to-all-start.1 = ((bf16[8,6,128,128]{3,2,1,0:T(8,128)(2,1)}), bf16[8,6,128,128]{3,2,1,0:T(8,128)(2,1)}, u32[]{:S(2)}, u32[]{:S(2)}) async-start(bf16[8,6,128,128]{3,2,1,0:T(8,128)(2,1)} %get-tuple-element.30), calls=%async_computation.1 | async-start | bytes 3145728 | tf_op jit(solution)/shard_map/all_to_all | solution.py:375
  29.5 26.4 %collective-permute-start = (bf16[8,4,128,128]{3,2,1,0:T(8,128)(2,1)S(1)}, bf16[8,4,128,128]{3,2,1,0:T(8,128)(2,1)S(1)}, u32[]{:S(2)}, u32[]{:S(2)}) collective-permute-start(bf16[8,4,128,128]{3,2,1,0:T(8,128)(2,1)S(1)} %all-to-all-done.kc_ref.vc_ref), channel_id=1, source_target_pairs={{0,8},{8,16},{16,24},{1,9},{9,17},{17,25},{2,10},{10,18},{18,26},{... | collective-permute-start | bytes 3145736 | tf_op jit(solution)/shard_map/ppermute | solution.py:382
  49.3 25.3 %all-to-all-start.2 = ((bf16[8,6,128,128]{3,2,1,0:T(8,128)(2,1)}), bf16[8,6,128,128]{3,2,1,0:T(8,128)(2,1)}, u32[]{:S(2)}, u32[]{:S(2)}) async-start(bf16[8,6,128,128]{3,2,1,0:T(8,128)(2,1)} %get-tuple-element.35), calls=%async_computation.2 | async-start | bytes 3145728 | tf_op jit(solution)/shard_map/all_to_all | solution.py:375
  74.6 33.5 %all-to-all-start.3 = ((bf16[8,8,128,128]{3,2,1,0:T(8,128)(2,1)}), bf16[8,8,128,128]{3,2,1,0:T(8,128)(2,1)S(1)}, u32[]{:S(2)}, u32[]{:S(2)}) async-start(bf16[8,8,128,128]{3,2,1,0:T(8,128)(2,1)} %get-tuple-element.36), calls=%async_computation.3 | async-start | bytes 4194304 | tf_op jit(solution)/shard_map/all_to_all | solution.py:375
  78.2 27.6 %collective-permute-start.2 = (bf16[8,4,128,128]{3,2,1,0:T(8,128)(2,1)}, bf16[8,4,128,128]{3,2,1,0:T(8,128)(2,1)S(1)}, u32[]{:S(2)}, u32[]{:S(2)}) collective-permute-start(bf16[8,4,128,128]{3,2,1,0:T(8,128)(2,1)} %get-tuple-element.39), channel_id=1, source_target_pairs={{8,0},{16,8},{24,16},{9,1},{17,9},{25,17},{10,2},{18,10},{26,18},{... | collective-permute-start | bytes 3145736 | tf_op jit(solution)/shard_map/ppermute | solution.py:329
  80.6 16.9 %collective-permute-start.1 = (bf16[8,2,128,128]{3,2,1,0:T(8,128)(2,1)S(1)}, bf16[8,2,128,128]{3,2,1,0:T(8,128)(2,1)S(1)}, u32[]{:S(2)}, u32[]{:S(2)}) collective-permute-start(bf16[8,2,128,128]{3,2,1,0:T(8,128)(2,1)S(1)} %slice.20), channel_id=1, source_target_pairs={{0,8},{8,16},{16,24},{1,9},{9,17},{17,25},{2,10},{10,18},{18,26},{... | collective-permute-start | bytes 1572872 | tf_op jit(solution)/shard_map/ppermute | solution.py:382
  87.6 18.2 %copy-start.3 = (f32[8,4,128,128]{3,2,1,0:T(8,128)S(1)}, f32[8,4,128,128]{3,2,1,0:T(8,128)}, u32[]{:S(2)}) copy-start(f32[8,4,128,128]{3,2,1,0:T(8,128)} %get-tuple-element.38) | copy-start | bytes 6291460
  87.6 31.6 %collective-permute-start.3 = (bf16[8,4,128,128]{3,2,1,0:T(8,128)(2,1)}, bf16[8,4,128,128]{3,2,1,0:T(8,128)(2,1)S(1)}, u32[]{:S(2)}, u32[]{:S(2)}) collective-permute-start(bf16[8,4,128,128]{3,2,1,0:T(8,128)(2,1)} %slice.21), channel_id=1, source_target_pairs={{0,8},{8,16},{16,24},{1,9},{9,17},{17,25},{2,10},{10,18},{18,26},{... | collective-permute-start | bytes 3145736 | tf_op jit(solution)/shard_map/ppermute | solution.py:382
  105.8 1.0 copy-start.6
  108.1 1.3 copy-start.1
  109.5 26.7 %all-to-all-start.4 = ((bf16[8,6,128,128]{3,2,1,0:T(8,128)(2,1)}), bf16[8,6,128,128]{3,2,1,0:T(8,128)(2,1)S(1)}, u32[]{:S(2)}, u32[]{:S(2)}) async-start(bf16[8,6,128,128]{3,2,1,0:T(8,128)(2,1)} %pad_maximum_fusion), calls=%async_computation.4 | async-start | bytes 3145728 | tf_op jit(solution)/shard_map/all_to_all | solution.py:375
  113.5 21.2 %copy-start.5 = (f32[8,2,128,128]{3,2,1,0:T(8,128)S(1)}, f32[8,2,128,128]{3,2,1,0:T(8,128)}, u32[]{:S(2)}) copy-start(f32[8,2,128,128]{3,2,1,0:T(8,128)} %get-tuple-element.40) | copy-start | bytes 3145732
  113.5 19.7 %collective-permute-start.4 = (bf16[8,2,128,128]{3,2,1,0:T(8,128)(2,1)}, bf16[8,2,128,128]{3,2,1,0:T(8,128)(2,1)S(1)}, u32[]{:S(2)}, u32[]{:S(2)}) collective-permute-start(bf16[8,2,128,128]{3,2,1,0:T(8,128)(2,1)} %get-tuple-element.44), channel_id=1, source_target_pairs={{8,0},{16,8},{24,16},{9,1},{17,9},{25,17},{10,2},{18,10},{26,18},{... | collective-permute-start | bytes 1572872 | tf_op jit(solution)/shard_map/ppermute | solution.py:329
  133.3 1.6 copy-start.4
  133.3 27.3 %collective-permute-start.5 = (bf16[8,4,128,128]{3,2,1,0:T(8,128)(2,1)}, bf16[8,4,128,128]{3,2,1,0:T(8,128)(2,1)}, u32[]{:S(2)}, u32[]{:S(2)}) collective-permute-start(bf16[8,4,128,128]{3,2,1,0:T(8,128)(2,1)} %get-tuple-element.50), channel_id=1, source_target_pairs={{8,0},{16,8},{24,16},{9,1},{17,9},{25,17},{10,2},{18,10},{26,18},{... | collective-permute-start | bytes 3145736 | tf_op jit(solution)/shard_map/ppermute | solution.py:329
  136.2 27.6 %all-to-all-start.5 = ((bf16[8,6,128,128]{3,2,1,0:T(8,128)(2,1)}), bf16[8,6,128,128]{3,2,1,0:T(8,128)(2,1)S(1)}, u32[]{:S(2)}, u32[]{:S(2)}) async-start(bf16[8,6,128,128]{3,2,1,0:T(8,128)(2,1)} %pad_maximum_fusion.1), calls=%async_computation.5 | async-start | bytes 3145728 | tf_op jit(solution)/shard_map/all_to_all | solution.py:375
  163.7 19.7 %all-to-all-start.6 = ((bf16[8,4,128,128]{3,2,1,0:T(8,128)(2,1)}), bf16[8,4,128,128]{3,2,1,0:T(8,128)(2,1)}, u32[]{:S(2)}, u32[]{:S(2)}) async-start(bf16[8,4,128,128]{3,2,1,0:T(8,128)(2,1)} %add_convert_fusion), calls=%async_computation.6 | async-start | bytes 2097152 | tf_op jit(solution)/shard_map/all_to_all | solution.py:375
  168.0 1.6 copy-start.2

commit v11 on v10

--- a/solution.py
+++ b/solution.py
@@ -313,7 +313,7 @@
         counts = (heads,)
         order = ((("kv", 0),), (("qc", 0),), (("o", 0),), (("d", 0),))
     firsts = [sum(counts[:i]) for i in range(len(counts))]
-    arrived, place, shifted, owed, made = [], {}, [], [], {}
+    arrived, place, shifted, owed, made, cut = [], {}, [], [], {}, ()
 
     def after(array, other):
         return lax.optimization_barrier((array, other))[0]
@@ -369,7 +369,7 @@
             parts.insert(0, packed)
         buffer = jnp.concatenate(parts, axis=1) if len(parts) > 1 else parts[0]
         if step == 2:
-            buffer = after(buffer, (bias, classes))
+            buffer = after(buffer, (bias, classes, cut))
         if arrived:
             buffer = after(buffer, arrived[-1])
         buffer = lax.all_to_all(buffer, group, split_axis=0, concat_axis=0, tiled=True)
@@ -378,8 +378,8 @@
         for name, i in items:
             place[name, i] = (buffer, slot)
             if name == "kv":
-                moved = buffer[:, slot : slot + 2 * counts[i]]
-                shifted.append(lax.ppermute(moved, "plane", up))
+                cut = buffer[:, slot : slot + 2 * counts[i]]
+                shifted.append(lax.ppermute(cut, "plane", up))
             slot += 2 * counts[i]
     outputs = []
     for name in ("o", "d"):

time: 187 us -> 189 us (1.011)
    all_to_all x7, waiting for transfers between devices: 40.7 us -> 43.9 us  [on_device(): lax.all_to_all(buffer, group, split_axis=0, concat_axis=0, tiled=True)]
    ppermute x3, waiting for transfers between devices: 12.6 us -> 9.97 us  [on_device(): shifted.append(lax.ppermute(cut, 'plane', up))]
where the time goes in v11:
time: 189 us; the launch traced here: 188 us
  waiting for transfers between devices  75.2 us (40%)
  Pallas kernels  47.7 us (25%)
  starting transfers between devices  45.6 us (24%)
  local copies, waits for them, and re-layouts  9.65 us (5%)
  other arithmetic  9.06 us (5%)
    all_to_all x7, waiting for transfers between devices, on_device(): lax.all_to_all(buffer, group, split_axis=0, concat_axis=0, tiled=True)  43.9 us
    pallas_call x3, Pallas kernels, attention(): pl.pallas_call(attention_body, grid=(count,), out_shape=[hbm(shape if tar...  36.4 us
    all_to_all x7, starting transfers between devices, on_device(): lax.all_to_all(buffer, group, split_axis=0, concat_axis=0, tiled=True)  29.5 us
    ppermute x3, waiting for transfers between devices, work_on(): owed.append((dkv, lax.ppermute(dkv_prev, 'plane', down)))  21.4 us
    ppermute x3, starting transfers between devices, on_device(): shifted.append(lax.ppermute(cut, 'plane', up))  12 us
    ppermute x3, waiting for transfers between devices, on_device(): shifted.append(lax.ppermute(cut, 'plane', up))  9.97 us
    pallas_call x2, Pallas kernels, pack(): pl.pallas_call(body, grid=(STEPS,), out_shape=[hbm((members, room, tokens...  6.89 us
    pallas_call x2, Pallas kernels, unpack(): pl.pallas_call(body, grid=(STEPS,), out_shape=[jax.ShapeDtypeStruct((toke...  4.46 us
  transfers between devices with their start and end apart: 13, of which 8 were waited for; matrix products, arithmetic and copies ran while one was open for 8% of the time, Pallas kernels for 23%

profile of v11, /device:TPU:0, one launch (start us, length us, event | category | flops | bytes accessed | tf_op | source)
XLA Modules:
  0.0 188.2 jit_solution(15439430019808204920)
XLA Ops:
  0.6 2.6 %pack.3 = bf16[8,4,128,128]{3,2,1,0:T(8,128)(2,1)} custom-call(bf16[128,5120]{1,0:T(8,128)(2,1)} %bitcast.18, bf16[128,5120]{1,0:T(8,128)(2,1)} %bitcast.20), custom_call_target="tpu_custom_call" | custom-call | bytes 5242880 | tf_op jit(solution)/shard_map/pack/pallas_call | solution.py:60
  3.2 5.3 %all-to-all-start = ((bf16[8,4,128,128]{3,2,1,0:T(8,128)(2,1)}), bf16[8,4,128,128]{3,2,1,0:T(8,128)(2,1)S(1)}, u32[]{:S(2)}, u32[]{:S(2)}) async-start(bf16[8,4,128,128]{3,2,1,0:T(8,128)(2,1)} %pack.3), calls=%async_computation | async-start | bytes 2097152 | tf_op jit(solution)/shard_map/all_to_all | solution.py:375
  8.9 4.3 %pack.2 = (bf16[8,6,128,128]{3,2,1,0:T(8,128)(2,1)}, bf16[8,6,128,128]{3,2,1,0:T(8,128)(2,1)}, bf16[8,8,128,128]{3,2,1,0:T(8,128)(2,1)}) custom-call(bf16[128,5120]{1,0:T(8,128)(2,1)} %bitcast.19, bf16[128,5120]{1,0:T(8,128)(2,1)} %bitcast.21, bf16[128,5120]{1,0:T(8,128)(2,1)} %bitcast.22, bf16[128,5120]{1,0:T(8,128)(2,1)} %bitcast.23), custom_call_target="tpu_custom_call" | custom-call | bytes 10485760 | tf_op jit(solution)/shard_map/pack/pallas_call | solution.py:60
  13.4 10.5 %all-to-all-done.kc_ref.vc_ref = bf16[8,4,128,128]{3,2,1,0:T(8,128)(2,1)S(1)} async-done(((bf16[8,4,128,128]{3,2,1,0:T(8,128)(2,1)}), bf16[8,4,128,128]{3,2,1,0:T(8,128)(2,1)S(1)}, u32[]{:S(2)}, u32[]{:S(2)}) %all-to-all-start) | async-done | bytes 1048608 | tf_op jit(solution)/shard_map/all_to_all | solution.py:375
  23.9 4.3 %all-to-all-start.1 = ((bf16[8,6,128,128]{3,2,1,0:T(8,128)(2,1)}), bf16[8,6,128,128]{3,2,1,0:T(8,128)(2,1)}, u32[]{:S(2)}, u32[]{:S(2)}) async-start(bf16[8,6,128,128]{3,2,1,0:T(8,128)(2,1)} %get-tuple-element.30), calls=%async_computation.1 | async-start | bytes 3145728 | tf_op jit(solution)/shard_map/all_to_all | solution.py:375
  29.5 3.5 %collective-permute-start = (bf16[8,4,128,128]{3,2,1,0:T(8,128)(2,1)S(1)}, bf16[8,4,128,128]{3,2,1,0:T(8,128)(2,1)S(1)}, u32[]{:S(2)}, u32[]{:S(2)}) collective-permute-start(bf16[8,4,128,128]{3,2,1,0:T(8,128)(2,1)S(1)} %all-to-all-done.kc_ref.vc_ref), channel_id=1, source_target_pairs={{0,8},{8,16},{16,24},{1,9},{9,17},{17,25},{2,10},{10,18},{18,26},{... | collective-permute-start | bytes 3145736 | tf_op jit(solution)/shard_map/ppermute | solution.py:382
  35.1 14.2 %all-to-all-done.1.q_ref.c_ref.kc_ref.vc_ref = bf16[8,6,128,128]{3,2,1,0:T(8,128)(2,1)} async-done(((bf16[8,6,128,128]{3,2,1,0:T(8,128)(2,1)}), bf16[8,6,128,128]{3,2,1,0:T(8,128)(2,1)}, u32[]{:S(2)}, u32[]{:S(2)}) %all-to-all-start.1) | async-done | bytes 1572896 | tf_op jit(solution)/shard_map/all_to_all | solution.py:375
  52.2 4.3 %all-to-all-start.2 = ((bf16[8,6,128,128]{3,2,1,0:T(8,128)(2,1)}), bf16[8,6,128,128]{3,2,1,0:T(8,128)(2,1)}, u32[]{:S(2)}, u32[]{:S(2)}) async-start(bf16[8,6,128,128]{3,2,1,0:T(8,128)(2,1)} %get-tuple-element.35), calls=%async_computation.2 | async-start | bytes 3145728 | tf_op jit(solution)/shard_map/all_to_all | solution.py:375
  56.5 14.0 %attention.3 = (bf16[8,8,128,128]{3,2,1,0:T(8,128)(2,1)}, f32[8,4,128,128]{3,2,1,0:T(8,128)}, bf16[8,4,128,128]{3,2,1,0:T(8,128)(2,1)}) custom-call(bf16[2,1536,128]{2,1,0:T(8,128)(2,1)} %bitcast.24, bf16[512,128]{1,0:T(8,128)(2,1)} %fusion.16.class_ref, ...), custom_call_target="tpu_custom_call", output_to_operand_aliasing={{0}: (8, {})} | custom-call | flops 9663676416 | bytes 9437184 | tf_op jit(solution)/shard_map/attention/pallas_call | solution.py:226
  70.5 7.0 %all-to-all-done.2.q_ref.c_ref.kc_ref.vc_ref = bf16[8,6,128,128]{3,2,1,0:T(8,128)(2,1)} async-done(((bf16[8,6,128,128]{3,2,1,0:T(8,128)(2,1)}), bf16[8,6,128,128]{3,2,1,0:T(8,128)(2,1)}, u32[]{:S(2)}, u32[]{:S(2)}) %all-to-all-start.2) | async-done | bytes 1572896 | tf_op jit(solution)/shard_map/all_to_all | solution.py:375
  77.5 3.6 %all-to-all-start.3 = ((bf16[8,8,128,128]{3,2,1,0:T(8,128)(2,1)}), bf16[8,8,128,128]{3,2,1,0:T(8,128)(2,1)S(1)}, u32[]{:S(2)}, u32[]{:S(2)}) async-start(bf16[8,8,128,128]{3,2,1,0:T(8,128)(2,1)} %get-tuple-element.36), calls=%async_computation.3 | async-start | bytes 4194304 | tf_op jit(solution)/shard_map/all_to_all | solution.py:375
  82.4 4.6 %collective-permute-start.1 = (bf16[8,2,128,128]{3,2,1,0:T(8,128)(2,1)}, bf16[8,2,128,128]{3,2,1,0:T(8,128)(2,1)S(1)}, u32[]{:S(2)}, u32[]{:S(2)}) collective-permute-start(bf16[8,2,128,128]{3,2,1,0:T(8,128)(2,1)} %slice.20), channel_id=1, source_target_pairs={{0,8},{8,16},{16,24},{1,9},{9,17},{17,25},{2,10},{10,18},{18,26},{... | collective-permute-start | bytes 1572872 | tf_op jit(solution)/shard_map/ppermute | solution.py:382
  89.3 3.8 %collective-permute-start.3 = (bf16[8,4,128,128]{3,2,1,0:T(8,128)(2,1)}, bf16[8,4,128,128]{3,2,1,0:T(8,128)(2,1)S(1)}, u32[]{:S(2)}, u32[]{:S(2)}) collective-permute-start(bf16[8,4,128,128]{3,2,1,0:T(8,128)(2,1)} %slice.21), channel_id=1, source_target_pairs={{0,8},{8,16},{16,24},{1,9},{9,17},{17,25},{2,10},{10,18},{18,26},{... | collective-permute-start | bytes 3145736 | tf_op jit(solution)/shard_map/ppermute | solution.py:382
  93.2 6.4 %collective-permute-done.1.kp_ref.vp_ref = bf16[8,2,128,128]{3,2,1,0:T(8,128)(2,1)S(1)} collective-permute-done((bf16[8,2,128,128]{3,2,1,0:T(8,128)(2,1)}, bf16[8,2,128,128]{3,2,1,0:T(8,128)(2,1)S(1)}, u32[]{:S(2)}, u32[]{:S(2)}) %collective-permute-start.1) | collective-permute-done | bytes 524320 | tf_op jit(solution)/shard_map/ppermute | solution.py:382
  99.6 8.3 %attention.4 = (bf16[8,2,128,128]{3,2,1,0:T(8,128)(2,1)}, f32[8,2,128,128]{3,2,1,0:T(8,128)}, bf16[8,2,128,128]{3,2,1,0:T(8,128)(2,1)}) custom-call(bf16[2,1536,128]{2,1,0:T(8,128)(2,1)} %bitcast.25, bf16[512,128]{1,0:T(8,128)(2,1)} %fusion.16.class_ref, bf16[8,6,128,128]{3,2,1,0:T(8,128)(2,1)} %all-to-all-done.2.q_ref.c_ref.kc_ref.vc_ref, ...), custom_call_target="tpu_custom_call" | custom-call | flops 4831838208 | bytes 4718592 | tf_op jit(solution)/shard_map/attention/pallas_call | solution.py:226
  112.3 3.9 %all-to-all-start.4 = ((bf16[8,6,128,128]{3,2,1,0:T(8,128)(2,1)}), bf16[8,6,128,128]{3,2,1,0:T(8,128)(2,1)S(1)}, u32[]{:S(2)}, u32[]{:S(2)}) async-start(bf16[8,6,128,128]{3,2,1,0:T(8,128)(2,1)} %pad_maximum_fusion), calls=%async_computation.4 | async-start | bytes 3145728 | tf_op jit(solution)/shard_map/all_to_all | solution.py:375
  117.6 3.5 %collective-permute-done.3.kp_ref.vp_ref = bf16[8,4,128,128]{3,2,1,0:T(8,128)(2,1)S(1)} collective-permute-done((bf16[8,4,128,128]{3,2,1,0:T(8,128)(2,1)}, bf16[8,4,128,128]{3,2,1,0:T(8,128)(2,1)S(1)}, u32[]{:S(2)}, u32[]{:S(2)}) %collective-permute-start.3) | collective-permute-done | bytes 1048608 | tf_op jit(solution)/shard_map/ppermute | solution.py:382
  121.2 14.1 %attention.5 = (bf16[8,4,128,128]{3,2,1,0:T(8,128)(2,1)}, f32[8,4,128,128]{3,2,1,0:T(8,128)}, bf16[8,4,128,128]{3,2,1,0:T(8,128)(2,1)}) custom-call(bf16[2,1536,128]{2,1,0:T(8,128)(2,1)} %bitcast.26, bf16[512,128]{1,0:T(8,128)(2,1)} %fusion.16.class_ref, bf16[8,8,128,128]{3,2,1,0:T(8,128)(2,1)} %copy-done.1, bf16[8,8,128,128]{3,2,1,0:T(8,128)(2,1)} %copy-done.1, ...), custom_call_target="tpu_custom_call" | custom-call | flops 9663676416 | bytes 9437184 | tf_op jit(solution)/shard_map/attention/pallas_call | solution.py:226
  138.2 3.9 %all-to-all-start.5 = ((bf16[8,6,128,128]{3,2,1,0:T(8,128)(2,1)}), bf16[8,6,128,128]{3,2,1,0:T(8,128)(2,1)S(1)}, u32[]{:S(2)}, u32[]{:S(2)}) async-start(bf16[8,6,128,128]{3,2,1,0:T(8,128)(2,1)} %pad_maximum_fusion.1), calls=%async_computation.5 | async-start | bytes 3145728 | tf_op jit(solution)/shard_map/all_to_all | solution.py:375
  142.0 20.5 %collective-permute-done.5 = bf16[8,4,128,128]{3,2,1,0:T(8,128)(2,1)} collective-permute-done((bf16[8,4,128,128]{3,2,1,0:T(8,128)(2,1)}, bf16[8,4,128,128]{3,2,1,0:T(8,128)(2,1)}, u32[]{:S(2)}, u32[]{:S(2)}) %collective-permute-start.5) | collective-permute-done | bytes 1048608 | tf_op jit(solution)/shard_map/ppermute | solution.py:329
  162.6 3.2 %add_convert_fusion = bf16[8,4,128,128]{3,2,1,0:T(8,128)(2,1)} fusion(f32[8,4,128,128]{3,2,1,0:T(8,128)} %get-tuple-element.45, bf16[8,4,128,128]{3,2,1,0:T(8,128)(2,1)} %collective-permute-done.5), kind=kLoop, calls=%fused_computation | loop fusion | flops 1572864 | bytes 4194304 | tf_op jit(solution)/shard_map/convert_element_type | solution.py:335
  165.7 4.3 %all-to-all-start.6 = ((bf16[8,4,128,128]{3,2,1,0:T(8,128)(2,1)}), bf16[8,4,128,128]{3,2,1,0:T(8,128)(2,1)}, u32[]{:S(2)}, u32[]{:S(2)}) async-start(bf16[8,4,128,128]{3,2,1,0:T(8,128)(2,1)} %add_convert_fusion), calls=%async_computation.6 | async-start | bytes 2097152 | tf_op jit(solution)/shard_map/all_to_all | solution.py:375
  173.3 12.1 %all-to-all-done.6.refs_2_ = bf16[8,4,128,128]{3,2,1,0:T(8,128)(2,1)} async-done(((bf16[8,4,128,128]{3,2,1,0:T(8,128)(2,1)}), bf16[8,4,128,128]{3,2,1,0:T(8,128)(2,1)}, u32[]{:S(2)}, u32[]{:S(2)}) %all-to-all-start.6) | async-done | bytes 1048608 | tf_op jit(solution)/shard_map/all_to_all | solution.py:375
  185.4 2.8 %unpack.3 = (bf16[128,5120]{1,0:T(8,128)(2,1)}, bf16[128,5120]{1,0:T(8,128)(2,1)}) custom-call(bf16[8,6,128,128]{3,2,1,0:T(8,128)(2,1)S(1)} %all-to-all-done.4.refs_1_.refs_0_, bf16[8,6,128,128]{3,2,1,0:T(8,128)(2,1)S(1)} %all-to-all-done.5.refs_2_.refs_1_, bf16[8,4,128,128]{3,2,1,0:T(8,128)(2,1)} %all-to-all-done.6.refs_2_), custom_call_target="tpu_custom_call" | custom-call | bytes 5242880 | tf_op jit(solution)/shard_map/unpack/pallas_call | solution.py:89
  (64 shorter events, 22.2 us)
Async XLA Ops:
  0.6 27.6 %copy-start = (s32[8,2,2,10]{3,2,1,0:T(2,128)S(1)}, s32[8,2,2,10]{3,2,1,0:T(2,128)}, u32[]{:S(2)}) copy-start(s32[8,2,2,10]{3,2,1,0:T(2,128)} %param.11) | copy-start | bytes 3844
  3.2 5.3 %copy-start.7 = (s32[16]{0:T(128)S(1)}, s32[16]{0:T(128)}, u32[]{:S(2)}) copy-start(s32[16]{0:T(128)} %param.10) | copy-start | bytes 196
  3.2 20.7 %all-to-all-start = ((bf16[8,4,128,128]{3,2,1,0:T(8,128)(2,1)}), bf16[8,4,128,128]{3,2,1,0:T(8,128)(2,1)S(1)}, u32[]{:S(2)}, u32[]{:S(2)}) async-start(bf16[8,4,128,128]{3,2,1,0:T(8,128)(2,1)} %pack.3), calls=%async_computation | async-start | bytes 2097152 | tf_op jit(solution)/shard_map/all_to_all | solution.py:375
  23.9 25.4 %all-to-all-start.1 = ((bf16[8,6,128,128]{3,2,1,0:T(8,128)(2,1)}), bf16[8,6,128,128]{3,2,1,0:T(8,128)(2,1)}, u32[]{:S(2)}, u32[]{:S(2)}) async-start(bf16[8,6,128,128]{3,2,1,0:T(8,128)(2,1)} %get-tuple-element.30), calls=%async_computation.1 | async-start | bytes 3145728 | tf_op jit(solution)/shard_map/all_to_all | solution.py:375
  29.5 27.0 %collective-permute-start = (bf16[8,4,128,128]{3,2,1,0:T(8,128)(2,1)S(1)}, bf16[8,4,128,128]{3,2,1,0:T(8,128)(2,1)S(1)}, u32[]{:S(2)}, u32[]{:S(2)}) collective-permute-start(bf16[8,4,128,128]{3,2,1,0:T(8,128)(2,1)S(1)} %all-to-all-done.kc_ref.vc_ref), channel_id=1, source_target_pairs={{0,8},{8,16},{16,24},{1,9},{9,17},{17,25},{2,10},{10,18},{18,26},{... | collective-permute-start | bytes 3145736 | tf_op jit(solution)/shard_map/ppermute | solution.py:382
  52.2 25.3 %all-to-all-start.2 = ((bf16[8,6,128,128]{3,2,1,0:T(8,128)(2,1)}), bf16[8,6,128,128]{3,2,1,0:T(8,128)(2,1)}, u32[]{:S(2)}, u32[]{:S(2)}) async-start(bf16[8,6,128,128]{3,2,1,0:T(8,128)(2,1)} %get-tuple-element.35), calls=%async_computation.2 | async-start | bytes 3145728 | tf_op jit(solution)/shard_map/all_to_all | solution.py:375
  77.5 33.5 %all-to-all-start.3 = ((bf16[8,8,128,128]{3,2,1,0:T(8,128)(2,1)}), bf16[8,8,128,128]{3,2,1,0:T(8,128)(2,1)S(1)}, u32[]{:S(2)}, u32[]{:S(2)}) async-start(bf16[8,8,128,128]{3,2,1,0:T(8,128)(2,1)} %get-tuple-element.36), calls=%async_computation.3 | async-start | bytes 4194304 | tf_op jit(solution)/shard_map/all_to_all | solution.py:375
  81.1 27.6 %collective-permute-start.2 = (bf16[8,4,128,128]{3,2,1,0:T(8,128)(2,1)}, bf16[8,4,128,128]{3,2,1,0:T(8,128)(2,1)S(1)}, u32[]{:S(2)}, u32[]{:S(2)}) collective-permute-start(bf16[8,4,128,128]{3,2,1,0:T(8,128)(2,1)} %get-tuple-element.39), channel_id=1, source_target_pairs={{8,0},{16,8},{24,16},{9,1},{17,9},{25,17},{10,2},{18,10},{26,18},{... | collective-permute-start | bytes 3145736 | tf_op jit(solution)/shard_map/ppermute | solution.py:329
  82.4 17.2 %collective-permute-start.1 = (bf16[8,2,128,128]{3,2,1,0:T(8,128)(2,1)}, bf16[8,2,128,128]{3,2,1,0:T(8,128)(2,1)S(1)}, u32[]{:S(2)}, u32[]{:S(2)}) collective-permute-start(bf16[8,2,128,128]{3,2,1,0:T(8,128)(2,1)} %slice.20), channel_id=1, source_target_pairs={{0,8},{8,16},{16,24},{1,9},{9,17},{17,25},{2,10},{10,18},{18,26},{... | collective-permute-start | bytes 1572872 | tf_op jit(solution)/shard_map/ppermute | solution.py:382
  89.3 19.3 %copy-start.3 = (f32[8,4,128,128]{3,2,1,0:T(8,128)S(1)}, f32[8,4,128,128]{3,2,1,0:T(8,128)}, u32[]{:S(2)}) copy-start(f32[8,4,128,128]{3,2,1,0:T(8,128)} %get-tuple-element.38) | copy-start | bytes 6291460
  89.3 31.9 %collective-permute-start.3 = (bf16[8,4,128,128]{3,2,1,0:T(8,128)(2,1)}, bf16[8,4,128,128]{3,2,1,0:T(8,128)(2,1)S(1)}, u32[]{:S(2)}, u32[]{:S(2)}) collective-permute-start(bf16[8,4,128,128]{3,2,1,0:T(8,128)(2,1)} %slice.21), channel_id=1, source_target_pairs={{0,8},{8,16},{16,24},{1,9},{9,17},{17,25},{2,10},{10,18},{18,26},{... | collective-permute-start | bytes 3145736 | tf_op jit(solution)/shard_map/ppermute | solution.py:382
  108.7 1.0 copy-start.6
  111.0 1.3 copy-start.1
  112.3 25.8 %all-to-all-start.4 = ((bf16[8,6,128,128]{3,2,1,0:T(8,128)(2,1)}), bf16[8,6,128,128]{3,2,1,0:T(8,128)(2,1)S(1)}, u32[]{:S(2)}, u32[]{:S(2)}) async-start(bf16[8,6,128,128]{3,2,1,0:T(8,128)(2,1)} %pad_maximum_fusion), calls=%async_computation.4 | async-start | bytes 3145728 | tf_op jit(solution)/shard_map/all_to_all | solution.py:375
  116.2 20.5 %copy-start.5 = (f32[8,2,128,128]{3,2,1,0:T(8,128)S(1)}, f32[8,2,128,128]{3,2,1,0:T(8,128)}, u32[]{:S(2)}) copy-start(f32[8,2,128,128]{3,2,1,0:T(8,128)} %get-tuple-element.40) | copy-start | bytes 3145732
  116.2 19.1 %collective-permute-start.4 = (bf16[8,2,128,128]{3,2,1,0:T(8,128)(2,1)}, bf16[8,2,128,128]{3,2,1,0:T(8,128)(2,1)S(1)}, u32[]{:S(2)}, u32[]{:S(2)}) collective-permute-start(bf16[8,2,128,128]{3,2,1,0:T(8,128)(2,1)} %get-tuple-element.44), channel_id=1, source_target_pairs={{8,0},{16,8},{24,16},{9,1},{17,9},{25,17},{10,2},{18,10},{26,18},{... | collective-permute-start | bytes 1572872 | tf_op jit(solution)/shard_map/ppermute | solution.py:329
  135.3 1.6 copy-start.4
  135.3 27.3 %collective-permute-start.5 = (bf16[8,4,128,128]{3,2,1,0:T(8,128)(2,1)}, bf16[8,4,128,128]{3,2,1,0:T(8,128)(2,1)}, u32[]{:S(2)}, u32[]{:S(2)}) collective-permute-start(bf16[8,4,128,128]{3,2,1,0:T(8,128)(2,1)} %get-tuple-element.50), channel_id=1, source_target_pairs={{8,0},{16,8},{24,16},{9,1},{17,9},{25,17},{10,2},{18,10},{26,18},{... | collective-permute-start | bytes 3145736 | tf_op jit(solution)/shard_map/ppermute | solution.py:329
  138.2 27.6 %all-to-all-start.5 = ((bf16[8,6,128,128]{3,2,1,0:T(8,128)(2,1)}), bf16[8,6,128,128]{3,2,1,0:T(8,128)(2,1)S(1)}, u32[]{:S(2)}, u32[]{:S(2)}) async-start(bf16[8,6,128,128]{3,2,1,0:T(8,128)(2,1)} %pad_maximum_fusion.1), calls=%async_computation.5 | async-start | bytes 3145728 | tf_op jit(solution)/shard_map/all_to_all | solution.py:375
  165.7 19.7 %all-to-all-start.6 = ((bf16[8,4,128,128]{3,2,1,0:T(8,128)(2,1)}), bf16[8,4,128,128]{3,2,1,0:T(8,128)(2,1)}, u32[]{:S(2)}, u32[]{:S(2)}) async-start(bf16[8,4,128,128]{3,2,1,0:T(8,128)(2,1)} %add_convert_fusion), calls=%async_computation.6 | async-start | bytes 2097152 | tf_op jit(solution)/shard_map/all_to_all | solution.py:375
  170.0 1.6 copy-start.2
